TPU v7x, 32 devices: a whole 2x2x4 slice. The times are simulated.
32 devices in a mesh: head: 4 (over z), blk: 8 (over y, x, core).
Axes of the slice: x: 2, y: 2, z: 4, core: 2. Of those that a mesh axis runs over, the one named last changes fastest.
Arguments:
- queries: bfloat16 [8, 512, 4096], P('blk', 'head'), may hold values from -6 to 6
- key_rows: bfloat16 [8, 512, 512], P('blk', 'head'), may hold values from -6 to 6
- value_rows: bfloat16 [8, 512, 512], P('blk', 'head'), may hold values from -6 to 6
- attn_out: bfloat16 [8, 512, 4096], P('blk', 'head'), may hold values from -6 to 6
- out_grad: bfloat16 [8, 512, 4096], P('blk', 'head'), may hold values from -3 to 3
- log_norm: float32 [8, 512, 32], P('blk', 'head'), may hold values from 5 to 7
- block_layout: int32 [16], replicated, may hold values from 0 to 15, each once
Outputs:
- query_grad: bfloat16 [8, 512, 4096], P('blk', 'head')
- key_grad: bfloat16 [8, 512, 512], P('blk', 'head')
- value_grad: bfloat16 [8, 512, 512], P('blk', 'head')
Inputs may be any that keep to these rules, and one draw needn't show every extreme that they name: Each block number stands once; the rows of blk index b are block block_layout[2 b] followed by block block_layout[2 b + 1].
All inputs are finite; a program needn't handle non-finite values.
Results may differ from a plain program's by a relative error of at most 0.014.
Values may be sent and summed in bfloat16 or wider, within the bound.
No kernel may reach another device: no remote copies, remote signals or barrier semaphores. Data moves between devices by JAX's collectives and lax.ppermute only.
A program may use at most 128 MiB of HBM per device.

v0:
```python
import functools
import math

import jax
import jax.numpy as jnp
from jax import lax
from jax.experimental import pallas as pl
from jax.experimental.pallas import tpu as pltpu
from jax.sharding import PartitionSpec as P

HD = 128
GROUP = 8
QUAD = 4
SCALE = 1.0 / math.sqrt(HD)
LOG2E = math.log2(math.e)
FAR = 1e30
TERM_ROWS = 16
COVER = 12
F32 = jnp.float32
BF16 = jnp.bfloat16
SMEM = pl.BlockSpec(memory_space=pltpu.SMEM)
VMEM = pl.BlockSpec(memory_space=pltpu.VMEM)
ANY = pl.BlockSpec(memory_space=pl.ANY)


def shifted(block, axis, distance):
    size = lax.axis_size(axis)
    route = [((i - distance) % size, i) for i in range(size)]
    return lax.ppermute(block, axis, route)


def crossed(block, mask):
    return lax.ppermute(block, "blk", [(i, i ^ mask) for i in range(lax.axis_size("blk"))])


def hopped(block, mask):
    n_z, n_blk = lax.axis_size("head"), lax.axis_size("blk")
    route = [(i * n_blk + b, (i + 1) % n_z * n_blk + (b ^ mask)) for i in range(n_z) for b in range(n_blk)]
    return lax.ppermute(block, ("head", "blk"), route)


def member(meta, mask):
    c = meta[0] % QUAD
    if mask & 1:
        c = c + 1 - 2 * (c % 2)
    if mask & 2:
        c = (c + 2) % QUAD
    return c


def block_of(meta, mask, size):
    return pl.ds(pl.multiple_of(member(meta, mask) * size, size), size)


def pack_kv(meta, keys, vals, *outs):
    for mask, out in enumerate(outs):
        cols = block_of(meta, mask, HD)
        out[0], out[1] = keys[0, :, cols], vals[0, :, cols]


def join_kv(meta, *refs):
    parts, (ring, tail) = refs[:QUAD], refs[QUAD:]
    tok = parts[0].shape[1]
    for mask, part in enumerate(parts):
        ring[:, block_of(meta, mask, tok), :] = part[...]
    tail[...] = ring[:, tok:, :]


def pack_rows(meta, queries, douts, outs, lse, _, *refs):
    packed, lse_t = refs[:QUAD], refs[QUAD]
    tok = queries.shape[1]
    wide = GROUP * HD
    lse_t[...] = lse[0].T * LOG2E
    for mask, out in enumerate(packed):
        cols = block_of(meta, mask, wide)
        out[0:tok, :] = queries[0, :, cols]
        out[tok:2 * tok, :] = douts[0, :, cols]
        norms = lse_t[block_of(meta, mask, GROUP), :]
        for h in range(GROUP):
            at = slice(h * HD, (h + 1) * HD)
            head = pl.ds(pl.multiple_of(member(meta, mask) * wide + h * HD, HD), HD)
            prod = out[tok:2 * tok, at].astype(F32) * outs[0, :, head].astype(F32)
            delta = jnp.sum(prod.T, axis=0, keepdims=True)
            lines = []
            for term in (norms[h:h + 1], delta):
                high = term.astype(BF16).astype(F32)
                lines += [high, term - high]
            block = jnp.concatenate(lines + [jnp.zeros((TERM_ROWS - 4, tok), F32)], axis=0).astype(BF16)
            out[2 * tok:, h * tok:(h + 1) * tok] = block


def do_nothing(*refs):
    del refs


def later(block, after):
    return pl.pallas_call(
        do_nothing,
        out_shape=jax.ShapeDtypeStruct(block.shape, block.dtype),
        in_specs=[ANY] * (1 + len(after)),
        out_specs=ANY,
        input_output_aliases={0: 0},
        compiler_params=pltpu.CompilerParams(vmem_limit_bytes=2**20),
        name="later",
    )(block, *after)


def pass_on(ring_in, *refs):
    tail = refs[-1]
    tail[...] = ring_in[:, ring_in.shape[1] - tail.shape[1]:, :]


def held(ring, after):
    planes, rows, cols = ring.shape
    return pl.pallas_call(
        pass_on,
        out_shape=[
            jax.ShapeDtypeStruct(ring.shape, ring.dtype),
            jax.ShapeDtypeStruct((planes, rows // QUAD * (QUAD - 1), cols), ring.dtype),
        ],
        in_specs=[VMEM] + [ANY] * len(after),
        out_specs=[ANY, VMEM],
        input_output_aliases={0: 0},
        compiler_params=pltpu.CompilerParams(vmem_limit_bytes=4 * 2**20),
        name="pass_on",
    )(ring, *after)


def total(n_packet, d_own, back, refs):
    tok = d_own.shape[1] // QUAD
    tail = d_own[:, tok:, :] + back[...].astype(F32)
    lead = d_own[:, 0:tok, :]
    if n_packet:
        lead += refs[0][:, 0:tok, :].astype(F32)
        tail += refs[0][:, tok:, :].astype(F32)
    return lead, tail


def pack_sum(n_packet, d_own, back, *refs):
    lead, tail = total(n_packet, d_own, back, refs)
    out = refs[-1]
    tok = lead.shape[1]
    out[:, 0:tok, :] = lead.astype(BF16)
    out[:, tok:, :] = tail.astype(BF16)


def split_sum(meta, d_own, back, packet, *refs):
    outs, whole = refs[:QUAD], refs[QUAD]
    lead, tail = total(1, d_own, back, (packet,))
    tok = lead.shape[1]
    whole[:, 0:tok, :] = lead
    whole[:, tok:, :] = tail
    for mask, out in enumerate(outs):
        out[...] = whole[:, block_of(meta, mask, tok), :].astype(BF16)


def pack_cross(masks, meta, *refs):
    n = len(masks)
    dqs, (d_own, back), outs, whole = refs[:n], refs[n:n + 2], refs[n + 2:-1], refs[-1]
    lead, tail = total(0, d_own, back, ())
    tok, wide = dqs[0].shape
    whole[:, 0:tok, :] = lead
    whole[:, tok:, :] = tail
    for mask, dq, out in zip(masks, dqs, outs):
        out[:, 0:wide] = dq[...]
        part = whole[:, block_of(meta, mask, tok), :].astype(BF16)
        out[:, wide:wide + HD] = part[0]
        out[:, wide + HD:] = part[1]
    if len(outs) > n:
        outs[n][...] = whole[:, block_of(meta, 0, tok), :]


def place_heads(meta, dq_own, got_one, got_two, got_three, out, done, sems):
    wide = dq_own.shape[1]
    copies = []
    for mask, src in enumerate((dq_own, got_one, got_two, got_three)):
        src = src if mask == 0 else src.at[:, 0:wide]
        copies.append(pltpu.make_async_copy(src, out.at[0, :, block_of(meta, mask, wide)], sems.at[mask]))
    for copy in copies:
        copy.start()
    done[...] = jnp.zeros_like(done)
    for copy in copies:
        copy.wait()


def finish(meta, kept, got_one, got_two, got_three, hop0, hop1, hop2, hop3, _, dkey, dval):
    wide = got_one.shape[1] - 2 * HD
    for mask, (got, hop) in enumerate(zip((kept, got_one, got_two, got_three), (hop0, hop1, hop2, hop3))):
        cols = block_of(meta, mask, HD)
        for plane, dst in ((0, dkey), (1, dval)):
            first = got[plane] if mask == 0 else got[:, wide + plane * HD:wide + (plane + 1) * HD].astype(F32)
            dst[0, :, cols] = (first + hop[plane].astype(F32)).astype(BF16)


def small_call(body, outs, specs, operands, scratch=(), cost=0, far_out=False):
    shapes = [jax.ShapeDtypeStruct(shape, kind) for shape, kind in outs]
    name = getattr(body, "func", body).__name__
    return pl.pallas_call(
        body,
        out_shape=shapes,
        in_specs=specs,
        out_specs=[ANY if i == 0 and far_out else VMEM for i in range(len(shapes))],
        scratch_shapes=list(scratch),
        compiler_params=pltpu.CompilerParams(vmem_limit_bytes=4 * 2**20),
        cost_estimate=pl.CostEstimate(flops=0, bytes_accessed=cost, transcendentals=0),
        name=name,
    )(*operands)


def attend(lag, masks, n_blk, n_z, first, last, closing, n_after, meta, layout, *refs):
    (rows_a, rows_b, near, far), refs = refs[:4], refs[4:]
    tok = near.shape[1] // QUAD
    if not first:
        acc_in, refs = refs[0], refs[1:]
    if closing:
        d_in, refs = refs[0], refs[1:]
    refs = refs[n_after:]
    if last:
        dq_outs, refs = refs[:2], refs[2:]
    else:
        acc_out, refs = refs[0], refs[1:]
    if closing:
        (d_own, d_far), refs = refs[:2], refs[2:]
    else:
        d_out, refs = refs[0], refs[1:]
    kbuf, vbuf, kbuf_t, dbuf, probs, dscores = refs
    n_far = QUAD - 1
    window = QUAD * tok
    quad = meta[0] - meta[0] % QUAD
    z = meta[1]
    shard = (z + n_z - lag) % n_z

    for plane, dst in ((0, kbuf), (1, vbuf)):
        dst[0:n_far * tok, :] = far[plane]
        dst[n_far * tok:, :] = near[plane]
    kbuf_t[...] = kbuf[...].T
    dbuf[...] = d_in[...] if closing else jnp.zeros_like(dbuf)

    def base(group, shard):
        return layout[2 * group + shard // 2] * (2 * tok) + (shard % 2) * tok

    for t, (mask, rows) in enumerate(zip(masks, (rows_a, rows_b))):
        i = member(meta, mask)
        chunk = pl.ds(pl.multiple_of(i * tok, tok), window)
        keys, vals, keys_t = kbuf[chunk, :], vbuf[chunk, :], kbuf_t[:, chunk]
        qbase = base(quad + i, z)
        gaps = [qbase - base((quad + i - n_far + c + n_blk) % n_blk, shard) for c in range(QUAD)]
        row = lax.broadcasted_iota(jnp.int32, (tok, 2 * tok), 0)
        col = lax.broadcasted_iota(jnp.int32, (tok, 2 * tok), 1) % tok
        linked = (col - row + gaps[QUAD - 1]) >= 0

        def stacked(start, heads):
            return jnp.concatenate([rows[start:start + tok, h * HD:(h + 1) * HD] for h in heads], axis=0)

        for g in range(GROUP // 2):
            heads = (2 * g, 2 * g + 1)
            query, dout = stacked(0, heads), stacked(tok, heads)
            span = slice(2 * g * tok, (2 * g + 2) * tok)
            terms = rows[2 * tok:, span].astype(F32)
            lse, delta = terms[0:1] + terms[1:2], terms[2:3] + terms[3:4]
            nt = (((1,), (1,)), ((), ()))
            score = lax.dot_general(keys, query, nt, preferred_element_type=F32) * (SCALE * LOG2E)
            dprob = lax.dot_general(vals, dout, nt, preferred_element_type=F32)
            for c in range(QUAD):
                part = slice(c * tok, (c + 1) * tok)
                if c == QUAD - 1:
                    prob = jnp.where(linked, jnp.exp2(score[part] - lse), 0.0)
                else:
                    prob = jnp.exp2(score[part] - jnp.where(gaps[c] > 0, lse, FAR))
                probs[t, part, span] = prob.astype(BF16)
                dscores[t, part, span] = (prob * (dprob[part] - delta)).astype(BF16)
        query, dout = stacked(0, range(GROUP)), stacked(tok, range(GROUP))
        dbuf[0, chunk, :] += jnp.dot(dscores[t], query, preferred_element_type=F32)
        dbuf[1, chunk, :] += jnp.dot(probs[t], dout, preferred_element_type=F32)
        dq = jnp.dot(keys_t, dscores[t], preferred_element_type=F32)
        if not first:
            dq = dq + acc_in[t]
        if last:
            for h in range(GROUP):
                at = slice(h * HD, (h + 1) * HD)
                dq_outs[t][:, at] = (dq[:, h * tok:(h + 1) * tok] * SCALE).T.astype(BF16)
        else:
            acc_out[t] = dq

    if closing:
        for plane, scale in ((0, SCALE), (1, 1.0)):
            d_far[plane] = (dbuf[plane, 0:n_far * tok, :] * scale).astype(BF16)
            d_own[plane] = dbuf[plane, n_far * tok:, :] * scale
    else:
        d_out[...] = dbuf[...]


def attend_call(lag, masks, n_blk, n_z, meta, layout, rows, keys, acc, d_in, after):
    tok = keys[0].shape[1] // QUAD
    first, last, closing = acc is None, lag == n_z - 1, d_in is not None
    chunks = (2 * QUAD - 1) * tok
    near, far = (2, QUAD * tok, HD), (2, (QUAD - 1) * tok, HD)
    outs = (
        [jax.ShapeDtypeStruct((tok, GROUP * HD), BF16)] * 2
        if last else [jax.ShapeDtypeStruct((2, HD, GROUP * tok), F32)]
    )
    n_heads = len(outs)
    if closing:
        outs = outs + [jax.ShapeDtypeStruct(near, F32), jax.ShapeDtypeStruct(far, BF16)]
    else:
        outs = outs + [jax.ShapeDtypeStruct((2, chunks, HD), F32)]
    inputs = [meta, layout, *rows, *keys]
    aliases = {}
    if not first:
        if not last:
            aliases[len(inputs)] = 0
        inputs.append(acc)
    if closing:
        inputs.append(d_in)
    results = pl.pallas_call(
        functools.partial(attend, lag, masks, n_blk, n_z, first, last, closing, len(after)),
        out_shape=outs,
        in_specs=[SMEM, SMEM] + [VMEM] * (len(inputs) - 2) + [ANY] * len(after),
        out_specs=[VMEM] * len(outs),
        scratch_shapes=[
            pltpu.VMEM((chunks, HD), BF16),
            pltpu.VMEM((chunks, HD), BF16),
            pltpu.VMEM((HD, chunks), BF16),
            pltpu.VMEM((2, chunks, HD), F32),
            pltpu.VMEM((2, QUAD * tok, GROUP * tok), BF16),
            pltpu.VMEM((2, QUAD * tok, GROUP * tok), BF16),
        ],
        input_output_aliases=aliases,
        compiler_params=pltpu.CompilerParams(vmem_limit_bytes=14 * 2**20),
        cost_estimate=pl.CostEstimate(
            flops=COVER * 4 * tok * GROUP * tok * HD, bytes_accessed=2**20, transcendentals=0
        ),
        name="attend",
    )(*inputs, *after)
    return results[:n_heads], results[n_heads:]


def shards(queries, key_rows, value_rows, attn_out, out_grad, log_norm, block_layout):
    tok = queries.shape[1]
    blk, z = lax.axis_index("blk"), lax.axis_index("head")
    n_blk, n_z = lax.axis_size("blk"), lax.axis_size("head")
    wide = GROUP * HD
    meta = jnp.stack([blk, z]).astype(jnp.int32)
    piece = ((2, tok, HD), BF16)
    ring_of, tail_of = ((2, QUAD * tok, HD), BF16), ((2, (QUAD - 1) * tok, HD), BF16)

    pieces = small_call(pack_kv, [piece] * QUAD, [SMEM, VMEM, VMEM], [meta, key_rows, value_rows])
    parts = [pieces[0]] + [crossed(pieces[mask], mask) for mask in range(1, QUAD)]
    ring, tail = small_call(join_kv, [ring_of, tail_of], [SMEM] + [VMEM] * QUAD, [meta, *parts])
    block = ((2 * tok + TERM_ROWS, wide), BF16)
    packed = small_call(
        pack_rows, [block] * QUAD, [SMEM] + [VMEM] * 4 + [ANY],
        [meta, queries, out_grad, attn_out, log_norm, pieces[0]],
        scratch=[pltpu.VMEM((log_norm.shape[2], tok), F32)], cost=4 * 2**20,
    )
    rows = [packed[0]] + [crossed(later(packed[mask], [tail]), mask) for mask in range(1, QUAD)]

    keys = [[ring, shifted(tail, "blk", QUAD)]]
    accs = [None, None]
    sums, backs = [None] * n_z, [None] * n_z

    def pass_keys(after):
        ring, tail = held(shifted(keys[-1][0], "head", 1), after)
        keys.append([ring, shifted(tail, "blk", QUAD)])

    def call(pair, lag, after=()):
        heads, grads = attend_call(
            lag, (2 * pair, 2 * pair + 1), n_blk, n_z, meta, block_layout, rows[2 * pair:2 * pair + 2], keys[lag],
            accs[pair], sums[lag], after,
        )
        accs[pair] = heads if lag == n_z - 1 else heads[0]
        if sums[lag] is not None:
            backs[lag] = shifted(grads[1], "blk", -QUAD)
        sums[lag] = grads[0]

    def pass_sums(lag, packet, after):
        parts = [sums[lag], backs[lag], *packet]
        out = small_call(
            functools.partial(pack_sum, len(packet)), [ring_of], [VMEM] * len(parts) + [ANY], parts + [after]
        )[0]
        return [shifted(out, "head", 1)]

    call(0, 0)
    pass_keys([accs[0]])
    call(0, 1)
    pass_keys([accs[0]])
    call(0, 2)
    pass_keys([accs[0]])
    call(1, 0, [accs[0]])
    call(1, 1)
    call(1, 2, [backs[0]])
    packet = pass_sums(1, [], accs[1])
    call(1, 3)
    cross = ((tok, wide + 2 * HD), BF16)
    whole = pltpu.VMEM(ring_of[0], F32)
    sent = small_call(
        functools.partial(pack_cross, (2, 3)), [cross] * 2, [SMEM] + [VMEM] * 4,
        [meta, *accs[1], sums[0], backs[0]], scratch=[whole], cost=2**20,
    )
    call(0, 3, [accs[1][0]])
    packet = pass_sums(2, packet, sums[3])
    near_sent, kept = small_call(
        functools.partial(pack_cross, (1,)), [cross, (piece[0], F32)], [SMEM] + [VMEM] * 3,
        [meta, accs[0][1], sums[0], backs[0]], scratch=[whole], cost=2**20,
    )
    got = [crossed(part, mask) for mask, part in enumerate([near_sent, *sent], 1)]
    hops = small_call(
        split_sum, [piece] * QUAD, [SMEM] + [VMEM] * 3, [meta, sums[3], backs[3], *packet],
        scratch=[pltpu.VMEM(ring_of[0], F32)],
    )
    hops = [hopped(hops[mask], mask) for mask in range(QUAD)]
    query_grad, placed = small_call(
        place_heads, [(queries.shape, BF16), ((8, HD), F32)], [SMEM] + [VMEM] * QUAD, [meta, accs[0][0], *got],
        scratch=[pltpu.SemaphoreType.DMA((QUAD,))], far_out=True,
    )
    flat = (key_rows.shape, BF16)
    key_grad, value_grad = small_call(
        finish, [flat, flat], [SMEM] + [VMEM] * 8 + [ANY], [meta, kept, *got, *hops, placed]
    )
    return query_grad, key_grad, value_grad


def solution(mesh):
    spread = P("blk", "head", None)
    return jax.shard_map(
        shards,
        mesh=mesh,
        in_specs=(spread,) * 6 + (P(),),
        out_specs=(spread,) * 3,
        check_vma=False,
    )
```

profile of v0, /device:TPU:0, one launch (start us, length us, event | category | flops | bytes accessed | tf_op | source)
XLA Modules:
  0.0 94.2 jit_solution(14179423780934400082)
XLA Ops:
  3.7 2.6 %collective-permute-start.1 = (bf16[2,128,128]{2,1,0:T(8,128)(2,1)S(1)}, bf16[2,128,128]{2,1,0:T(8,128)(2,1)S(1)}, u32[]{:S(2)}, u32[]{:S(2)}) collective-permute-start(bf16[2,128,128]{2,1,0:T(8,128)(2,1)S(1)} %get-tuple-element.57), channel_id=1, source_target_pairs={{0,2},{1,3},{2,0},{3,1},{4,6},{5,7},{6,4},{7,5},{8,10},{9,11},{10,... | collective-permute-start | bytes 196616 | tf_op jit(solution)/shard_map/ppermute | solution.py:33
  12.1 2.0 %collective-permute-start.5 = (bf16[2,384,128]{2,1,0:T(8,128)(2,1)S(1)}, bf16[2,384,128]{2,1,0:T(8,128)(2,1)S(1)}, u32[]{:S(2)}, u32[]{:S(2)}) collective-permute-start(bf16[2,384,128]{2,1,0:T(8,128)(2,1)S(1)} %get-tuple-element.59.refs_1_), channel_id=1, source_target_pairs={{4,0},{5,1},{6,2},{7,3},{0,4},{1,5},{2,6},{3,7},{12,8},{13,9},{14,... | collective-permute-start | bytes 589832 | tf_op jit(solution)/shard_map/ppermute | solution.py:29
  14.1 1.6 %collective-permute-start.4 = (bf16[2,512,128]{2,1,0:T(8,128)(2,1)S(1)}, bf16[2,512,128]{2,1,0:T(8,128)(2,1)S(1)}, u32[]{:S(2)}, u32[]{:S(2)}) collective-permute-start(bf16[2,512,128]{2,1,0:T(8,128)(2,1)S(1)} %get-tuple-element.60.refs_2_), channel_id=1, source_target_pairs={{24,0},{0,8},{8,16},{16,24},{25,1},{1,9},{9,17},{17,25},{26,2},{2,... | collective-permute-start | bytes 786440 | tf_op jit(solution)/shard_map/ppermute | solution.py:29
  15.7 1.5 %collective-permute-start.11 = (bf16[272,1024]{1,0:T(8,128)(2,1)S(1)}, bf16[272,1024]{1,0:T(8,128)(2,1)S(1)}, u32[]{:S(2)}, u32[]{:S(2)}) collective-permute-start(bf16[272,1024]{1,0:T(8,128)(2,1)S(1)} %later.4), channel_id=1, source_target_pairs={{0,2},{1,3},{2,0},{3,1},{4,6},{5,7},{6,4},{7,5},{8,10},{9,11},{10,... | collective-permute-start | bytes 1671176 | tf_op jit(solution)/shard_map/ppermute | solution.py:33
  17.2 2.2 %collective-permute-done.5.refs_3_ = bf16[2,384,128]{2,1,0:T(8,128)(2,1)S(1)} collective-permute-done((bf16[2,384,128]{2,1,0:T(8,128)(2,1)S(1)}, bf16[2,384,128]{2,1,0:T(8,128)(2,1)S(1)}, u32[]{:S(2)}, u32[]{:S(2)}) %collective-permute-start.5) | collective-permute-done | bytes 196640 | tf_op jit(solution)/shard_map/ppermute | solution.py:29
  19.3 3.3 %attend.8 = (f32[2,128,1024]{2,1,0:T(8,128)S(1)}, f32[2,896,128]{2,1,0:T(8,128)S(1)}) custom-call(s32[2]{0:T(128)S(1)} %pad_add_fusion.meta, s32[16]{0:T(128)S(1)} %copy-done.5, bf16[272,1024]{1,0:T(8,128)(2,1)S(1)} %get-tuple-element.54.refs_0_, bf16[272,1024]{1,0:T(8,128)(2,1)S(1)} %collective-permute-done.3.refs_1_, ...), custom_call_target="tpu_custom_call" | custom-call | flops 805306368 | bytes 1048576 | tf_op jit(solution)/shard_map/attend/pallas_call | solution.py:315
  26.0 4.0 %collective-permute-done.7.refs_3_ = bf16[2,384,128]{2,1,0:T(8,128)(2,1)S(1)} collective-permute-done((bf16[2,384,128]{2,1,0:T(8,128)(2,1)S(1)}, bf16[2,384,128]{2,1,0:T(8,128)(2,1)S(1)}, u32[]{:S(2)}, u32[]{:S(2)}) %collective-permute-start.7) | collective-permute-done | bytes 196640 | tf_op jit(solution)/shard_map/ppermute | solution.py:29
  30.0 3.4 %attend.9 = (f32[2,128,1024]{2,1,0:T(8,128)S(1)}, f32[2,896,128]{2,1,0:T(8,128)S(1)}) custom-call(s32[2]{0:T(128)S(1)} %pad_add_fusion.meta, s32[16]{0:T(128)S(1)} %copy-done.5, bf16[272,1024]{1,0:T(8,128)(2,1)S(1)} %get-tuple-element.54.refs_0_, bf16[272,1024]{1,0:T(8,128)(2,1)S(1)} %collective-permute-done.3.refs_1_, ...), custom_call_target="tpu_custom_call", output_to_operand_aliasing={{0}: (6, {})} | custom-call | flops 805306368 | bytes 1048576 | tf_op jit(solution)/shard_map/attend/pallas_call | solution.py:315
  35.7 3.8 %collective-permute-done.9.refs_3_ = bf16[2,384,128]{2,1,0:T(8,128)(2,1)S(1)} collective-permute-done((bf16[2,384,128]{2,1,0:T(8,128)(2,1)S(1)}, bf16[2,384,128]{2,1,0:T(8,128)(2,1)S(1)}, u32[]{:S(2)}, u32[]{:S(2)}) %collective-permute-start.9) | collective-permute-done | bytes 196640 | tf_op jit(solution)/shard_map/ppermute | solution.py:29
  39.5 3.4 %attend.10 = (f32[2,128,1024]{2,1,0:T(8,128)S(1)}, f32[2,896,128]{2,1,0:T(8,128)S(1)}) custom-call(s32[2]{0:T(128)S(1)} %pad_add_fusion.meta, s32[16]{0:T(128)S(1)} %copy-done.5, bf16[272,1024]{1,0:T(8,128)(2,1)S(1)} %get-tuple-element.54.refs_0_, bf16[272,1024]{1,0:T(8,128)(2,1)S(1)} %collective-permute-done.3.refs_1_, ...), custom_call_target="tpu_custom_call", output_to_operand_aliasing={{0}: (6, {})} | custom-call | flops 805306368 | bytes 1048576 | tf_op jit(solution)/shard_map/attend/pallas_call | solution.py:315
  42.9 3.3 %attend.11 = (f32[2,128,1024]{2,1,0:T(8,128)S(1)}, f32[2,512,128]{2,1,0:T(8,128)S(1)}, bf16[2,384,128]{2,1,0:T(8,128)(2,1)S(1)}) custom-call(s32[2]{0:T(128)S(1)} %pad_add_fusion.meta, s32[16]{0:T(128)S(1)} %copy-done.5, bf16[272,1024]{1,0:T(8,128)(2,1)S(1)} %collective-permute-done.11.refs_0_, bf16[272,1024]{1,0:T(8,128)(2,1)S(1)} %collective-permute-done.12.refs_1_, ...), custom_call_target="tpu_custom_call" | custom-call | flops 805306368 | bytes 1048576 | tf_op jit(solution)/shard_map/attend/pallas_call | solution.py:315
  47.5 3.4 %attend.12 = (f32[2,128,1024]{2,1,0:T(8,128)S(1)}, f32[2,512,128]{2,1,0:T(8,128)S(1)}, bf16[2,384,128]{2,1,0:T(8,128)(2,1)S(1)}) custom-call(s32[2]{0:T(128)S(1)} %pad_add_fusion.meta, s32[16]{0:T(128)S(1)} %copy-done.5, bf16[272,1024]{1,0:T(8,128)(2,1)S(1)} %collective-permute-done.11.refs_0_, ...), custom_call_target="tpu_custom_call", output_to_operand_aliasing={{0}: (6, {})} | custom-call | flops 805306368 | bytes 1048576 | tf_op jit(solution)/shard_map/attend/pallas_call | solution.py:315
  53.1 3.4 %attend.13 = (f32[2,128,1024]{2,1,0:T(8,128)S(1)}, f32[2,512,128]{2,1,0:T(8,128)S(1)}, bf16[2,384,128]{2,1,0:T(8,128)(2,1)S(1)}) custom-call(s32[2]{0:T(128)S(1)} %pad_add_fusion.meta, s32[16]{0:T(128)S(1)} %copy-done.5, bf16[272,1024]{1,0:T(8,128)(2,1)S(1)} %collective-permute-done.11.refs_0_, ...), custom_call_target="tpu_custom_call", output_to_operand_aliasing={{0}: (6, {})} | custom-call | flops 805306368 | bytes 1048576 | tf_op jit(solution)/shard_map/attend/pallas_call | solution.py:315
  56.5 1.9 %collective-permute-done.19.back = bf16[2,384,128]{2,1,0:T(8,128)(2,1)S(1)} collective-permute-done((bf16[2,384,128]{2,1,0:T(8,128)(2,1)S(1)}, bf16[2,384,128]{2,1,0:T(8,128)(2,1)S(1)}, u32[]{:S(2)}, u32[]{:S(2)}) %collective-permute-start.19) | collective-permute-done | bytes 196640 | tf_op jit(solution)/shard_map/ppermute | solution.py:29
  60.2 2.2 %collective-permute-done.10.refs_3_ = bf16[2,384,128]{2,1,0:T(8,128)(2,1)S(1)} collective-permute-done((bf16[2,384,128]{2,1,0:T(8,128)(2,1)S(1)}, bf16[2,384,128]{2,1,0:T(8,128)(2,1)S(1)}, u32[]{:S(2)}, u32[]{:S(2)}) %collective-permute-start.10) | collective-permute-done | bytes 196640 | tf_op jit(solution)/shard_map/ppermute | solution.py:29
  62.5 3.4 %attend.14 = (bf16[128,1024]{1,0:T(8,128)(2,1)S(1)}, bf16[128,1024]{1,0:T(8,128)(2,1)S(1)}, f32[2,896,128]{2,1,0:T(8,128)S(1)}) custom-call(s32[2]{0:T(128)S(1)} %pad_add_fusion.meta, s32[16]{0:T(128)S(1)} %copy-done.5, bf16[272,1024]{1,0:T(8,128)(2,1)S(1)} %collective-permute-done.11.refs_0_, bf16[272,1024]{1,0:T(8,128)(2,1)S(1)} %collective-permute-done.12.refs_1_, ...), custom_call_target="tpu_custom_call" | custom-call | flops 805306368 | bytes 1048576 | tf_op jit(solution)/shard_map/attend/pallas_call | solution.py:315
  66.5 1.6 %collective-permute-start.15 = (bf16[128,1280]{1,0:T(8,128)(2,1)S(1)}, bf16[128,1280]{1,0:T(8,128)(2,1)S(1)}, u32[]{:S(2)}, u32[]{:S(2)}) collective-permute-start(bf16[128,1280]{1,0:T(8,128)(2,1)S(1)} %get-tuple-element.86), channel_id=1, source_target_pairs={{0,2},{1,3},{2,0},{3,1},{4,6},{5,7},{6,4},{7,5},{8,10},{9,11},{10,... | collective-permute-start | bytes 983048 | tf_op jit(solution)/shard_map/ppermute | solution.py:33
  68.1 3.4 %attend.15 = (bf16[128,1024]{1,0:T(8,128)(2,1)S(1)}, bf16[128,1024]{1,0:T(8,128)(2,1)S(1)}, f32[2,512,128]{2,1,0:T(8,128)S(1)}, bf16[2,384,128]{2,1,0:T(8,128)(2,1)S(1)}) custom-call(s32[2]{0:T(128)S(1)} %pad_add_fusion.meta, s32[16]{0:T(128)S(1)} %copy-done.5, bf16[272,1024]{1,0:T(8,128)(2,1)S(1)} %get-tuple-element.54.refs_0_, ...), custom_call_target="tpu_custom_call" | custom-call | flops 805306368 | bytes 1048576 | tf_op jit(solution)/shard_map/attend/pallas_call | solution.py:315
  74.2 6.5 %collective-permute-done.17.back = bf16[2,384,128]{2,1,0:T(8,128)(2,1)S(1)} collective-permute-done((bf16[2,384,128]{2,1,0:T(8,128)(2,1)S(1)}, bf16[2,384,128]{2,1,0:T(8,128)(2,1)S(1)}, u32[]{:S(2)}, u32[]{:S(2)}) %collective-permute-start.17) | collective-permute-done | bytes 196640 | tf_op jit(solution)/shard_map/ppermute | solution.py:29
  80.6 1.6 %collective-permute-done.21.packet = bf16[2,512,128]{2,1,0:T(8,128)(2,1)S(1)} collective-permute-done((bf16[2,512,128]{2,1,0:T(8,128)(2,1)S(1)}, bf16[2,512,128]{2,1,0:T(8,128)(2,1)S(1)}, u32[]{:S(2)}, u32[]{:S(2)}) %collective-permute-start.21) | collective-permute-done | bytes 262176 | tf_op jit(solution)/shard_map/ppermute | solution.py:29
  83.1 1.7 %collective-permute-start.24 = (bf16[2,128,128]{2,1,0:T(8,128)(2,1)S(1)}, bf16[2,128,128]{2,1,0:T(8,128)(2,1)S(1)}, u32[]{:S(2)}, u32[]{:S(2)}) collective-permute-start(bf16[2,128,128]{2,1,0:T(8,128)(2,1)S(1)} %get-tuple-element.98), channel_id=1, source_target_pairs={{0,10},{1,11},{2,8},{3,9},{4,14},{5,15},{6,12},{7,13},{8,18},{9,19... | collective-permute-start | bytes 196616 | tf_op jit(solution)/shard_map/ppermute | solution.py:39
  84.8 3.5 %collective-permute-start.25 = (bf16[2,128,128]{2,1,0:T(8,128)(2,1)S(1)}, bf16[2,128,128]{2,1,0:T(8,128)(2,1)S(1)}, u32[]{:S(2)}, u32[]{:S(2)}) collective-permute-start(bf16[2,128,128]{2,1,0:T(8,128)(2,1)S(1)} %get-tuple-element.99), channel_id=1, source_target_pairs={{0,11},{1,10},{2,9},{3,8},{4,15},{5,14},{6,13},{7,12},{8,19},{9,18... | collective-permute-start | bytes 196616 | tf_op jit(solution)/shard_map/ppermute | solution.py:39
  88.3 1.5 %place_heads.1 = (bf16[1,128,4096]{2,1,0:T(8,128)(2,1)}, f32[8,128]{1,0:T(8,128)S(1)}) custom-call(s32[2]{0:T(128)S(1)} %pad_add_fusion.meta, bf16[128,1024]{1,0:T(8,128)(2,1)S(1)} %get-tuple-element.81.dq_own, bf16[128,1280]{1,0:T(8,128)(2,1)S(1)} %collective-permute-done.14.got_one, bf16[128,1280]{1,0:T(8,128)(2,1)S(1)} %collective-permute-done.15.got_two, ...), custom_call_target="tpu_custom_call" | custom-call | tf_op jit(solution)/shard_map/place_heads/pallas_call | solution.py:198
  89.9 2.1 %collective-permute-done.24.hop2 = bf16[2,128,128]{2,1,0:T(8,128)(2,1)S(1)} collective-permute-done((bf16[2,128,128]{2,1,0:T(8,128)(2,1)S(1)}, bf16[2,128,128]{2,1,0:T(8,128)(2,1)S(1)}, u32[]{:S(2)}, u32[]{:S(2)}) %collective-permute-start.24) | collective-permute-done | bytes 65568 | tf_op jit(solution)/shard_map/ppermute | solution.py:39
  (68 shorter events, 26.4 us)
Async XLA Ops:
  3.1 8.2 %collective-permute-start = (bf16[2,128,128]{2,1,0:T(8,128)(2,1)S(1)}, bf16[2,128,128]{2,1,0:T(8,128)(2,1)S(1)}, u32[]{:S(2)}, u32[]{:S(2)}) collective-permute-start(bf16[2,128,128]{2,1,0:T(8,128)(2,1)S(1)} %get-tuple-element.56), channel_id=1, source_target_pairs={{0,1},{1,0},{2,3},{3,2},{4,5},{5,4},{6,7},{7,6},{8,9},{9,8},{10,11... | collective-permute-start | bytes 196616 | tf_op jit(solution)/shard_map/ppermute | solution.py:33
  3.7 7.7 %collective-permute-start.1 = (bf16[2,128,128]{2,1,0:T(8,128)(2,1)S(1)}, bf16[2,128,128]{2,1,0:T(8,128)(2,1)S(1)}, u32[]{:S(2)}, u32[]{:S(2)}) collective-permute-start(bf16[2,128,128]{2,1,0:T(8,128)(2,1)S(1)} %get-tuple-element.57), channel_id=1, source_target_pairs={{0,2},{1,3},{2,0},{3,1},{4,6},{5,7},{6,4},{7,5},{8,10},{9,11},{10,... | collective-permute-start | bytes 196616 | tf_op jit(solution)/shard_map/ppermute | solution.py:33
  11.9 7.4 %collective-permute-start.3 = (bf16[272,1024]{1,0:T(8,128)(2,1)S(1)}, bf16[272,1024]{1,0:T(8,128)(2,1)S(1)}, u32[]{:S(2)}, u32[]{:S(2)}) collective-permute-start(bf16[272,1024]{1,0:T(8,128)(2,1)S(1)} %later.3), channel_id=1, source_target_pairs={{0,1},{1,0},{2,3},{3,2},{4,5},{5,4},{6,7},{7,6},{8,9},{9,8},{10,11... | collective-permute-start | bytes 1671176 | tf_op jit(solution)/shard_map/ppermute | solution.py:33
  12.1 7.2 %collective-permute-start.5 = (bf16[2,384,128]{2,1,0:T(8,128)(2,1)S(1)}, bf16[2,384,128]{2,1,0:T(8,128)(2,1)S(1)}, u32[]{:S(2)}, u32[]{:S(2)}) collective-permute-start(bf16[2,384,128]{2,1,0:T(8,128)(2,1)S(1)} %get-tuple-element.59.refs_1_), channel_id=1, source_target_pairs={{4,0},{5,1},{6,2},{7,3},{0,4},{1,5},{2,6},{3,7},{12,8},{13,9},{14,... | collective-permute-start | bytes 589832 | tf_op jit(solution)/shard_map/ppermute | solution.py:29
  14.1 10.0 %collective-permute-start.4 = (bf16[2,512,128]{2,1,0:T(8,128)(2,1)S(1)}, bf16[2,512,128]{2,1,0:T(8,128)(2,1)S(1)}, u32[]{:S(2)}, u32[]{:S(2)}) collective-permute-start(bf16[2,512,128]{2,1,0:T(8,128)(2,1)S(1)} %get-tuple-element.60.refs_2_), channel_id=1, source_target_pairs={{24,0},{0,8},{8,16},{16,24},{25,1},{1,9},{9,17},{17,25},{26,2},{2,... | collective-permute-start | bytes 786440 | tf_op jit(solution)/shard_map/ppermute | solution.py:29
  15.7 27.2 %collective-permute-start.11 = (bf16[272,1024]{1,0:T(8,128)(2,1)S(1)}, bf16[272,1024]{1,0:T(8,128)(2,1)S(1)}, u32[]{:S(2)}, u32[]{:S(2)}) collective-permute-start(bf16[272,1024]{1,0:T(8,128)(2,1)S(1)} %later.4), channel_id=1, source_target_pairs={{0,2},{1,3},{2,0},{3,1},{4,6},{5,7},{6,4},{7,5},{8,10},{9,11},{10,... | collective-permute-start | bytes 1671176 | tf_op jit(solution)/shard_map/ppermute | solution.py:33
  17.2 25.7 %collective-permute-start.12 = (bf16[272,1024]{1,0:T(8,128)(2,1)S(1)}, bf16[272,1024]{1,0:T(8,128)(2,1)S(1)}, u32[]{:S(2)}, u32[]{:S(2)}) collective-permute-start(bf16[272,1024]{1,0:T(8,128)(2,1)S(1)} %later.5), channel_id=1, source_target_pairs={{0,3},{1,2},{2,1},{3,0},{4,7},{5,6},{6,5},{7,4},{8,11},{9,10},{10,... | collective-permute-start | bytes 1671176 | tf_op jit(solution)/shard_map/ppermute | solution.py:33
  24.1 6.0 %collective-permute-start.7 = (bf16[2,384,128]{2,1,0:T(8,128)(2,1)S(1)}, bf16[2,384,128]{2,1,0:T(8,128)(2,1)S(1)}, u32[]{:S(2)}, u32[]{:S(2)}) collective-permute-start(bf16[2,384,128]{2,1,0:T(8,128)(2,1)S(1)} %get-tuple-element.63), channel_id=1, source_target_pairs={{4,0},{5,1},{6,2},{7,3},{0,4},{1,5},{2,6},{3,7},{12,8},{13,9},{14,... | collective-permute-start | bytes 589832 | tf_op jit(solution)/shard_map/ppermute | solution.py:29
  24.6 9.1 %collective-permute-start.6 = (bf16[2,512,128]{2,1,0:T(8,128)(2,1)S(1)}, bf16[2,512,128]{2,1,0:T(8,128)(2,1)S(1)}, u32[]{:S(2)}, u32[]{:S(2)}) collective-permute-start(bf16[2,512,128]{2,1,0:T(8,128)(2,1)S(1)} %get-tuple-element.62.refs_2_), channel_id=1, source_target_pairs={{24,0},{0,8},{8,16},{16,24},{25,1},{1,9},{9,17},{17,25},{26,2},{2,... | collective-permute-start | bytes 786440 | tf_op jit(solution)/shard_map/ppermute | solution.py:29
  35.1 16.6 %collective-permute-start.8 = (bf16[2,512,128]{2,1,0:T(8,128)(2,1)S(1)}, bf16[2,512,128]{2,1,0:T(8,128)(2,1)S(1)}, u32[]{:S(2)}, u32[]{:S(2)}) collective-permute-start(bf16[2,512,128]{2,1,0:T(8,128)(2,1)S(1)} %get-tuple-element.65.refs_2_), channel_id=1, source_target_pairs={{24,0},{0,8},{8,16},{16,24},{25,1},{1,9},{9,17},{17,25},{26,2},{2,... | collective-permute-start | bytes 786440 | tf_op jit(solution)/shard_map/ppermute | solution.py:29
  46.2 6.9 %collective-permute-start.13 = (bf16[2,384,128]{2,1,0:T(8,128)(2,1)S(1)}, bf16[2,384,128]{2,1,0:T(8,128)(2,1)S(1)}, u32[]{:S(2)}, u32[]{:S(2)}) collective-permute-start(bf16[2,384,128]{2,1,0:T(8,128)(2,1)S(1)} %get-tuple-element.77), channel_id=1, source_target_pairs={{4,0},{5,1},{6,2},{7,3},{0,4},{1,5},{2,6},{3,7},{12,8},{13,9},{14,... | collective-permute-start | bytes 589832 | tf_op jit(solution)/shard_map/ppermute | solution.py:29
  50.9 7.4 %collective-permute-start.19 = (bf16[2,384,128]{2,1,0:T(8,128)(2,1)S(1)}, bf16[2,384,128]{2,1,0:T(8,128)(2,1)S(1)}, u32[]{:S(2)}, u32[]{:S(2)}) collective-permute-start(bf16[2,384,128]{2,1,0:T(8,128)(2,1)S(1)} %get-tuple-element.95), channel_id=1, source_target_pairs={{4,0},{5,1},{6,2},{7,3},{0,4},{1,5},{2,6},{3,7},{12,8},{13,9},{14,... | collective-permute-start | bytes 589832 | tf_op jit(solution)/shard_map/ppermute | solution.py:29
  51.7 10.8 %collective-permute-start.10 = (bf16[2,384,128]{2,1,0:T(8,128)(2,1)S(1)}, bf16[2,384,128]{2,1,0:T(8,128)(2,1)S(1)}, u32[]{:S(2)}, u32[]{:S(2)}) collective-permute-start(bf16[2,384,128]{2,1,0:T(8,128)(2,1)S(1)} %get-tuple-element.69), channel_id=1, source_target_pairs={{4,0},{5,1},{6,2},{7,3},{0,4},{1,5},{2,6},{3,7},{12,8},{13,9},{14,... | collective-permute-start | bytes 589832 | tf_op jit(solution)/shard_map/ppermute | solution.py:29
  58.4 13.1 %collective-permute-start.20 = (bf16[2,512,128]{2,1,0:T(8,128)(2,1)S(1)}, bf16[2,512,128]{2,1,0:T(8,128)(2,1)S(1)}, u32[]{:S(2)}, u32[]{:S(2)}) collective-permute-start(bf16[2,512,128]{2,1,0:T(8,128)(2,1)S(1)} %pack_sum.2), channel_id=1, source_target_pairs={{24,0},{0,8},{8,16},{16,24},{25,1},{1,9},{9,17},{17,25},{26,2},{2,... | collective-permute-start | bytes 786440 | tf_op jit(solution)/shard_map/ppermute | solution.py:29
  59.7 11.7 %collective-permute-start.18 = (bf16[2,384,128]{2,1,0:T(8,128)(2,1)S(1)}, bf16[2,384,128]{2,1,0:T(8,128)(2,1)S(1)}, u32[]{:S(2)}, u32[]{:S(2)}) collective-permute-start(bf16[2,384,128]{2,1,0:T(8,128)(2,1)S(1)} %get-tuple-element.93), channel_id=1, source_target_pairs={{4,0},{5,1},{6,2},{7,3},{0,4},{1,5},{2,6},{3,7},{12,8},{13,9},{14,... | collective-permute-start | bytes 589832 | tf_op jit(solution)/shard_map/ppermute | solution.py:29
  66.5 16.6 %collective-permute-start.15 = (bf16[128,1280]{1,0:T(8,128)(2,1)S(1)}, bf16[128,1280]{1,0:T(8,128)(2,1)S(1)}, u32[]{:S(2)}, u32[]{:S(2)}) collective-permute-start(bf16[128,1280]{1,0:T(8,128)(2,1)S(1)} %get-tuple-element.86), channel_id=1, source_target_pairs={{0,2},{1,3},{2,0},{3,1},{4,6},{5,7},{6,4},{7,5},{8,10},{9,11},{10,... | collective-permute-start | bytes 983048 | tf_op jit(solution)/shard_map/ppermute | solution.py:33
  68.1 16.7 %collective-permute-start.16 = (bf16[128,1280]{1,0:T(8,128)(2,1)S(1)}, bf16[128,1280]{1,0:T(8,128)(2,1)S(1)}, u32[]{:S(2)}, u32[]{:S(2)}) collective-permute-start(bf16[128,1280]{1,0:T(8,128)(2,1)S(1)} %get-tuple-element.87), channel_id=1, source_target_pairs={{0,3},{1,2},{2,1},{3,0},{4,7},{5,6},{6,5},{7,4},{8,11},{9,10},{10,... | collective-permute-start | bytes 983048 | tf_op jit(solution)/shard_map/ppermute | solution.py:33
  71.6 10.7 %collective-permute-start.21 = (bf16[2,512,128]{2,1,0:T(8,128)(2,1)S(1)}, bf16[2,512,128]{2,1,0:T(8,128)(2,1)S(1)}, u32[]{:S(2)}, u32[]{:S(2)}) collective-permute-start(bf16[2,512,128]{2,1,0:T(8,128)(2,1)S(1)} %pack_sum.3), channel_id=1, source_target_pairs={{24,0},{0,8},{8,16},{16,24},{25,1},{1,9},{9,17},{17,25},{26,2},{2,... | collective-permute-start | bytes 786440 | tf_op jit(solution)/shard_map/ppermute | solution.py:29
  73.2 15.0 %collective-permute-start.14 = (bf16[128,1280]{1,0:T(8,128)(2,1)S(1)}, bf16[128,1280]{1,0:T(8,128)(2,1)S(1)}, u32[]{:S(2)}, u32[]{:S(2)}) collective-permute-start(bf16[128,1280]{1,0:T(8,128)(2,1)S(1)} %get-tuple-element.84), channel_id=1, source_target_pairs={{0,1},{1,0},{2,3},{3,2},{4,5},{5,4},{6,7},{7,6},{8,9},{9,8},{10,11... | collective-permute-start | bytes 983048 | tf_op jit(solution)/shard_map/ppermute | solution.py:33
  73.7 7.0 %collective-permute-start.17 = (bf16[2,384,128]{2,1,0:T(8,128)(2,1)S(1)}, bf16[2,384,128]{2,1,0:T(8,128)(2,1)S(1)}, u32[]{:S(2)}, u32[]{:S(2)}) collective-permute-start(bf16[2,384,128]{2,1,0:T(8,128)(2,1)S(1)} %get-tuple-element.91), channel_id=1, source_target_pairs={{4,0},{5,1},{6,2},{7,3},{0,4},{1,5},{2,6},{3,7},{12,8},{13,9},{14,... | collective-permute-start | bytes 589832 | tf_op jit(solution)/shard_map/ppermute | solution.py:29
  82.9 6.9 %collective-permute-start.22 = (bf16[2,128,128]{2,1,0:T(8,128)(2,1)S(1)}, bf16[2,128,128]{2,1,0:T(8,128)(2,1)S(1)}, u32[]{:S(2)}, u32[]{:S(2)}) collective-permute-start(bf16[2,128,128]{2,1,0:T(8,128)(2,1)S(1)} %get-tuple-element.96), channel_id=1, source_target_pairs={{0,8},{1,9},{2,10},{3,11},{4,12},{5,13},{6,14},{7,15},{8,16},{9,17... | collective-permute-start | bytes 196616 | tf_op jit(solution)/shard_map/ppermute | solution.py:39
  83.1 6.8 %collective-permute-start.23 = (bf16[2,128,128]{2,1,0:T(8,128)(2,1)S(1)}, bf16[2,128,128]{2,1,0:T(8,128)(2,1)S(1)}, u32[]{:S(2)}, u32[]{:S(2)}) collective-permute-start(bf16[2,128,128]{2,1,0:T(8,128)(2,1)S(1)} %get-tuple-element.97), channel_id=1, source_target_pairs={{0,9},{1,8},{2,11},{3,10},{4,13},{5,12},{6,15},{7,14},{8,17},{9,16... | collective-permute-start | bytes 196616 | tf_op jit(solution)/shard_map/ppermute | solution.py:39
  83.1 8.9 %collective-permute-start.24 = (bf16[2,128,128]{2,1,0:T(8,128)(2,1)S(1)}, bf16[2,128,128]{2,1,0:T(8,128)(2,1)S(1)}, u32[]{:S(2)}, u32[]{:S(2)}) collective-permute-start(bf16[2,128,128]{2,1,0:T(8,128)(2,1)S(1)} %get-tuple-element.98), channel_id=1, source_target_pairs={{0,10},{1,11},{2,8},{3,9},{4,14},{5,15},{6,12},{7,13},{8,18},{9,19... | collective-permute-start | bytes 196616 | tf_op jit(solution)/shard_map/ppermute | solution.py:39
  84.8 8.2 %collective-permute-start.25 = (bf16[2,128,128]{2,1,0:T(8,128)(2,1)S(1)}, bf16[2,128,128]{2,1,0:T(8,128)(2,1)S(1)}, u32[]{:S(2)}, u32[]{:S(2)}) collective-permute-start(bf16[2,128,128]{2,1,0:T(8,128)(2,1)S(1)} %get-tuple-element.99), channel_id=1, source_target_pairs={{0,11},{1,10},{2,9},{3,8},{4,15},{5,14},{6,13},{7,12},{8,19},{9,18... | collective-permute-start | bytes 196616 | tf_op jit(solution)/shard_map/ppermute | solution.py:39
  (9 other events, 22.3 us)
where the time goes:
time: 94.5 us; the launch traced here: 94.2 us
  Pallas kernels  34.2 us (36%)
  waiting for transfers between devices  26.9 us (28%)
  starting transfers between devices  26.6 us (28%)
  local copies, waits for them, and re-layouts  5.58 us (6%)
    pallas_call x8, Pallas kernels, attend_call(): pl.pallas_call(functools.partial(attend, lag, masks, n_blk, n_z, first, l...  26.9 us
    ppermute x13, waiting for transfers between devices, shifted(): return lax.ppermute(block, axis, route)  23.8 us
    ppermute x13, starting transfers between devices, shifted(): return lax.ppermute(block, axis, route)  14.4 us
    pallas_call x10, Pallas kernels, small_call(): pl.pallas_call(body, out_shape=shapes, in_specs=specs, out_specs=[ANY if...  7.3 us
    ppermute x9, starting transfers between devices, crossed(): lax.ppermute(block, 'blk', [(i, i ^ mask) for i in range(lax.axis_size('b...  6.83 us
    unnamed x15, local copies, waits for them, and re-layouts  5.58 us
    ppermute x4, starting transfers between devices, hopped(): return lax.ppermute(block, ('head', 'blk'), route)  5.34 us
    ppermute x4, waiting for transfers between devices, hopped(): return lax.ppermute(block, ('head', 'blk'), route)  3.07 us
  transfers between devices with their start and end apart: 26, of which 11 were waited for; matrix products, arithmetic and copies ran while one was open for 0% of the time, Pallas kernels for 34%

commit v1 on v0

--- a/solution.py
+++ b/solution.py
@@ -93,7 +93,7 @@
     del refs
 
 
-def later(block, after):
+def later(block, after=(), cost=0):
     return pl.pallas_call(
         do_nothing,
         out_shape=jax.ShapeDtypeStruct(block.shape, block.dtype),
@@ -101,6 +101,7 @@
         out_specs=ANY,
         input_output_aliases={0: 0},
         compiler_params=pltpu.CompilerParams(vmem_limit_bytes=2**20),
+        cost_estimate=pl.CostEstimate(flops=cost, bytes_accessed=0, transcendentals=0),
         name="later",
     )(block, *after)
 
@@ -126,9 +127,9 @@
     )(ring, *after)
 
 
-def total(n_packet, d_own, back, refs):
+def total(part, n_packet, d_own, back, refs):
     tok = d_own.shape[1] // QUAD
-    tail = d_own[:, tok:, :] + back[...].astype(F32)
+    tail = d_own[:, tok:, :] + back[2 * part:2 * part + 2].astype(F32)
     lead = d_own[:, 0:tok, :]
     if n_packet:
         lead += refs[0][:, 0:tok, :].astype(F32)
@@ -136,8 +137,8 @@
     return lead, tail
 
 
-def pack_sum(n_packet, d_own, back, *refs):
-    lead, tail = total(n_packet, d_own, back, refs)
+def pack_sum(part, n_packet, d_own, back, *refs):
+    lead, tail = total(part, n_packet, d_own, back, refs)
     out = refs[-1]
     tok = lead.shape[1]
     out[:, 0:tok, :] = lead.astype(BF16)
@@ -146,7 +147,7 @@
 
 def split_sum(meta, d_own, back, packet, *refs):
     outs, whole = refs[:QUAD], refs[QUAD]
-    lead, tail = total(1, d_own, back, (packet,))
+    lead, tail = total(0, 1, d_own, back, (packet,))
     tok = lead.shape[1]
     whole[:, 0:tok, :] = lead
     whole[:, tok:, :] = tail
@@ -157,7 +158,7 @@
 def pack_cross(masks, meta, *refs):
     n = len(masks)
     dqs, (d_own, back), outs, whole = refs[:n], refs[n:n + 2], refs[n + 2:-1], refs[-1]
-    lead, tail = total(0, d_own, back, ())
+    lead, tail = total(0, 0, d_own, back, ())
     tok, wide = dqs[0].shape
     whole[:, 0:tok, :] = lead
     whole[:, tok:, :] = tail
@@ -166,16 +167,31 @@
         part = whole[:, block_of(meta, mask, tok), :].astype(BF16)
         out[:, wide:wide + HD] = part[0]
         out[:, wide + HD:] = part[1]
-    if len(outs) > n:
-        outs[n][...] = whole[:, block_of(meta, 0, tok), :]
-
-
-def place_heads(meta, dq_own, got_one, got_two, got_three, out, done, sems):
+
+
+def pack_near(meta, dq, d_own, back, _, first, second, kept, whole):
+    lead, tail = total(0, 0, d_own, back, ())
+    tok, wide = dq.shape
+    half = first.shape[1]
+    whole[:, 0:tok, :] = lead
+    whole[:, tok:, :] = tail
+    part = whole[:, block_of(meta, 1, tok), :].astype(BF16)
+    first[...] = dq[:, 0:half]
+    second[:, 0:wide - half] = dq[:, half:]
+    second[:, wide - half:wide - half + HD] = part[0]
+    second[:, wide - half + HD:] = part[1]
+    kept[...] = whole[:, block_of(meta, 0, tok), :]
+
+
+def place_heads(meta, dq_own, near_one, near_two, got_two, got_three, out, done, sems):
     wide = dq_own.shape[1]
+    half = near_one.shape[1]
     copies = []
-    for mask, src in enumerate((dq_own, got_one, got_two, got_three)):
-        src = src if mask == 0 else src.at[:, 0:wide]
-        copies.append(pltpu.make_async_copy(src, out.at[0, :, block_of(meta, mask, wide)], sems.at[mask]))
+    for mask, src in ((0, dq_own), (2, got_two.at[:, 0:wide]), (3, got_three.at[:, 0:wide])):
+        copies.append(pltpu.make_async_copy(src, out.at[0, :, block_of(meta, mask, wide)], sems.at[len(copies)]))
+    for start, src in ((0, near_one), (half, near_two.at[:, 0:wide - half])):
+        cols = pl.ds(pl.multiple_of(member(meta, 1) * wide + start, HD), src.shape[1])
+        copies.append(pltpu.make_async_copy(src, out.at[0, :, cols], sems.at[len(copies)]))
     for copy in copies:
         copy.start()
     done[...] = jnp.zeros_like(done)
@@ -183,12 +199,15 @@
         copy.wait()
 
 
-def finish(meta, kept, got_one, got_two, got_three, hop0, hop1, hop2, hop3, _, dkey, dval):
-    wide = got_one.shape[1] - 2 * HD
-    for mask, (got, hop) in enumerate(zip((kept, got_one, got_two, got_three), (hop0, hop1, hop2, hop3))):
+def finish(meta, kept, near_two, got_two, got_three, hop0, hop1, hop2, hop3, _, dkey, dval):
+    for mask, (got, hop) in enumerate(zip((kept, near_two, got_two, got_three), (hop0, hop1, hop2, hop3))):
         cols = block_of(meta, mask, HD)
         for plane, dst in ((0, dkey), (1, dval)):
-            first = got[plane] if mask == 0 else got[:, wide + plane * HD:wide + (plane + 1) * HD].astype(F32)
+            if mask == 0:
+                first = got[plane]
+            else:
+                start = got.shape[1] - (2 - plane) * HD
+                first = got[:, start:start + HD].astype(F32)
             dst[0, :, cols] = (first + hop[plane].astype(F32)).astype(BF16)
 
 
@@ -207,7 +226,7 @@
     )(*operands)
 
 
-def attend(lag, masks, n_blk, n_z, first, last, closing, n_after, meta, layout, *refs):
+def attend(lag, masks, n_blk, n_z, first, last, closing, n_after, place, meta, layout, *refs):
     (rows_a, rows_b, near, far), refs = refs[:4], refs[4:]
     tok = near.shape[1] // QUAD
     if not first:
@@ -284,17 +303,17 @@
 
     if closing:
         for plane, scale in ((0, SCALE), (1, 1.0)):
-            d_far[plane] = (dbuf[plane, 0:n_far * tok, :] * scale).astype(BF16)
+            d_far[2 * place + plane] = (dbuf[plane, 0:n_far * tok, :] * scale).astype(BF16)
             d_own[plane] = dbuf[plane, n_far * tok:, :] * scale
     else:
         d_out[...] = dbuf[...]
 
 
-def attend_call(lag, masks, n_blk, n_z, meta, layout, rows, keys, acc, d_in, after):
+def attend_call(lag, masks, n_blk, n_z, meta, layout, rows, keys, acc, d_in, after, parts, carried):
     tok = keys[0].shape[1] // QUAD
     first, last, closing = acc is None, lag == n_z - 1, d_in is not None
     chunks = (2 * QUAD - 1) * tok
-    near, far = (2, QUAD * tok, HD), (2, (QUAD - 1) * tok, HD)
+    near, far = (2, QUAD * tok, HD), (2 * parts, (QUAD - 1) * tok, HD)
     outs = (
         [jax.ShapeDtypeStruct((tok, GROUP * HD), BF16)] * 2
         if last else [jax.ShapeDtypeStruct((2, HD, GROUP * tok), F32)]
@@ -312,8 +331,13 @@
         inputs.append(acc)
     if closing:
         inputs.append(d_in)
+    if carried is not None:
+        aliases[len(inputs)] = len(outs) - 1
+        after = [carried, *after]
     results = pl.pallas_call(
-        functools.partial(attend, lag, masks, n_blk, n_z, first, last, closing, len(after)),
+        functools.partial(
+            attend, lag, masks, n_blk, n_z, first, last, closing, len(after), int(carried is not None)
+        ),
         out_shape=outs,
         in_specs=[SMEM, SMEM] + [VMEM] * (len(inputs) - 2) + [ANY] * len(after),
         out_specs=[VMEM] * len(outs),
@@ -347,9 +371,9 @@
     pieces = small_call(pack_kv, [piece] * QUAD, [SMEM, VMEM, VMEM], [meta, key_rows, value_rows])
     parts = [pieces[0]] + [crossed(pieces[mask], mask) for mask in range(1, QUAD)]
     ring, tail = small_call(join_kv, [ring_of, tail_of], [SMEM] + [VMEM] * QUAD, [meta, *parts])
-    block = ((2 * tok + TERM_ROWS, wide), BF16)
+    row_block = ((2 * tok + TERM_ROWS, wide), BF16)
     packed = small_call(
-        pack_rows, [block] * QUAD, [SMEM] + [VMEM] * 4 + [ANY],
+        pack_rows, [row_block] * QUAD, [SMEM] + [VMEM] * 4 + [ANY],
         [meta, queries, out_grad, attn_out, log_norm, pieces[0]],
         scratch=[pltpu.VMEM((log_norm.shape[2], tok), F32)], cost=4 * 2**20,
     )
@@ -357,28 +381,30 @@
 
     keys = [[ring, shifted(tail, "blk", QUAD)]]
     accs = [None, None]
-    sums, backs = [None] * n_z, [None] * n_z
+    sums = [None] * n_z
 
     def pass_keys(after):
         ring, tail = held(shifted(keys[-1][0], "head", 1), after)
         keys.append([ring, shifted(tail, "blk", QUAD)])
 
-    def call(pair, lag, after=()):
+    def call(pair, lag, after=(), parts=1, carried=None):
         heads, grads = attend_call(
             lag, (2 * pair, 2 * pair + 1), n_blk, n_z, meta, block_layout, rows[2 * pair:2 * pair + 2], keys[lag],
-            accs[pair], sums[lag], after,
+            accs[pair], sums[lag], after, parts, carried,
         )
         accs[pair] = heads if lag == n_z - 1 else heads[0]
-        if sums[lag] is not None:
-            backs[lag] = shifted(grads[1], "blk", -QUAD)
         sums[lag] = grads[0]
-
-    def pass_sums(lag, packet, after):
-        parts = [sums[lag], backs[lag], *packet]
+        return grads[-1]
+
+    def send_back(grads):
+        return shifted(grads, "blk", -QUAD)
+
+    def pass_sums(lag, part, back, packet, after):
+        parts = [sums[lag], back, *packet]
         out = small_call(
-            functools.partial(pack_sum, len(packet)), [ring_of], [VMEM] * len(parts) + [ANY], parts + [after]
+            functools.partial(pack_sum, part, len(packet)), [ring_of], [VMEM] * len(parts) + [ANY], parts + [after]
         )[0]
-        return [shifted(out, "head", 1)]
+        return out, [shifted(out, "head", 1)]
 
     call(0, 0)
     pass_keys([accs[0]])
@@ -386,36 +412,38 @@
     pass_keys([accs[0]])
     call(0, 2)
     pass_keys([accs[0]])
-    call(1, 0, [accs[0]])
-    call(1, 1)
-    call(1, 2, [backs[0]])
-    packet = pass_sums(1, [], accs[1])
+    back_zero = send_back(call(1, 0, [accs[0]]))
+    back_one = send_back(call(1, 1))
+    back_two = send_back(call(1, 2, [back_zero]))
+    _, packet = pass_sums(1, 0, back_one, [], accs[1])
     call(1, 3)
     cross = ((tok, wide + 2 * HD), BF16)
     whole = pltpu.VMEM(ring_of[0], F32)
     sent = small_call(
         functools.partial(pack_cross, (2, 3)), [cross] * 2, [SMEM] + [VMEM] * 4,
-        [meta, *accs[1], sums[0], backs[0]], scratch=[whole], cost=2**20,
-    )
-    call(0, 3, [accs[1][0]])
-    packet = pass_sums(2, packet, sums[3])
-    near_sent, kept = small_call(
-        functools.partial(pack_cross, (1,)), [cross, (piece[0], F32)], [SMEM] + [VMEM] * 3,
-        [meta, accs[0][1], sums[0], backs[0]], scratch=[whole], cost=2**20,
-    )
-    got = [crossed(part, mask) for mask, part in enumerate([near_sent, *sent], 1)]
+        [meta, *accs[1], sums[0], back_zero], scratch=[whole], cost=2**20,
+    )
+    block, packet = pass_sums(2, 0, back_two, packet, accs[1][0])
+    back_three = send_back(call(0, 3, [block]))
+    near_half = ((tok, (wide + 2 * HD) // 2), BF16)
+    near_one, near_two, kept = small_call(
+        pack_near, [near_half] * 2 + [(piece[0], F32)], [SMEM] + [VMEM] * 3 + [ANY],
+        [meta, accs[0][1], sums[0], back_zero, *packet], scratch=[whole], cost=2**20,
+    )
+    near_one, near_two = crossed(near_one, 1), crossed(near_two, 1)
+    got = [crossed(part, mask) for mask, part in enumerate(sent, 2)]
     hops = small_call(
-        split_sum, [piece] * QUAD, [SMEM] + [VMEM] * 3, [meta, sums[3], backs[3], *packet],
+        split_sum, [piece] * QUAD, [SMEM] + [VMEM] * 3, [meta, sums[3], back_three, *packet],
         scratch=[pltpu.VMEM(ring_of[0], F32)],
     )
     hops = [hopped(hops[mask], mask) for mask in range(QUAD)]
     query_grad, placed = small_call(
-        place_heads, [(queries.shape, BF16), ((8, HD), F32)], [SMEM] + [VMEM] * QUAD, [meta, accs[0][0], *got],
-        scratch=[pltpu.SemaphoreType.DMA((QUAD,))], far_out=True,
+        place_heads, [(queries.shape, BF16), ((8, HD), F32)], [SMEM] + [VMEM] * 5, [meta, accs[0][0], near_one, near_two, *got],
+        scratch=[pltpu.SemaphoreType.DMA((5,))], far_out=True,
     )
     flat = (key_rows.shape, BF16)
     key_grad, value_grad = small_call(
-        finish, [flat, flat], [SMEM] + [VMEM] * 8 + [ANY], [meta, kept, *got, *hops, placed]
+        finish, [flat, flat], [SMEM] + [VMEM] * 8 + [ANY], [meta, kept, near_two, *got, *hops, placed]
     )
     return query_grad, key_grad, value_grad
 

time: 94.5 us -> 93.5 us (0.989)
    ppermute x13, waiting for transfers between devices: 23.8 us -> 21.9 us  [shifted(): return lax.ppermute(block, axis, route)]
    ppermute x4, waiting for transfers between devices: 3.07 us -> 4.11 us  [hopped(): return lax.ppermute(block, ('head', 'blk'), route)]
    ppermute x9 -> x10, starting transfers between devices: 6.83 us -> 6.99 us  [crossed(): lax.ppermute(block, 'blk', [(i, i ^ mask) for i in range(lax.axis_size('b...]
  transfers between devices with their start and end apart: 26 -> 27, of which waited for: 11 -> 13; matrix products, arithmetic and copies ran while one was open for 0% -> 0% of each run, Pallas kernels for 34% -> 34%
where the time goes in v1:
time: 93.5 us; the launch traced here: 93.2 us
  Pallas kernels  34.2 us (37%)
  starting transfers between devices  26.4 us (28%)
  waiting for transfers between devices  26 us (28%)
  local copies, waits for them, and re-layouts  5.58 us (6%)
    pallas_call x8, Pallas kernels, attend_call(): pl.pallas_call(functools.partial(attend, lag, masks, n_blk, n_z, first, l...  26.9 us
    ppermute x13, waiting for transfers between devices, shifted(): return lax.ppermute(block, axis, route)  21.9 us
    ppermute x13, starting transfers between devices, shifted(): return lax.ppermute(block, axis, route)  14.1 us
    pallas_call x10, Pallas kernels, small_call(): pl.pallas_call(body, out_shape=shapes, in_specs=specs, out_specs=[ANY if...  7.3 us
    ppermute x10, starting transfers between devices, crossed(): lax.ppermute(block, 'blk', [(i, i ^ mask) for i in range(lax.axis_size('b...  6.99 us
    unnamed x15, local copies, waits for them, and re-layouts  5.58 us
    ppermute x4, starting transfers between devices, hopped(): return lax.ppermute(block, ('head', 'blk'), route)  5.34 us
    ppermute x4, waiting for transfers between devices, hopped(): return lax.ppermute(block, ('head', 'blk'), route)  4.11 us
  transfers between devices with their start and end apart: 27, of which 13 were waited for; matrix products, arithmetic and copies ran while one was open for 0% of the time, Pallas kernels for 34%

profile of v1, /device:TPU:0, one launch (start us, length us, event | category | flops | bytes accessed | tf_op | source)
XLA Modules:
  0.0 93.2 jit_solution(927780049883728266)
XLA Ops:
  3.7 2.6 %collective-permute-start.1 = (bf16[2,128,128]{2,1,0:T(8,128)(2,1)S(1)}, bf16[2,128,128]{2,1,0:T(8,128)(2,1)S(1)}, u32[]{:S(2)}, u32[]{:S(2)}) collective-permute-start(bf16[2,128,128]{2,1,0:T(8,128)(2,1)S(1)} %get-tuple-element.58), channel_id=1, source_target_pairs={{0,2},{1,3},{2,0},{3,1},{4,6},{5,7},{6,4},{7,5},{8,10},{9,11},{10,... | collective-permute-start | bytes 196616 | tf_op jit(solution)/shard_map/ppermute | solution.py:33
  12.1 2.0 %collective-permute-start.5 = (bf16[2,384,128]{2,1,0:T(8,128)(2,1)S(1)}, bf16[2,384,128]{2,1,0:T(8,128)(2,1)S(1)}, u32[]{:S(2)}, u32[]{:S(2)}) collective-permute-start(bf16[2,384,128]{2,1,0:T(8,128)(2,1)S(1)} %get-tuple-element.60.refs_1_), channel_id=1, source_target_pairs={{4,0},{5,1},{6,2},{7,3},{0,4},{1,5},{2,6},{3,7},{12,8},{13,9},{14,... | collective-permute-start | bytes 589832 | tf_op jit(solution)/shard_map/ppermute | solution.py:29
  14.1 1.6 %collective-permute-start.4 = (bf16[2,512,128]{2,1,0:T(8,128)(2,1)S(1)}, bf16[2,512,128]{2,1,0:T(8,128)(2,1)S(1)}, u32[]{:S(2)}, u32[]{:S(2)}) collective-permute-start(bf16[2,512,128]{2,1,0:T(8,128)(2,1)S(1)} %get-tuple-element.61.refs_2_), channel_id=1, source_target_pairs={{24,0},{0,8},{8,16},{16,24},{25,1},{1,9},{9,17},{17,25},{26,2},{2,... | collective-permute-start | bytes 786440 | tf_op jit(solution)/shard_map/ppermute | solution.py:29
  15.7 1.5 %collective-permute-start.11 = (bf16[272,1024]{1,0:T(8,128)(2,1)S(1)}, bf16[272,1024]{1,0:T(8,128)(2,1)S(1)}, u32[]{:S(2)}, u32[]{:S(2)}) collective-permute-start(bf16[272,1024]{1,0:T(8,128)(2,1)S(1)} %later.4), channel_id=1, source_target_pairs={{0,2},{1,3},{2,0},{3,1},{4,6},{5,7},{6,4},{7,5},{8,10},{9,11},{10,... | collective-permute-start | bytes 1671176 | tf_op jit(solution)/shard_map/ppermute | solution.py:33
  17.2 2.2 %collective-permute-done.5.refs_3_ = bf16[2,384,128]{2,1,0:T(8,128)(2,1)S(1)} collective-permute-done((bf16[2,384,128]{2,1,0:T(8,128)(2,1)S(1)}, bf16[2,384,128]{2,1,0:T(8,128)(2,1)S(1)}, u32[]{:S(2)}, u32[]{:S(2)}) %collective-permute-start.5) | collective-permute-done | bytes 196640 | tf_op jit(solution)/shard_map/ppermute | solution.py:29
  19.3 3.3 %attend.8 = (f32[2,128,1024]{2,1,0:T(8,128)S(1)}, f32[2,896,128]{2,1,0:T(8,128)S(1)}) custom-call(s32[2]{0:T(128)S(1)} %pad_add_fusion.meta, s32[16]{0:T(128)S(1)} %copy-done.5, bf16[272,1024]{1,0:T(8,128)(2,1)S(1)} %get-tuple-element.55.refs_0_, bf16[272,1024]{1,0:T(8,128)(2,1)S(1)} %collective-permute-done.3.refs_1_, ...), custom_call_target="tpu_custom_call" | custom-call | flops 805306368 | bytes 1048576 | tf_op jit(solution)/shard_map/attend/pallas_call | solution.py:337
  22.6 1.4 %collective-permute-done.4.ring_in = bf16[2,512,128]{2,1,0:T(8,128)(2,1)S(1)} collective-permute-done((bf16[2,512,128]{2,1,0:T(8,128)(2,1)S(1)}, bf16[2,512,128]{2,1,0:T(8,128)(2,1)S(1)}, u32[]{:S(2)}, u32[]{:S(2)}) %collective-permute-start.4) | collective-permute-done | bytes 262176 | tf_op jit(solution)/shard_map/ppermute | solution.py:29
  26.0 4.0 %collective-permute-done.7.refs_3_ = bf16[2,384,128]{2,1,0:T(8,128)(2,1)S(1)} collective-permute-done((bf16[2,384,128]{2,1,0:T(8,128)(2,1)S(1)}, bf16[2,384,128]{2,1,0:T(8,128)(2,1)S(1)}, u32[]{:S(2)}, u32[]{:S(2)}) %collective-permute-start.7) | collective-permute-done | bytes 196640 | tf_op jit(solution)/shard_map/ppermute | solution.py:29
  30.0 3.4 %attend.9 = (f32[2,128,1024]{2,1,0:T(8,128)S(1)}, f32[2,896,128]{2,1,0:T(8,128)S(1)}) custom-call(s32[2]{0:T(128)S(1)} %pad_add_fusion.meta, s32[16]{0:T(128)S(1)} %copy-done.5, bf16[272,1024]{1,0:T(8,128)(2,1)S(1)} %get-tuple-element.55.refs_0_, bf16[272,1024]{1,0:T(8,128)(2,1)S(1)} %collective-permute-done.3.refs_1_, ...), custom_call_target="tpu_custom_call", output_to_operand_aliasing={{0}: (6, {})} | custom-call | flops 805306368 | bytes 1048576 | tf_op jit(solution)/shard_map/attend/pallas_call | solution.py:337
  35.7 3.8 %collective-permute-done.9.refs_3_ = bf16[2,384,128]{2,1,0:T(8,128)(2,1)S(1)} collective-permute-done((bf16[2,384,128]{2,1,0:T(8,128)(2,1)S(1)}, bf16[2,384,128]{2,1,0:T(8,128)(2,1)S(1)}, u32[]{:S(2)}, u32[]{:S(2)}) %collective-permute-start.9) | collective-permute-done | bytes 196640 | tf_op jit(solution)/shard_map/ppermute | solution.py:29
  39.5 3.4 %attend.10 = (f32[2,128,1024]{2,1,0:T(8,128)S(1)}, f32[2,896,128]{2,1,0:T(8,128)S(1)}) custom-call(s32[2]{0:T(128)S(1)} %pad_add_fusion.meta, s32[16]{0:T(128)S(1)} %copy-done.5, bf16[272,1024]{1,0:T(8,128)(2,1)S(1)} %get-tuple-element.55.refs_0_, bf16[272,1024]{1,0:T(8,128)(2,1)S(1)} %collective-permute-done.3.refs_1_, ...), custom_call_target="tpu_custom_call", output_to_operand_aliasing={{0}: (6, {})} | custom-call | flops 805306368 | bytes 1048576 | tf_op jit(solution)/shard_map/attend/pallas_call | solution.py:337
  42.9 3.3 %attend.11 = (f32[2,128,1024]{2,1,0:T(8,128)S(1)}, f32[2,512,128]{2,1,0:T(8,128)S(1)}, bf16[2,384,128]{2,1,0:T(8,128)(2,1)S(1)}) custom-call(s32[2]{0:T(128)S(1)} %pad_add_fusion.meta, s32[16]{0:T(128)S(1)} %copy-done.5, bf16[272,1024]{1,0:T(8,128)(2,1)S(1)} %collective-permute-done.11.refs_0_, bf16[272,1024]{1,0:T(8,128)(2,1)S(1)} %collective-permute-done.12.refs_1_, ...), custom_call_target="tpu_custom_call" | custom-call | flops 805306368 | bytes 1048576 | tf_op jit(solution)/shard_map/attend/pallas_call | solution.py:337
  47.5 3.4 %attend.12 = (f32[2,128,1024]{2,1,0:T(8,128)S(1)}, f32[2,512,128]{2,1,0:T(8,128)S(1)}, bf16[2,384,128]{2,1,0:T(8,128)(2,1)S(1)}) custom-call(s32[2]{0:T(128)S(1)} %pad_add_fusion.meta, s32[16]{0:T(128)S(1)} %copy-done.5, bf16[272,1024]{1,0:T(8,128)(2,1)S(1)} %collective-permute-done.11.refs_0_, ...), custom_call_target="tpu_custom_call", output_to_operand_aliasing={{0}: (6, {})} | custom-call | flops 805306368 | bytes 1048576 | tf_op jit(solution)/shard_map/attend/pallas_call | solution.py:337
  53.1 3.4 %attend.13 = (f32[2,128,1024]{2,1,0:T(8,128)S(1)}, f32[2,512,128]{2,1,0:T(8,128)S(1)}, bf16[2,384,128]{2,1,0:T(8,128)(2,1)S(1)}) custom-call(s32[2]{0:T(128)S(1)} %pad_add_fusion.meta, s32[16]{0:T(128)S(1)} %copy-done.5, bf16[272,1024]{1,0:T(8,128)(2,1)S(1)} %collective-permute-done.11.refs_0_, ...), custom_call_target="tpu_custom_call", output_to_operand_aliasing={{0}: (6, {})} | custom-call | flops 805306368 | bytes 1048576 | tf_op jit(solution)/shard_map/attend/pallas_call | solution.py:337
  56.5 1.9 %collective-permute-done.15.back = bf16[2,384,128]{2,1,0:T(8,128)(2,1)S(1)} collective-permute-done((bf16[2,384,128]{2,1,0:T(8,128)(2,1)S(1)}, bf16[2,384,128]{2,1,0:T(8,128)(2,1)S(1)}, u32[]{:S(2)}, u32[]{:S(2)}) %collective-permute-start.15) | collective-permute-done | bytes 196640 | tf_op jit(solution)/shard_map/ppermute | solution.py:29
  60.2 2.2 %collective-permute-done.10.refs_3_ = bf16[2,384,128]{2,1,0:T(8,128)(2,1)S(1)} collective-permute-done((bf16[2,384,128]{2,1,0:T(8,128)(2,1)S(1)}, bf16[2,384,128]{2,1,0:T(8,128)(2,1)S(1)}, u32[]{:S(2)}, u32[]{:S(2)}) %collective-permute-start.10) | collective-permute-done | bytes 196640 | tf_op jit(solution)/shard_map/ppermute | solution.py:29
  62.5 3.4 %attend.14 = (bf16[128,1024]{1,0:T(8,128)(2,1)S(1)}, bf16[128,1024]{1,0:T(8,128)(2,1)S(1)}, f32[2,896,128]{2,1,0:T(8,128)S(1)}) custom-call(s32[2]{0:T(128)S(1)} %pad_add_fusion.meta, s32[16]{0:T(128)S(1)} %copy-done.5, bf16[272,1024]{1,0:T(8,128)(2,1)S(1)} %collective-permute-done.11.refs_0_, bf16[272,1024]{1,0:T(8,128)(2,1)S(1)} %collective-permute-done.12.refs_1_, ...), custom_call_target="tpu_custom_call" | custom-call | flops 805306368 | bytes 1048576 | tf_op jit(solution)/shard_map/attend/pallas_call | solution.py:337
  67.8 1.6 %collective-permute-start.20 = (bf16[128,1280]{1,0:T(8,128)(2,1)S(1)}, bf16[128,1280]{1,0:T(8,128)(2,1)S(1)}, u32[]{:S(2)}, u32[]{:S(2)}) collective-permute-start(bf16[128,1280]{1,0:T(8,128)(2,1)S(1)} %get-tuple-element.92), channel_id=1, source_target_pairs={{0,2},{1,3},{2,0},{3,1},{4,6},{5,7},{6,4},{7,5},{8,10},{9,11},{10,... | collective-permute-start | bytes 983048 | tf_op jit(solution)/shard_map/ppermute | solution.py:33
  69.3 3.4 %attend.15 = (bf16[128,1024]{1,0:T(8,128)(2,1)S(1)}, bf16[128,1024]{1,0:T(8,128)(2,1)S(1)}, f32[2,512,128]{2,1,0:T(8,128)S(1)}, bf16[2,384,128]{2,1,0:T(8,128)(2,1)S(1)}) custom-call(s32[2]{0:T(128)S(1)} %pad_add_fusion.meta, s32[16]{0:T(128)S(1)} %copy-done.5, bf16[272,1024]{1,0:T(8,128)(2,1)S(1)} %get-tuple-element.55.refs_0_, ...), custom_call_target="tpu_custom_call" | custom-call | flops 805306368 | bytes 1048576 | tf_op jit(solution)/shard_map/attend/pallas_call | solution.py:337
  76.3 3.9 %collective-permute-done.22.back = bf16[2,384,128]{2,1,0:T(8,128)(2,1)S(1)} collective-permute-done((bf16[2,384,128]{2,1,0:T(8,128)(2,1)S(1)}, bf16[2,384,128]{2,1,0:T(8,128)(2,1)S(1)}, u32[]{:S(2)}, u32[]{:S(2)}) %collective-permute-start.22) | collective-permute-done | bytes 196640 | tf_op jit(solution)/shard_map/ppermute | solution.py:29
  80.9 1.7 %collective-permute-start.23 = (bf16[2,128,128]{2,1,0:T(8,128)(2,1)S(1)}, bf16[2,128,128]{2,1,0:T(8,128)(2,1)S(1)}, u32[]{:S(2)}, u32[]{:S(2)}) collective-permute-start(bf16[2,128,128]{2,1,0:T(8,128)(2,1)S(1)} %get-tuple-element.98), channel_id=1, source_target_pairs={{0,8},{1,9},{2,10},{3,11},{4,12},{5,13},{6,14},{7,15},{8,16},{9,17... | collective-permute-start | bytes 196616 | tf_op jit(solution)/shard_map/ppermute | solution.py:39
  82.6 2.6 %collective-permute-start.25 = (bf16[2,128,128]{2,1,0:T(8,128)(2,1)S(1)}, bf16[2,128,128]{2,1,0:T(8,128)(2,1)S(1)}, u32[]{:S(2)}, u32[]{:S(2)}) collective-permute-start(bf16[2,128,128]{2,1,0:T(8,128)(2,1)S(1)} %get-tuple-element.100), channel_id=1, source_target_pairs={{0,10},{1,11},{2,8},{3,9},{4,14},{5,15},{6,12},{7,13},{8,18},{9,19... | collective-permute-start | bytes 196616 | tf_op jit(solution)/shard_map/ppermute | solution.py:39
  86.2 1.5 %place_heads.1 = (bf16[1,128,4096]{2,1,0:T(8,128)(2,1)}, f32[8,128]{1,0:T(8,128)S(1)}) custom-call(s32[2]{0:T(128)S(1)} %pad_add_fusion.meta, bf16[128,1024]{1,0:T(8,128)(2,1)S(1)} %get-tuple-element.86.dq_own, bf16[128,640]{1,0:T(8,128)(2,1)S(1)} %collective-permute-done.18.near_one, bf16[128,640]{1,0:T(8,128)(2,1)S(1)} %collective-permute-done.19.near_two, ...), custom_call_target="tpu_custom_call" | custom-call | tf_op jit(solution)/shard_map/place_heads/pallas_call | solution.py:217
  90.2 1.7 %collective-permute-done.26.hop3 = bf16[2,128,128]{2,1,0:T(8,128)(2,1)S(1)} collective-permute-done((bf16[2,128,128]{2,1,0:T(8,128)(2,1)S(1)}, bf16[2,128,128]{2,1,0:T(8,128)(2,1)S(1)}, u32[]{:S(2)}, u32[]{:S(2)}) %collective-permute-start.26) | collective-permute-done | bytes 65568 | tf_op jit(solution)/shard_map/ppermute | solution.py:39
  (70 shorter events, 29.4 us)
Async XLA Ops:
  3.1 8.2 %collective-permute-start = (bf16[2,128,128]{2,1,0:T(8,128)(2,1)S(1)}, bf16[2,128,128]{2,1,0:T(8,128)(2,1)S(1)}, u32[]{:S(2)}, u32[]{:S(2)}) collective-permute-start(bf16[2,128,128]{2,1,0:T(8,128)(2,1)S(1)} %get-tuple-element.57), channel_id=1, source_target_pairs={{0,1},{1,0},{2,3},{3,2},{4,5},{5,4},{6,7},{7,6},{8,9},{9,8},{10,11... | collective-permute-start | bytes 196616 | tf_op jit(solution)/shard_map/ppermute | solution.py:33
  3.7 7.7 %collective-permute-start.1 = (bf16[2,128,128]{2,1,0:T(8,128)(2,1)S(1)}, bf16[2,128,128]{2,1,0:T(8,128)(2,1)S(1)}, u32[]{:S(2)}, u32[]{:S(2)}) collective-permute-start(bf16[2,128,128]{2,1,0:T(8,128)(2,1)S(1)} %get-tuple-element.58), channel_id=1, source_target_pairs={{0,2},{1,3},{2,0},{3,1},{4,6},{5,7},{6,4},{7,5},{8,10},{9,11},{10,... | collective-permute-start | bytes 196616 | tf_op jit(solution)/shard_map/ppermute | solution.py:33
  11.9 7.4 %collective-permute-start.3 = (bf16[272,1024]{1,0:T(8,128)(2,1)S(1)}, bf16[272,1024]{1,0:T(8,128)(2,1)S(1)}, u32[]{:S(2)}, u32[]{:S(2)}) collective-permute-start(bf16[272,1024]{1,0:T(8,128)(2,1)S(1)} %later.3), channel_id=1, source_target_pairs={{0,1},{1,0},{2,3},{3,2},{4,5},{5,4},{6,7},{7,6},{8,9},{9,8},{10,11... | collective-permute-start | bytes 1671176 | tf_op jit(solution)/shard_map/ppermute | solution.py:33
  12.1 7.2 %collective-permute-start.5 = (bf16[2,384,128]{2,1,0:T(8,128)(2,1)S(1)}, bf16[2,384,128]{2,1,0:T(8,128)(2,1)S(1)}, u32[]{:S(2)}, u32[]{:S(2)}) collective-permute-start(bf16[2,384,128]{2,1,0:T(8,128)(2,1)S(1)} %get-tuple-element.60.refs_1_), channel_id=1, source_target_pairs={{4,0},{5,1},{6,2},{7,3},{0,4},{1,5},{2,6},{3,7},{12,8},{13,9},{14,... | collective-permute-start | bytes 589832 | tf_op jit(solution)/shard_map/ppermute | solution.py:29
  14.1 10.0 %collective-permute-start.4 = (bf16[2,512,128]{2,1,0:T(8,128)(2,1)S(1)}, bf16[2,512,128]{2,1,0:T(8,128)(2,1)S(1)}, u32[]{:S(2)}, u32[]{:S(2)}) collective-permute-start(bf16[2,512,128]{2,1,0:T(8,128)(2,1)S(1)} %get-tuple-element.61.refs_2_), channel_id=1, source_target_pairs={{24,0},{0,8},{8,16},{16,24},{25,1},{1,9},{9,17},{17,25},{26,2},{2,... | collective-permute-start | bytes 786440 | tf_op jit(solution)/shard_map/ppermute | solution.py:29
  15.7 27.2 %collective-permute-start.11 = (bf16[272,1024]{1,0:T(8,128)(2,1)S(1)}, bf16[272,1024]{1,0:T(8,128)(2,1)S(1)}, u32[]{:S(2)}, u32[]{:S(2)}) collective-permute-start(bf16[272,1024]{1,0:T(8,128)(2,1)S(1)} %later.4), channel_id=1, source_target_pairs={{0,2},{1,3},{2,0},{3,1},{4,6},{5,7},{6,4},{7,5},{8,10},{9,11},{10,... | collective-permute-start | bytes 1671176 | tf_op jit(solution)/shard_map/ppermute | solution.py:33
  17.2 25.7 %collective-permute-start.12 = (bf16[272,1024]{1,0:T(8,128)(2,1)S(1)}, bf16[272,1024]{1,0:T(8,128)(2,1)S(1)}, u32[]{:S(2)}, u32[]{:S(2)}) collective-permute-start(bf16[272,1024]{1,0:T(8,128)(2,1)S(1)} %later.5), channel_id=1, source_target_pairs={{0,3},{1,2},{2,1},{3,0},{4,7},{5,6},{6,5},{7,4},{8,11},{9,10},{10,... | collective-permute-start | bytes 1671176 | tf_op jit(solution)/shard_map/ppermute | solution.py:33
  24.6 9.1 %collective-permute-start.6 = (bf16[2,512,128]{2,1,0:T(8,128)(2,1)S(1)}, bf16[2,512,128]{2,1,0:T(8,128)(2,1)S(1)}, u32[]{:S(2)}, u32[]{:S(2)}) collective-permute-start(bf16[2,512,128]{2,1,0:T(8,128)(2,1)S(1)} %get-tuple-element.63.refs_2_), channel_id=1, source_target_pairs={{24,0},{0,8},{8,16},{16,24},{25,1},{1,9},{9,17},{17,25},{26,2},{2,... | collective-permute-start | bytes 786440 | tf_op jit(solution)/shard_map/ppermute | solution.py:29
  35.1 16.6 %collective-permute-start.8 = (bf16[2,512,128]{2,1,0:T(8,128)(2,1)S(1)}, bf16[2,512,128]{2,1,0:T(8,128)(2,1)S(1)}, u32[]{:S(2)}, u32[]{:S(2)}) collective-permute-start(bf16[2,512,128]{2,1,0:T(8,128)(2,1)S(1)} %get-tuple-element.66.refs_2_), channel_id=1, source_target_pairs={{24,0},{0,8},{8,16},{16,24},{25,1},{1,9},{9,17},{17,25},{26,2},{2,... | collective-permute-start | bytes 786440 | tf_op jit(solution)/shard_map/ppermute | solution.py:29
  46.2 6.9 %collective-permute-start.13 = (bf16[2,384,128]{2,1,0:T(8,128)(2,1)S(1)}, bf16[2,384,128]{2,1,0:T(8,128)(2,1)S(1)}, u32[]{:S(2)}, u32[]{:S(2)}) collective-permute-start(bf16[2,384,128]{2,1,0:T(8,128)(2,1)S(1)} %get-tuple-element.78), channel_id=1, source_target_pairs={{4,0},{5,1},{6,2},{7,3},{0,4},{1,5},{2,6},{3,7},{12,8},{13,9},{14,... | collective-permute-start | bytes 589832 | tf_op jit(solution)/shard_map/ppermute | solution.py:29
  50.9 7.4 %collective-permute-start.15 = (bf16[2,384,128]{2,1,0:T(8,128)(2,1)S(1)}, bf16[2,384,128]{2,1,0:T(8,128)(2,1)S(1)}, u32[]{:S(2)}, u32[]{:S(2)}) collective-permute-start(bf16[2,384,128]{2,1,0:T(8,128)(2,1)S(1)} %get-tuple-element.84), channel_id=1, source_target_pairs={{4,0},{5,1},{6,2},{7,3},{0,4},{1,5},{2,6},{3,7},{12,8},{13,9},{14,... | collective-permute-start | bytes 589832 | tf_op jit(solution)/shard_map/ppermute | solution.py:29
  51.7 10.8 %collective-permute-start.10 = (bf16[2,384,128]{2,1,0:T(8,128)(2,1)S(1)}, bf16[2,384,128]{2,1,0:T(8,128)(2,1)S(1)}, u32[]{:S(2)}, u32[]{:S(2)}) collective-permute-start(bf16[2,384,128]{2,1,0:T(8,128)(2,1)S(1)} %get-tuple-element.70), channel_id=1, source_target_pairs={{4,0},{5,1},{6,2},{7,3},{0,4},{1,5},{2,6},{3,7},{12,8},{13,9},{14,... | collective-permute-start | bytes 589832 | tf_op jit(solution)/shard_map/ppermute | solution.py:29
  58.4 8.4 %collective-permute-start.16 = (bf16[2,512,128]{2,1,0:T(8,128)(2,1)S(1)}, bf16[2,512,128]{2,1,0:T(8,128)(2,1)S(1)}, u32[]{:S(2)}, u32[]{:S(2)}) collective-permute-start(bf16[2,512,128]{2,1,0:T(8,128)(2,1)S(1)} %pack_sum.2), channel_id=1, source_target_pairs={{24,0},{0,8},{8,16},{16,24},{25,1},{1,9},{9,17},{17,25},{26,2},{2,... | collective-permute-start | bytes 786440 | tf_op jit(solution)/shard_map/ppermute | solution.py:29
  59.7 6.1 %collective-permute-start.14 = (bf16[2,384,128]{2,1,0:T(8,128)(2,1)S(1)}, bf16[2,384,128]{2,1,0:T(8,128)(2,1)S(1)}, u32[]{:S(2)}, u32[]{:S(2)}) collective-permute-start(bf16[2,384,128]{2,1,0:T(8,128)(2,1)S(1)} %get-tuple-element.82), channel_id=1, source_target_pairs={{4,0},{5,1},{6,2},{7,3},{0,4},{1,5},{2,6},{3,7},{12,8},{13,9},{14,... | collective-permute-start | bytes 589832 | tf_op jit(solution)/shard_map/ppermute | solution.py:29
  66.9 8.2 %collective-permute-start.17 = (bf16[2,512,128]{2,1,0:T(8,128)(2,1)S(1)}, bf16[2,512,128]{2,1,0:T(8,128)(2,1)S(1)}, u32[]{:S(2)}, u32[]{:S(2)}) collective-permute-start(bf16[2,512,128]{2,1,0:T(8,128)(2,1)S(1)} %pack_sum.3.refs_6_), channel_id=1, source_target_pairs={{24,0},{0,8},{8,16},{16,24},{25,1},{1,9},{9,17},{17,25},{26,2},{2,... | collective-permute-start | bytes 786440 | tf_op jit(solution)/shard_map/ppermute | solution.py:29
  67.8 14.8 %collective-permute-start.20 = (bf16[128,1280]{1,0:T(8,128)(2,1)S(1)}, bf16[128,1280]{1,0:T(8,128)(2,1)S(1)}, u32[]{:S(2)}, u32[]{:S(2)}) collective-permute-start(bf16[128,1280]{1,0:T(8,128)(2,1)S(1)} %get-tuple-element.92), channel_id=1, source_target_pairs={{0,2},{1,3},{2,0},{3,1},{4,6},{5,7},{6,4},{7,5},{8,10},{9,11},{10,... | collective-permute-start | bytes 983048 | tf_op jit(solution)/shard_map/ppermute | solution.py:33
  69.3 13.3 %collective-permute-start.21 = (bf16[128,1280]{1,0:T(8,128)(2,1)S(1)}, bf16[128,1280]{1,0:T(8,128)(2,1)S(1)}, u32[]{:S(2)}, u32[]{:S(2)}) collective-permute-start(bf16[128,1280]{1,0:T(8,128)(2,1)S(1)} %get-tuple-element.93), channel_id=1, source_target_pairs={{0,3},{1,2},{2,1},{3,0},{4,7},{5,6},{6,5},{7,4},{8,11},{9,10},{10,... | collective-permute-start | bytes 983048 | tf_op jit(solution)/shard_map/ppermute | solution.py:33
  72.7 7.5 %collective-permute-start.22 = (bf16[2,384,128]{2,1,0:T(8,128)(2,1)S(1)}, bf16[2,384,128]{2,1,0:T(8,128)(2,1)S(1)}, u32[]{:S(2)}, u32[]{:S(2)}) collective-permute-start(bf16[2,384,128]{2,1,0:T(8,128)(2,1)S(1)} %get-tuple-element.97), channel_id=1, source_target_pairs={{4,0},{5,1},{6,2},{7,3},{0,4},{1,5},{2,6},{3,7},{12,8},{13,9},{14,... | collective-permute-start | bytes 589832 | tf_op jit(solution)/shard_map/ppermute | solution.py:29
  75.7 9.4 %collective-permute-start.18 = (bf16[128,640]{1,0:T(8,128)(2,1)S(1)}, bf16[128,640]{1,0:T(8,128)(2,1)S(1)}, u32[]{:S(2)}, u32[]{:S(2)}) collective-permute-start(bf16[128,640]{1,0:T(8,128)(2,1)S(1)} %get-tuple-element.89), channel_id=1, source_target_pairs={{0,1},{1,0},{2,3},{3,2},{4,5},{5,4},{6,7},{7,6},{8,9},{9,8},{10,11... | collective-permute-start | bytes 491528 | tf_op jit(solution)/shard_map/ppermute | solution.py:33
  75.8 10.4 %collective-permute-start.19 = (bf16[128,640]{1,0:T(8,128)(2,1)S(1)}, bf16[128,640]{1,0:T(8,128)(2,1)S(1)}, u32[]{:S(2)}, u32[]{:S(2)}) collective-permute-start(bf16[128,640]{1,0:T(8,128)(2,1)S(1)} %get-tuple-element.90), channel_id=1, source_target_pairs={{0,1},{1,0},{2,3},{3,2},{4,5},{5,4},{6,7},{7,6},{8,9},{9,8},{10,11... | collective-permute-start | bytes 491528 | tf_op jit(solution)/shard_map/ppermute | solution.py:33
  80.9 6.9 %collective-permute-start.23 = (bf16[2,128,128]{2,1,0:T(8,128)(2,1)S(1)}, bf16[2,128,128]{2,1,0:T(8,128)(2,1)S(1)}, u32[]{:S(2)}, u32[]{:S(2)}) collective-permute-start(bf16[2,128,128]{2,1,0:T(8,128)(2,1)S(1)} %get-tuple-element.98), channel_id=1, source_target_pairs={{0,8},{1,9},{2,10},{3,11},{4,12},{5,13},{6,14},{7,15},{8,16},{9,17... | collective-permute-start | bytes 196616 | tf_op jit(solution)/shard_map/ppermute | solution.py:39
  82.6 6.2 %collective-permute-start.24 = (bf16[2,128,128]{2,1,0:T(8,128)(2,1)S(1)}, bf16[2,128,128]{2,1,0:T(8,128)(2,1)S(1)}, u32[]{:S(2)}, u32[]{:S(2)}) collective-permute-start(bf16[2,128,128]{2,1,0:T(8,128)(2,1)S(1)} %get-tuple-element.99), channel_id=1, source_target_pairs={{0,9},{1,8},{2,11},{3,10},{4,13},{5,12},{6,15},{7,14},{8,17},{9,16... | collective-permute-start | bytes 196616 | tf_op jit(solution)/shard_map/ppermute | solution.py:39
  82.6 7.6 %collective-permute-start.25 = (bf16[2,128,128]{2,1,0:T(8,128)(2,1)S(1)}, bf16[2,128,128]{2,1,0:T(8,128)(2,1)S(1)}, u32[]{:S(2)}, u32[]{:S(2)}) collective-permute-start(bf16[2,128,128]{2,1,0:T(8,128)(2,1)S(1)} %get-tuple-element.100), channel_id=1, source_target_pairs={{0,10},{1,11},{2,8},{3,9},{4,14},{5,15},{6,12},{7,13},{8,18},{9,19... | collective-permute-start | bytes 196616 | tf_op jit(solution)/shard_map/ppermute | solution.py:39
  85.2 6.7 %collective-permute-start.26 = (bf16[2,128,128]{2,1,0:T(8,128)(2,1)S(1)}, bf16[2,128,128]{2,1,0:T(8,128)(2,1)S(1)}, u32[]{:S(2)}, u32[]{:S(2)}) collective-permute-start(bf16[2,128,128]{2,1,0:T(8,128)(2,1)S(1)} %get-tuple-element.101), channel_id=1, source_target_pairs={{0,11},{1,10},{2,9},{3,8},{4,15},{5,14},{6,13},{7,12},{8,19},{9,18... | collective-permute-start | bytes 196616 | tf_op jit(solution)/shard_map/ppermute | solution.py:39
  (10 other events, 28.2 us)

commit v2 on v1

--- a/solution.py
+++ b/solution.py
@@ -127,6 +127,11 @@
     )(ring, *after)
 
 
+def side_by_side(first, second, out):
+    out[0:2] = first[...]
+    out[2:4] = second[...]
+
+
 def total(part, n_packet, d_own, back, refs):
     tok = d_own.shape[1] // QUAD
     tail = d_own[:, tok:, :] + back[2 * part:2 * part + 2].astype(F32)
@@ -158,7 +163,7 @@
 def pack_cross(masks, meta, *refs):
     n = len(masks)
     dqs, (d_own, back), outs, whole = refs[:n], refs[n:n + 2], refs[n + 2:-1], refs[-1]
-    lead, tail = total(0, 0, d_own, back, ())
+    lead, tail = total(1, 0, d_own, back, ())
     tok, wide = dqs[0].shape
     whole[:, 0:tok, :] = lead
     whole[:, tok:, :] = tail
@@ -169,8 +174,8 @@
         out[:, wide + HD:] = part[1]
 
 
-def pack_near(meta, dq, d_own, back, _, first, second, kept, whole):
-    lead, tail = total(0, 0, d_own, back, ())
+def pack_near(meta, dq, d_own, back, first, second, kept, whole):
+    lead, tail = total(1, 0, d_own, back, ())
     tok, wide = dq.shape
     half = first.shape[1]
     whole[:, 0:tok, :] = lead
@@ -258,48 +263,75 @@
     def base(group, shard):
         return layout[2 * group + shard // 2] * (2 * tok) + (shard % 2) * tok
 
-    for t, (mask, rows) in enumerate(zip(masks, (rows_a, rows_b))):
+    sets = []
+    for mask, rows in zip(masks, (rows_a, rows_b)):
         i = member(meta, mask)
         chunk = pl.ds(pl.multiple_of(i * tok, tok), window)
-        keys, vals, keys_t = kbuf[chunk, :], vbuf[chunk, :], kbuf_t[:, chunk]
         qbase = base(quad + i, z)
         gaps = [qbase - base((quad + i - n_far + c + n_blk) % n_blk, shard) for c in range(QUAD)]
-        row = lax.broadcasted_iota(jnp.int32, (tok, 2 * tok), 0)
-        col = lax.broadcasted_iota(jnp.int32, (tok, 2 * tok), 1) % tok
+        sets.append((rows, chunk, gaps))
+    row = lax.broadcasted_iota(jnp.int32, (tok, 2 * tok), 0)
+    col = lax.broadcasted_iota(jnp.int32, (tok, 2 * tok), 1) % tok
+    nt = (((1,), (1,)), ((), ()))
+    half = GROUP // 2
+    steps = [(t, part) for t in range(2) for part in range(2)]
+    scores = {}
+
+    def stacked(rows, start, heads):
+        return jnp.concatenate([rows[start:start + tok, h * HD:(h + 1) * HD] for h in heads], axis=0)
+
+    def score_part(t, part):
+        rows, chunk, _ = sets[t]
+        keys, vals = kbuf[chunk, :], vbuf[chunk, :]
+        for g in range(part * half, (part + 1) * half, 2):
+            query, dout = stacked(rows, 0, (g, g + 1)), stacked(rows, tok, (g, g + 1))
+            scores[t, g] = (
+                lax.dot_general(keys, query, nt, preferred_element_type=F32),
+                lax.dot_general(vals, dout, nt, preferred_element_type=F32),
+            )
+
+    def prob_part(t, part):
+        rows, _, gaps = sets[t]
         linked = (col - row + gaps[QUAD - 1]) >= 0
-
-        def stacked(start, heads):
-            return jnp.concatenate([rows[start:start + tok, h * HD:(h + 1) * HD] for h in heads], axis=0)
-
-        for g in range(GROUP // 2):
-            heads = (2 * g, 2 * g + 1)
-            query, dout = stacked(0, heads), stacked(tok, heads)
-            span = slice(2 * g * tok, (2 * g + 2) * tok)
+        for g in range(part * half, (part + 1) * half, 2):
+            score, dprob = scores.pop((t, g))
+            span = slice(g * tok, (g + 2) * tok)
             terms = rows[2 * tok:, span].astype(F32)
             lse, delta = terms[0:1] + terms[1:2], terms[2:3] + terms[3:4]
-            nt = (((1,), (1,)), ((), ()))
-            score = lax.dot_general(keys, query, nt, preferred_element_type=F32) * (SCALE * LOG2E)
-            dprob = lax.dot_general(vals, dout, nt, preferred_element_type=F32)
             for c in range(QUAD):
-                part = slice(c * tok, (c + 1) * tok)
+                at = slice(c * tok, (c + 1) * tok)
+                scaled = score[at] * (SCALE * LOG2E)
                 if c == QUAD - 1:
-                    prob = jnp.where(linked, jnp.exp2(score[part] - lse), 0.0)
+                    prob = jnp.where(linked, jnp.exp2(scaled - lse), 0.0)
                 else:
-                    prob = jnp.exp2(score[part] - jnp.where(gaps[c] > 0, lse, FAR))
-                probs[t, part, span] = prob.astype(BF16)
-                dscores[t, part, span] = (prob * (dprob[part] - delta)).astype(BF16)
-        query, dout = stacked(0, range(GROUP)), stacked(tok, range(GROUP))
-        dbuf[0, chunk, :] += jnp.dot(dscores[t], query, preferred_element_type=F32)
-        dbuf[1, chunk, :] += jnp.dot(probs[t], dout, preferred_element_type=F32)
-        dq = jnp.dot(keys_t, dscores[t], preferred_element_type=F32)
+                    prob = jnp.exp2(scaled - jnp.where(gaps[c] > 0, lse, FAR))
+                probs[t, at, span] = prob.astype(BF16)
+                dscores[t, at, span] = (prob * (dprob[at] - delta)).astype(BF16)
+
+    def grad_part(t, part):
+        rows, chunk, _ = sets[t]
+        heads = range(part * half, (part + 1) * half)
+        query, dout = stacked(rows, 0, heads), stacked(rows, tok, heads)
+        span = slice(part * half * tok, (part + 1) * half * tok)
+        dbuf[0, chunk, :] += jnp.dot(dscores[t, :, span], query, preferred_element_type=F32)
+        dbuf[1, chunk, :] += jnp.dot(probs[t, :, span], dout, preferred_element_type=F32)
+        dq = jnp.dot(kbuf_t[:, chunk], dscores[t, :, span], preferred_element_type=F32)
         if not first:
-            dq = dq + acc_in[t]
+            dq = dq + acc_in[t, :, span]
         if last:
-            for h in range(GROUP):
+            for n, h in enumerate(heads):
                 at = slice(h * HD, (h + 1) * HD)
-                dq_outs[t][:, at] = (dq[:, h * tok:(h + 1) * tok] * SCALE).T.astype(BF16)
+                dq_outs[t][:, at] = (dq[:, n * tok:(n + 1) * tok] * SCALE).T.astype(BF16)
         else:
-            acc_out[t] = dq
+            acc_out[t, :, span] = dq
+
+    for n in range(len(steps) + 2):
+        if n < len(steps):
+            score_part(*steps[n])
+        if 1 <= n <= len(steps):
+            prob_part(*steps[n - 1])
+        if n >= 2:
+            grad_part(*steps[n - 2])
 
     if closing:
         for plane, scale in ((0, SCALE), (1, 1.0)):
@@ -350,7 +382,7 @@
             pltpu.VMEM((2, QUAD * tok, GROUP * tok), BF16),
         ],
         input_output_aliases=aliases,
-        compiler_params=pltpu.CompilerParams(vmem_limit_bytes=14 * 2**20),
+        compiler_params=pltpu.CompilerParams(vmem_limit_bytes=18 * 2**20),
         cost_estimate=pl.CostEstimate(
             flops=COVER * 4 * tok * GROUP * tok * HD, bytes_accessed=2**20, transcendentals=0
         ),
@@ -387,6 +419,13 @@
         ring, tail = held(shifted(keys[-1][0], "head", 1), after)
         keys.append([ring, shifted(tail, "blk", QUAD)])
 
+    def keys_and_back(tail, grads):
+        pair = ((4, *tail_of[0][1:]), BF16)
+        if n_blk != 2 * QUAD:
+            tail, grads = shifted(tail, "blk", QUAD), shifted(grads, "blk", -QUAD)
+        both = small_call(side_by_side, [pair], [VMEM] * 2, [tail, grads])[0]
+        return shifted(both, "blk", QUAD) if n_blk == 2 * QUAD else both
+
     def call(pair, lag, after=(), parts=1, carried=None):
         heads, grads = attend_call(
             lag, (2 * pair, 2 * pair + 1), n_blk, n_z, meta, block_layout, rows[2 * pair:2 * pair + 2], keys[lag],
@@ -411,24 +450,25 @@
     call(0, 1)
     pass_keys([accs[0]])
     call(0, 2)
-    pass_keys([accs[0]])
-    back_zero = send_back(call(1, 0, [accs[0]]))
+    ring, tail = held(shifted(keys[-1][0], "head", 1), [accs[0]])
+    back_zero = keys_and_back(tail, call(1, 0, [accs[0]]))
+    keys.append([ring, back_zero])
     back_one = send_back(call(1, 1))
-    back_two = send_back(call(1, 2, [back_zero]))
-    _, packet = pass_sums(1, 0, back_one, [], accs[1])
+    back_two = send_back(call(1, 2))
     call(1, 3)
+    _, packet = pass_sums(1, 0, back_one, [], accs[1][0])
     cross = ((tok, wide + 2 * HD), BF16)
     whole = pltpu.VMEM(ring_of[0], F32)
     sent = small_call(
         functools.partial(pack_cross, (2, 3)), [cross] * 2, [SMEM] + [VMEM] * 4,
         [meta, *accs[1], sums[0], back_zero], scratch=[whole], cost=2**20,
     )
-    block, packet = pass_sums(2, 0, back_two, packet, accs[1][0])
-    back_three = send_back(call(0, 3, [block]))
+    back_three = send_back(call(0, 3, [accs[1][0], sent[0], back_two]))
+    _, packet = pass_sums(2, 0, back_two, packet, sums[3])
     near_half = ((tok, (wide + 2 * HD) // 2), BF16)
     near_one, near_two, kept = small_call(
-        pack_near, [near_half] * 2 + [(piece[0], F32)], [SMEM] + [VMEM] * 3 + [ANY],
-        [meta, accs[0][1], sums[0], back_zero, *packet], scratch=[whole], cost=2**20,
+        pack_near, [near_half] * 2 + [(piece[0], F32)], [SMEM] + [VMEM] * 3,
+        [meta, accs[0][1], sums[0], back_zero], scratch=[whole], cost=2**20,
     )
     near_one, near_two = crossed(near_one, 1), crossed(near_two, 1)
     got = [crossed(part, mask) for mask, part in enumerate(sent, 2)]

time: 93.5 us -> 91.4 us (0.978)
  waiting for transfers between devices: 26 us -> 24.4 us
  starting transfers between devices: 26.4 us -> 25.4 us
    ppermute x13 -> x12, starting transfers between devices: 14.1 us -> 12.9 us  [shifted(): return lax.ppermute(block, axis, route)]
    ppermute x4, waiting for transfers between devices: 4.11 us -> 3.03 us  [hopped(): return lax.ppermute(block, ('head', 'blk'), route)]
    ppermute x13 -> x12, waiting for transfers between devices: 21.9 us -> 21.4 us  [shifted(): return lax.ppermute(block, axis, route)]
    pallas_call x10 -> x11, Pallas kernels: 7.3 us -> 7.34 us  [small_call(): pl.pallas_call(body, out_shape=shapes, in_specs=specs, out_specs=[ANY if...]
  transfers between devices with their start and end apart: 27 -> 26, of which waited for: 13 -> 12; matrix products, arithmetic and copies ran while one was open for 0% -> 0% of each run, Pallas kernels for 34% -> 35%
where the time goes in v2:
time: 91.4 us; the launch traced here: 91.1 us
  Pallas kernels  34.7 us (38%)
  starting transfers between devices  25.4 us (28%)
  waiting for transfers between devices  24.4 us (27%)
  local copies, waits for them, and re-layouts  5.58 us (6%)
    pallas_call x8, Pallas kernels, attend_call(): pl.pallas_call(functools.partial(attend, lag, masks, n_blk, n_z, first, l...  27.3 us
    ppermute x12, waiting for transfers between devices, shifted(): return lax.ppermute(block, axis, route)  21.4 us
    ppermute x12, starting transfers between devices, shifted(): return lax.ppermute(block, axis, route)  12.9 us
    pallas_call x11, Pallas kernels, small_call(): pl.pallas_call(body, out_shape=shapes, in_specs=specs, out_specs=[ANY if...  7.34 us
    ppermute x10, starting transfers between devices, crossed(): lax.ppermute(block, 'blk', [(i, i ^ mask) for i in range(lax.axis_size('b...  7.19 us
    unnamed x15, local copies, waits for them, and re-layouts  5.58 us
    ppermute x4, starting transfers between devices, hopped(): return lax.ppermute(block, ('head', 'blk'), route)  5.31 us
    ppermute x4, waiting for transfers between devices, hopped(): return lax.ppermute(block, ('head', 'blk'), route)  3.03 us
  transfers between devices with their start and end apart: 26, of which 12 were waited for; matrix products, arithmetic and copies ran while one was open for 0% of the time, Pallas kernels for 35%

profile of v2, /device:TPU:0, one launch (start us, length us, event | category | flops | bytes accessed | tf_op | source)
XLA Modules:
  0.0 91.1 jit_solution(3907983515670691210)
XLA Ops:
  3.7 2.6 %collective-permute-start.1 = (bf16[2,128,128]{2,1,0:T(8,128)(2,1)S(1)}, bf16[2,128,128]{2,1,0:T(8,128)(2,1)S(1)}, u32[]{:S(2)}, u32[]{:S(2)}) collective-permute-start(bf16[2,128,128]{2,1,0:T(8,128)(2,1)S(1)} %get-tuple-element.58), channel_id=1, source_target_pairs={{0,2},{1,3},{2,0},{3,1},{4,6},{5,7},{6,4},{7,5},{8,10},{9,11},{10,... | collective-permute-start | bytes 196616 | tf_op jit(solution)/shard_map/ppermute | solution.py:33
  12.1 2.0 %collective-permute-start.5 = (bf16[2,384,128]{2,1,0:T(8,128)(2,1)S(1)}, bf16[2,384,128]{2,1,0:T(8,128)(2,1)S(1)}, u32[]{:S(2)}, u32[]{:S(2)}) collective-permute-start(bf16[2,384,128]{2,1,0:T(8,128)(2,1)S(1)} %get-tuple-element.60.refs_1_), channel_id=1, source_target_pairs={{4,0},{5,1},{6,2},{7,3},{0,4},{1,5},{2,6},{3,7},{12,8},{13,9},{14,... | collective-permute-start | bytes 589832 | tf_op jit(solution)/shard_map/ppermute | solution.py:29
  14.1 1.6 %collective-permute-start.4 = (bf16[2,512,128]{2,1,0:T(8,128)(2,1)S(1)}, bf16[2,512,128]{2,1,0:T(8,128)(2,1)S(1)}, u32[]{:S(2)}, u32[]{:S(2)}) collective-permute-start(bf16[2,512,128]{2,1,0:T(8,128)(2,1)S(1)} %get-tuple-element.61.refs_2_), channel_id=1, source_target_pairs={{24,0},{0,8},{8,16},{16,24},{25,1},{1,9},{9,17},{17,25},{26,2},{2,... | collective-permute-start | bytes 786440 | tf_op jit(solution)/shard_map/ppermute | solution.py:29
  15.7 1.5 %collective-permute-start.10 = (bf16[272,1024]{1,0:T(8,128)(2,1)S(1)}, bf16[272,1024]{1,0:T(8,128)(2,1)S(1)}, u32[]{:S(2)}, u32[]{:S(2)}) collective-permute-start(bf16[272,1024]{1,0:T(8,128)(2,1)S(1)} %later.4), channel_id=1, source_target_pairs={{0,2},{1,3},{2,0},{3,1},{4,6},{5,7},{6,4},{7,5},{8,10},{9,11},{10,... | collective-permute-start | bytes 1671176 | tf_op jit(solution)/shard_map/ppermute | solution.py:33
  17.2 2.2 %collective-permute-done.5.refs_3_ = bf16[2,384,128]{2,1,0:T(8,128)(2,1)S(1)} collective-permute-done((bf16[2,384,128]{2,1,0:T(8,128)(2,1)S(1)}, bf16[2,384,128]{2,1,0:T(8,128)(2,1)S(1)}, u32[]{:S(2)}, u32[]{:S(2)}) %collective-permute-start.5) | collective-permute-done | bytes 196640 | tf_op jit(solution)/shard_map/ppermute | solution.py:29
  19.3 3.3 %attend.8 = (f32[2,128,1024]{2,1,0:T(8,128)S(1)}, f32[2,896,128]{2,1,0:T(8,128)S(1)}) custom-call(s32[2]{0:T(128)S(1)} %pad_add_fusion.meta, s32[16]{0:T(128)S(1)} %copy-done.5, bf16[272,1024]{1,0:T(8,128)(2,1)S(1)} %get-tuple-element.55.refs_0_, bf16[272,1024]{1,0:T(8,128)(2,1)S(1)} %collective-permute-done.3.refs_1_, ...), custom_call_target="tpu_custom_call" | custom-call | flops 805306368 | bytes 1048576 | tf_op jit(solution)/shard_map/attend/pallas_call | solution.py:369
  22.6 1.4 %collective-permute-done.4.ring_in = bf16[2,512,128]{2,1,0:T(8,128)(2,1)S(1)} collective-permute-done((bf16[2,512,128]{2,1,0:T(8,128)(2,1)S(1)}, bf16[2,512,128]{2,1,0:T(8,128)(2,1)S(1)}, u32[]{:S(2)}, u32[]{:S(2)}) %collective-permute-start.4) | collective-permute-done | bytes 262176 | tf_op jit(solution)/shard_map/ppermute | solution.py:29
  24.6 1.4 %collective-permute-start.6 = (bf16[2,512,128]{2,1,0:T(8,128)(2,1)S(1)}, bf16[2,512,128]{2,1,0:T(8,128)(2,1)S(1)}, u32[]{:S(2)}, u32[]{:S(2)}) collective-permute-start(bf16[2,512,128]{2,1,0:T(8,128)(2,1)S(1)} %get-tuple-element.63.refs_2_), channel_id=1, source_target_pairs={{24,0},{0,8},{8,16},{16,24},{25,1},{1,9},{9,17},{17,25},{26,2},{2,... | collective-permute-start | bytes 786440 | tf_op jit(solution)/shard_map/ppermute | solution.py:29
  26.1 4.0 %collective-permute-done.7.refs_3_ = bf16[2,384,128]{2,1,0:T(8,128)(2,1)S(1)} collective-permute-done((bf16[2,384,128]{2,1,0:T(8,128)(2,1)S(1)}, bf16[2,384,128]{2,1,0:T(8,128)(2,1)S(1)}, u32[]{:S(2)}, u32[]{:S(2)}) %collective-permute-start.7) | collective-permute-done | bytes 196640 | tf_op jit(solution)/shard_map/ppermute | solution.py:29
  30.0 3.4 %attend.9 = (f32[2,128,1024]{2,1,0:T(8,128)S(1)}, f32[2,896,128]{2,1,0:T(8,128)S(1)}) custom-call(s32[2]{0:T(128)S(1)} %pad_add_fusion.meta, s32[16]{0:T(128)S(1)} %copy-done.5, bf16[272,1024]{1,0:T(8,128)(2,1)S(1)} %get-tuple-element.55.refs_0_, bf16[272,1024]{1,0:T(8,128)(2,1)S(1)} %collective-permute-done.3.refs_1_, ...), custom_call_target="tpu_custom_call", output_to_operand_aliasing={{0}: (6, {})} | custom-call | flops 805306368 | bytes 1048576 | tf_op jit(solution)/shard_map/attend/pallas_call | solution.py:369
  35.7 3.7 %collective-permute-done.9.refs_3_ = bf16[2,384,128]{2,1,0:T(8,128)(2,1)S(1)} collective-permute-done((bf16[2,384,128]{2,1,0:T(8,128)(2,1)S(1)}, bf16[2,384,128]{2,1,0:T(8,128)(2,1)S(1)}, u32[]{:S(2)}, u32[]{:S(2)}) %collective-permute-start.9) | collective-permute-done | bytes 196640 | tf_op jit(solution)/shard_map/ppermute | solution.py:29
  39.5 3.4 %attend.10 = (f32[2,128,1024]{2,1,0:T(8,128)S(1)}, f32[2,896,128]{2,1,0:T(8,128)S(1)}) custom-call(s32[2]{0:T(128)S(1)} %pad_add_fusion.meta, s32[16]{0:T(128)S(1)} %copy-done.5, bf16[272,1024]{1,0:T(8,128)(2,1)S(1)} %get-tuple-element.55.refs_0_, bf16[272,1024]{1,0:T(8,128)(2,1)S(1)} %collective-permute-done.3.refs_1_, ...), custom_call_target="tpu_custom_call", output_to_operand_aliasing={{0}: (6, {})} | custom-call | flops 805306368 | bytes 1048576 | tf_op jit(solution)/shard_map/attend/pallas_call | solution.py:369
  42.9 3.3 %attend.11 = (f32[2,128,1024]{2,1,0:T(8,128)S(1)}, f32[2,512,128]{2,1,0:T(8,128)S(1)}, bf16[2,384,128]{2,1,0:T(8,128)(2,1)S(1)}) custom-call(s32[2]{0:T(128)S(1)} %pad_add_fusion.meta, s32[16]{0:T(128)S(1)} %copy-done.5, bf16[272,1024]{1,0:T(8,128)(2,1)S(1)} %collective-permute-done.10.refs_0_, bf16[272,1024]{1,0:T(8,128)(2,1)S(1)} %collective-permute-done.11.refs_1_, ...), custom_call_target="tpu_custom_call" | custom-call | flops 805306368 | bytes 1048576 | tf_op jit(solution)/shard_map/attend/pallas_call | solution.py:369
  47.6 3.5 %attend.12 = (f32[2,128,1024]{2,1,0:T(8,128)S(1)}, f32[2,512,128]{2,1,0:T(8,128)S(1)}, bf16[2,384,128]{2,1,0:T(8,128)(2,1)S(1)}) custom-call(s32[2]{0:T(128)S(1)} %pad_add_fusion.meta, s32[16]{0:T(128)S(1)} %copy-done.5, bf16[272,1024]{1,0:T(8,128)(2,1)S(1)} %collective-permute-done.10.refs_0_, ...), custom_call_target="tpu_custom_call", output_to_operand_aliasing={{0}: (6, {})} | custom-call | flops 805306368 | bytes 1048576 | tf_op jit(solution)/shard_map/attend/pallas_call | solution.py:369
  51.9 3.5 %attend.13 = (f32[2,128,1024]{2,1,0:T(8,128)S(1)}, f32[2,512,128]{2,1,0:T(8,128)S(1)}, bf16[2,384,128]{2,1,0:T(8,128)(2,1)S(1)}) custom-call(s32[2]{0:T(128)S(1)} %pad_add_fusion.meta, s32[16]{0:T(128)S(1)} %copy-done.5, bf16[272,1024]{1,0:T(8,128)(2,1)S(1)} %collective-permute-done.10.refs_0_, ...), custom_call_target="tpu_custom_call", output_to_operand_aliasing={{0}: (6, {})} | custom-call | flops 805306368 | bytes 1048576 | tf_op jit(solution)/shard_map/attend/pallas_call | solution.py:369
  55.3 1.3 %collective-permute-start.13 = (bf16[2,384,128]{2,1,0:T(8,128)(2,1)S(1)}, bf16[2,384,128]{2,1,0:T(8,128)(2,1)S(1)}, u32[]{:S(2)}, u32[]{:S(2)}) collective-permute-start(bf16[2,384,128]{2,1,0:T(8,128)(2,1)S(1)} %get-tuple-element.85), channel_id=1, source_target_pairs={{4,0},{5,1},{6,2},{7,3},{0,4},{1,5},{2,6},{3,7},{12,8},{13,9},{14,... | collective-permute-start | bytes 589832 | tf_op jit(solution)/shard_map/ppermute | solution.py:29
  56.7 1.7 %collective-permute-done.12.refs_3_.back = bf16[4,384,128]{2,1,0:T(8,128)(2,1)S(1)} collective-permute-done((bf16[4,384,128]{2,1,0:T(8,128)(2,1)S(1)}, bf16[4,384,128]{2,1,0:T(8,128)(2,1)S(1)}, u32[]{:S(2)}, u32[]{:S(2)}) %collective-permute-start.12) | collective-permute-done | bytes 393248 | tf_op jit(solution)/shard_map/ppermute | solution.py:29
  58.4 3.6 %attend.14 = (bf16[128,1024]{1,0:T(8,128)(2,1)S(1)}, bf16[128,1024]{1,0:T(8,128)(2,1)S(1)}, f32[2,896,128]{2,1,0:T(8,128)S(1)}) custom-call(s32[2]{0:T(128)S(1)} %pad_add_fusion.meta, s32[16]{0:T(128)S(1)} %copy-done.5, bf16[272,1024]{1,0:T(8,128)(2,1)S(1)} %collective-permute-done.10.refs_0_, bf16[272,1024]{1,0:T(8,128)(2,1)S(1)} %collective-permute-done.11.refs_1_, ...), custom_call_target="tpu_custom_call" | custom-call | flops 805306368 | bytes 1048576 | tf_op jit(solution)/shard_map/attend/pallas_call | solution.py:369
  64.7 3.4 %attend.15 = (bf16[128,1024]{1,0:T(8,128)(2,1)S(1)}, bf16[128,1024]{1,0:T(8,128)(2,1)S(1)}, f32[2,512,128]{2,1,0:T(8,128)S(1)}, bf16[2,384,128]{2,1,0:T(8,128)(2,1)S(1)}) custom-call(s32[2]{0:T(128)S(1)} %pad_add_fusion.meta, s32[16]{0:T(128)S(1)} %copy-done.5, bf16[272,1024]{1,0:T(8,128)(2,1)S(1)} %get-tuple-element.55.refs_0_, ...), custom_call_target="tpu_custom_call" | custom-call | flops 805306368 | bytes 1048576 | tf_op jit(solution)/shard_map/attend/pallas_call | solution.py:369
  68.7 1.5 %collective-permute-start.16 = (bf16[128,1280]{1,0:T(8,128)(2,1)S(1)}, bf16[128,1280]{1,0:T(8,128)(2,1)S(1)}, u32[]{:S(2)}, u32[]{:S(2)}) collective-permute-start(bf16[128,1280]{1,0:T(8,128)(2,1)S(1)} %get-tuple-element.84.refs_7_), channel_id=1, source_target_pairs={{0,2},{1,3},{2,0},{3,1},{4,6},{5,7},{6,4},{7,5},{8,10},{9,11},{10,... | collective-permute-start | bytes 983048 | tf_op jit(solution)/shard_map/ppermute | solution.py:33
  73.8 5.3 %collective-permute-done.21.packet = bf16[2,512,128]{2,1,0:T(8,128)(2,1)S(1)} collective-permute-done((bf16[2,512,128]{2,1,0:T(8,128)(2,1)S(1)}, bf16[2,512,128]{2,1,0:T(8,128)(2,1)S(1)}, u32[]{:S(2)}, u32[]{:S(2)}) %collective-permute-start.21) | collective-permute-done | bytes 262176 | tf_op jit(solution)/shard_map/ppermute | solution.py:29
  80.3 4.9 %collective-permute-start.25 = (bf16[2,128,128]{2,1,0:T(8,128)(2,1)S(1)}, bf16[2,128,128]{2,1,0:T(8,128)(2,1)S(1)}, u32[]{:S(2)}, u32[]{:S(2)}) collective-permute-start(bf16[2,128,128]{2,1,0:T(8,128)(2,1)S(1)} %get-tuple-element.101), channel_id=1, source_target_pairs={{0,11},{1,10},{2,9},{3,8},{4,15},{5,14},{6,13},{7,12},{8,19},{9,18... | collective-permute-start | bytes 196616 | tf_op jit(solution)/shard_map/ppermute | solution.py:39
  85.2 1.5 %place_heads.1 = (bf16[1,128,4096]{2,1,0:T(8,128)(2,1)}, f32[8,128]{1,0:T(8,128)S(1)}) custom-call(s32[2]{0:T(128)S(1)} %pad_add_fusion.meta, bf16[128,1024]{1,0:T(8,128)(2,1)S(1)} %get-tuple-element.86.dq_own, bf16[128,640]{1,0:T(8,128)(2,1)S(1)} %collective-permute-done.14.near_one, bf16[128,640]{1,0:T(8,128)(2,1)S(1)} %collective-permute-done.15.near_two, ...), custom_call_target="tpu_custom_call" | custom-call | tf_op jit(solution)/shard_map/place_heads/pallas_call | solution.py:222
  86.8 3.0 %collective-permute-done.24.hop2 = bf16[2,128,128]{2,1,0:T(8,128)(2,1)S(1)} collective-permute-done((bf16[2,128,128]{2,1,0:T(8,128)(2,1)S(1)}, bf16[2,128,128]{2,1,0:T(8,128)(2,1)S(1)}, u32[]{:S(2)}, u32[]{:S(2)}) %collective-permute-start.24) | collective-permute-done | bytes 65568 | tf_op jit(solution)/shard_map/ppermute | solution.py:39
  (69 shorter events, 23.3 us)
Async XLA Ops:
  3.1 8.2 %collective-permute-start = (bf16[2,128,128]{2,1,0:T(8,128)(2,1)S(1)}, bf16[2,128,128]{2,1,0:T(8,128)(2,1)S(1)}, u32[]{:S(2)}, u32[]{:S(2)}) collective-permute-start(bf16[2,128,128]{2,1,0:T(8,128)(2,1)S(1)} %get-tuple-element.57), channel_id=1, source_target_pairs={{0,1},{1,0},{2,3},{3,2},{4,5},{5,4},{6,7},{7,6},{8,9},{9,8},{10,11... | collective-permute-start | bytes 196616 | tf_op jit(solution)/shard_map/ppermute | solution.py:33
  3.7 7.7 %collective-permute-start.1 = (bf16[2,128,128]{2,1,0:T(8,128)(2,1)S(1)}, bf16[2,128,128]{2,1,0:T(8,128)(2,1)S(1)}, u32[]{:S(2)}, u32[]{:S(2)}) collective-permute-start(bf16[2,128,128]{2,1,0:T(8,128)(2,1)S(1)} %get-tuple-element.58), channel_id=1, source_target_pairs={{0,2},{1,3},{2,0},{3,1},{4,6},{5,7},{6,4},{7,5},{8,10},{9,11},{10,... | collective-permute-start | bytes 196616 | tf_op jit(solution)/shard_map/ppermute | solution.py:33
  11.9 7.4 %collective-permute-start.3 = (bf16[272,1024]{1,0:T(8,128)(2,1)S(1)}, bf16[272,1024]{1,0:T(8,128)(2,1)S(1)}, u32[]{:S(2)}, u32[]{:S(2)}) collective-permute-start(bf16[272,1024]{1,0:T(8,128)(2,1)S(1)} %later.3), channel_id=1, source_target_pairs={{0,1},{1,0},{2,3},{3,2},{4,5},{5,4},{6,7},{7,6},{8,9},{9,8},{10,11... | collective-permute-start | bytes 1671176 | tf_op jit(solution)/shard_map/ppermute | solution.py:33
  12.1 7.2 %collective-permute-start.5 = (bf16[2,384,128]{2,1,0:T(8,128)(2,1)S(1)}, bf16[2,384,128]{2,1,0:T(8,128)(2,1)S(1)}, u32[]{:S(2)}, u32[]{:S(2)}) collective-permute-start(bf16[2,384,128]{2,1,0:T(8,128)(2,1)S(1)} %get-tuple-element.60.refs_1_), channel_id=1, source_target_pairs={{4,0},{5,1},{6,2},{7,3},{0,4},{1,5},{2,6},{3,7},{12,8},{13,9},{14,... | collective-permute-start | bytes 589832 | tf_op jit(solution)/shard_map/ppermute | solution.py:29
  14.1 10.0 %collective-permute-start.4 = (bf16[2,512,128]{2,1,0:T(8,128)(2,1)S(1)}, bf16[2,512,128]{2,1,0:T(8,128)(2,1)S(1)}, u32[]{:S(2)}, u32[]{:S(2)}) collective-permute-start(bf16[2,512,128]{2,1,0:T(8,128)(2,1)S(1)} %get-tuple-element.61.refs_2_), channel_id=1, source_target_pairs={{24,0},{0,8},{8,16},{16,24},{25,1},{1,9},{9,17},{17,25},{26,2},{2,... | collective-permute-start | bytes 786440 | tf_op jit(solution)/shard_map/ppermute | solution.py:29
  15.7 27.2 %collective-permute-start.10 = (bf16[272,1024]{1,0:T(8,128)(2,1)S(1)}, bf16[272,1024]{1,0:T(8,128)(2,1)S(1)}, u32[]{:S(2)}, u32[]{:S(2)}) collective-permute-start(bf16[272,1024]{1,0:T(8,128)(2,1)S(1)} %later.4), channel_id=1, source_target_pairs={{0,2},{1,3},{2,0},{3,1},{4,6},{5,7},{6,4},{7,5},{8,10},{9,11},{10,... | collective-permute-start | bytes 1671176 | tf_op jit(solution)/shard_map/ppermute | solution.py:33
  17.2 25.7 %collective-permute-start.11 = (bf16[272,1024]{1,0:T(8,128)(2,1)S(1)}, bf16[272,1024]{1,0:T(8,128)(2,1)S(1)}, u32[]{:S(2)}, u32[]{:S(2)}) collective-permute-start(bf16[272,1024]{1,0:T(8,128)(2,1)S(1)} %later.5), channel_id=1, source_target_pairs={{0,3},{1,2},{2,1},{3,0},{4,7},{5,6},{6,5},{7,4},{8,11},{9,10},{10,... | collective-permute-start | bytes 1671176 | tf_op jit(solution)/shard_map/ppermute | solution.py:33
  24.1 6.0 %collective-permute-start.7 = (bf16[2,384,128]{2,1,0:T(8,128)(2,1)S(1)}, bf16[2,384,128]{2,1,0:T(8,128)(2,1)S(1)}, u32[]{:S(2)}, u32[]{:S(2)}) collective-permute-start(bf16[2,384,128]{2,1,0:T(8,128)(2,1)S(1)} %get-tuple-element.64), channel_id=1, source_target_pairs={{4,0},{5,1},{6,2},{7,3},{0,4},{1,5},{2,6},{3,7},{12,8},{13,9},{14,... | collective-permute-start | bytes 589832 | tf_op jit(solution)/shard_map/ppermute | solution.py:29
  24.6 9.1 %collective-permute-start.6 = (bf16[2,512,128]{2,1,0:T(8,128)(2,1)S(1)}, bf16[2,512,128]{2,1,0:T(8,128)(2,1)S(1)}, u32[]{:S(2)}, u32[]{:S(2)}) collective-permute-start(bf16[2,512,128]{2,1,0:T(8,128)(2,1)S(1)} %get-tuple-element.63.refs_2_), channel_id=1, source_target_pairs={{24,0},{0,8},{8,16},{16,24},{25,1},{1,9},{9,17},{17,25},{26,2},{2,... | collective-permute-start | bytes 786440 | tf_op jit(solution)/shard_map/ppermute | solution.py:29
  33.7 5.7 %collective-permute-start.9 = (bf16[2,384,128]{2,1,0:T(8,128)(2,1)S(1)}, bf16[2,384,128]{2,1,0:T(8,128)(2,1)S(1)}, u32[]{:S(2)}, u32[]{:S(2)}) collective-permute-start(bf16[2,384,128]{2,1,0:T(8,128)(2,1)S(1)} %get-tuple-element.67), channel_id=1, source_target_pairs={{4,0},{5,1},{6,2},{7,3},{0,4},{1,5},{2,6},{3,7},{12,8},{13,9},{14,... | collective-permute-start | bytes 589832 | tf_op jit(solution)/shard_map/ppermute | solution.py:29
  35.1 11.1 %collective-permute-start.8 = (bf16[2,512,128]{2,1,0:T(8,128)(2,1)S(1)}, bf16[2,512,128]{2,1,0:T(8,128)(2,1)S(1)}, u32[]{:S(2)}, u32[]{:S(2)}) collective-permute-start(bf16[2,512,128]{2,1,0:T(8,128)(2,1)S(1)} %get-tuple-element.66.refs_2_), channel_id=1, source_target_pairs={{24,0},{0,8},{8,16},{16,24},{25,1},{1,9},{9,17},{17,25},{26,2},{2,... | collective-permute-start | bytes 786440 | tf_op jit(solution)/shard_map/ppermute | solution.py:29
  46.3 12.1 %collective-permute-start.12 = (bf16[4,384,128]{2,1,0:T(8,128)(2,1)S(1)}, bf16[4,384,128]{2,1,0:T(8,128)(2,1)S(1)}, u32[]{:S(2)}, u32[]{:S(2)}) collective-permute-start(bf16[4,384,128]{2,1,0:T(8,128)(2,1)S(1)} %side_by_side.1), channel_id=1, source_target_pairs={{4,0},{5,1},{6,2},{7,3},{0,4},{1,5},{2,6},{3,7},{12,8},{13,9},{14,... | collective-permute-start | bytes 1179656 | tf_op jit(solution)/shard_map/ppermute | solution.py:29
  51.1 11.5 %collective-permute-start.19 = (bf16[2,384,128]{2,1,0:T(8,128)(2,1)S(1)}, bf16[2,384,128]{2,1,0:T(8,128)(2,1)S(1)}, u32[]{:S(2)}, u32[]{:S(2)}) collective-permute-start(bf16[2,384,128]{2,1,0:T(8,128)(2,1)S(1)} %get-tuple-element.97), channel_id=1, source_target_pairs={{4,0},{5,1},{6,2},{7,3},{0,4},{1,5},{2,6},{3,7},{12,8},{13,9},{14,... | collective-permute-start | bytes 589832 | tf_op jit(solution)/shard_map/ppermute | solution.py:29
  55.3 9.4 %collective-permute-start.13 = (bf16[2,384,128]{2,1,0:T(8,128)(2,1)S(1)}, bf16[2,384,128]{2,1,0:T(8,128)(2,1)S(1)}, u32[]{:S(2)}, u32[]{:S(2)}) collective-permute-start(bf16[2,384,128]{2,1,0:T(8,128)(2,1)S(1)} %get-tuple-element.85), channel_id=1, source_target_pairs={{4,0},{5,1},{6,2},{7,3},{0,4},{1,5},{2,6},{3,7},{12,8},{13,9},{14,... | collective-permute-start | bytes 589832 | tf_op jit(solution)/shard_map/ppermute | solution.py:29
  62.6 8.2 %collective-permute-start.20 = (bf16[2,512,128]{2,1,0:T(8,128)(2,1)S(1)}, bf16[2,512,128]{2,1,0:T(8,128)(2,1)S(1)}, u32[]{:S(2)}, u32[]{:S(2)}) collective-permute-start(bf16[2,512,128]{2,1,0:T(8,128)(2,1)S(1)} %pack_sum.2), channel_id=1, source_target_pairs={{24,0},{0,8},{8,16},{16,24},{25,1},{1,9},{9,17},{17,25},{26,2},{2,... | collective-permute-start | bytes 786440 | tf_op jit(solution)/shard_map/ppermute | solution.py:29
  68.7 11.7 %collective-permute-start.16 = (bf16[128,1280]{1,0:T(8,128)(2,1)S(1)}, bf16[128,1280]{1,0:T(8,128)(2,1)S(1)}, u32[]{:S(2)}, u32[]{:S(2)}) collective-permute-start(bf16[128,1280]{1,0:T(8,128)(2,1)S(1)} %get-tuple-element.84.refs_7_), channel_id=1, source_target_pairs={{0,2},{1,3},{2,0},{3,1},{4,6},{5,7},{6,4},{7,5},{8,10},{9,11},{10,... | collective-permute-start | bytes 983048 | tf_op jit(solution)/shard_map/ppermute | solution.py:33
  70.9 8.2 %collective-permute-start.21 = (bf16[2,512,128]{2,1,0:T(8,128)(2,1)S(1)}, bf16[2,512,128]{2,1,0:T(8,128)(2,1)S(1)}, u32[]{:S(2)}, u32[]{:S(2)}) collective-permute-start(bf16[2,512,128]{2,1,0:T(8,128)(2,1)S(1)} %pack_sum.3), channel_id=1, source_target_pairs={{24,0},{0,8},{8,16},{16,24},{25,1},{1,9},{9,17},{17,25},{26,2},{2,... | collective-permute-start | bytes 786440 | tf_op jit(solution)/shard_map/ppermute | solution.py:29
  71.8 13.4 %collective-permute-start.17 = (bf16[128,1280]{1,0:T(8,128)(2,1)S(1)}, bf16[128,1280]{1,0:T(8,128)(2,1)S(1)}, u32[]{:S(2)}, u32[]{:S(2)}) collective-permute-start(bf16[128,1280]{1,0:T(8,128)(2,1)S(1)} %get-tuple-element.90), channel_id=1, source_target_pairs={{0,3},{1,2},{2,1},{3,0},{4,7},{5,6},{6,5},{7,4},{8,11},{9,10},{10,... | collective-permute-start | bytes 983048 | tf_op jit(solution)/shard_map/ppermute | solution.py:33
  72.4 7.5 %collective-permute-start.14 = (bf16[128,640]{1,0:T(8,128)(2,1)S(1)}, bf16[128,640]{1,0:T(8,128)(2,1)S(1)}, u32[]{:S(2)}, u32[]{:S(2)}) collective-permute-start(bf16[128,640]{1,0:T(8,128)(2,1)S(1)} %get-tuple-element.88), channel_id=1, source_target_pairs={{0,1},{1,0},{2,3},{3,2},{4,5},{5,4},{6,7},{7,6},{8,9},{9,8},{10,11... | collective-permute-start | bytes 491528 | tf_op jit(solution)/shard_map/ppermute | solution.py:33
  73.8 6.2 %collective-permute-start.15 = (bf16[128,640]{1,0:T(8,128)(2,1)S(1)}, bf16[128,640]{1,0:T(8,128)(2,1)S(1)}, u32[]{:S(2)}, u32[]{:S(2)}) collective-permute-start(bf16[128,640]{1,0:T(8,128)(2,1)S(1)} %get-tuple-element.89), channel_id=1, source_target_pairs={{0,1},{1,0},{2,3},{3,2},{4,5},{5,4},{6,7},{7,6},{8,9},{9,8},{10,11... | collective-permute-start | bytes 491528 | tf_op jit(solution)/shard_map/ppermute | solution.py:33
  79.8 6.9 %collective-permute-start.22 = (bf16[2,128,128]{2,1,0:T(8,128)(2,1)S(1)}, bf16[2,128,128]{2,1,0:T(8,128)(2,1)S(1)}, u32[]{:S(2)}, u32[]{:S(2)}) collective-permute-start(bf16[2,128,128]{2,1,0:T(8,128)(2,1)S(1)} %get-tuple-element.98), channel_id=1, source_target_pairs={{0,8},{1,9},{2,10},{3,11},{4,12},{5,13},{6,14},{7,15},{8,16},{9,17... | collective-permute-start | bytes 196616 | tf_op jit(solution)/shard_map/ppermute | solution.py:39
  79.9 6.8 %collective-permute-start.23 = (bf16[2,128,128]{2,1,0:T(8,128)(2,1)S(1)}, bf16[2,128,128]{2,1,0:T(8,128)(2,1)S(1)}, u32[]{:S(2)}, u32[]{:S(2)}) collective-permute-start(bf16[2,128,128]{2,1,0:T(8,128)(2,1)S(1)} %get-tuple-element.99), channel_id=1, source_target_pairs={{0,9},{1,8},{2,11},{3,10},{4,13},{5,12},{6,15},{7,14},{8,17},{9,16... | collective-permute-start | bytes 196616 | tf_op jit(solution)/shard_map/ppermute | solution.py:39
  80.0 9.8 %collective-permute-start.24 = (bf16[2,128,128]{2,1,0:T(8,128)(2,1)S(1)}, bf16[2,128,128]{2,1,0:T(8,128)(2,1)S(1)}, u32[]{:S(2)}, u32[]{:S(2)}) collective-permute-start(bf16[2,128,128]{2,1,0:T(8,128)(2,1)S(1)} %get-tuple-element.100), channel_id=1, source_target_pairs={{0,10},{1,11},{2,8},{3,9},{4,14},{5,15},{6,12},{7,13},{8,18},{9,19... | collective-permute-start | bytes 196616 | tf_op jit(solution)/shard_map/ppermute | solution.py:39
  80.3 9.5 %collective-permute-start.25 = (bf16[2,128,128]{2,1,0:T(8,128)(2,1)S(1)}, bf16[2,128,128]{2,1,0:T(8,128)(2,1)S(1)}, u32[]{:S(2)}, u32[]{:S(2)}) collective-permute-start(bf16[2,128,128]{2,1,0:T(8,128)(2,1)S(1)} %get-tuple-element.101), channel_id=1, source_target_pairs={{0,11},{1,10},{2,9},{3,8},{4,15},{5,14},{6,13},{7,12},{8,19},{9,18... | collective-permute-start | bytes 196616 | tf_op jit(solution)/shard_map/ppermute | solution.py:39
  (9 other events, 22.3 us)

commit v3 on v2

--- a/solution.py
+++ b/solution.py
@@ -136,23 +136,22 @@
     tok = d_own.shape[1] // QUAD
     tail = d_own[:, tok:, :] + back[2 * part:2 * part + 2].astype(F32)
     lead = d_own[:, 0:tok, :]
-    if n_packet:
-        lead += refs[0][:, 0:tok, :].astype(F32)
-        tail += refs[0][:, tok:, :].astype(F32)
+    for packet in refs[:n_packet]:
+        lead += packet[:, 0:tok, :].astype(F32)
+        tail += packet[:, tok:, :].astype(F32)
     return lead, tail
 
 
-def pack_sum(part, n_packet, d_own, back, *refs):
-    lead, tail = total(part, n_packet, d_own, back, refs)
-    out = refs[-1]
+def pack_sum(d_own, back, _, out):
+    lead, tail = total(0, 0, d_own, back, ())
     tok = lead.shape[1]
     out[:, 0:tok, :] = lead.astype(BF16)
     out[:, tok:, :] = tail.astype(BF16)
 
 
-def split_sum(meta, d_own, back, packet, *refs):
+def split_sum(meta, d_own, back, packet_one, packet_two, *refs):
     outs, whole = refs[:QUAD], refs[QUAD]
-    lead, tail = total(0, 1, d_own, back, (packet,))
+    lead, tail = total(0, 2, d_own, back, (packet_one, packet_two))
     tok = lead.shape[1]
     whole[:, 0:tok, :] = lead
     whole[:, tok:, :] = tail
@@ -174,7 +173,8 @@
         out[:, wide + HD:] = part[1]
 
 
-def pack_near(meta, dq, d_own, back, first, second, kept, whole):
+def pack_near(meta, dq, d_own, back, *refs):
+    first, second, kept, whole = refs[-4:]
     lead, tail = total(1, 0, d_own, back, ())
     tok, wide = dq.shape
     half = first.shape[1]
@@ -438,12 +438,9 @@
     def send_back(grads):
         return shifted(grads, "blk", -QUAD)
 
-    def pass_sums(lag, part, back, packet, after):
-        parts = [sums[lag], back, *packet]
-        out = small_call(
-            functools.partial(pack_sum, part, len(packet)), [ring_of], [VMEM] * len(parts) + [ANY], parts + [after]
-        )[0]
-        return out, [shifted(out, "head", 1)]
+    def pass_sums(lag, back, after):
+        out = small_call(pack_sum, [ring_of], [VMEM] * 2 + [ANY], [sums[lag], back, after])[0]
+        return out, shifted(out, "head", n_z - 1 - lag)
 
     call(0, 0)
     pass_keys([accs[0]])
@@ -456,24 +453,24 @@
     back_one = send_back(call(1, 1))
     back_two = send_back(call(1, 2))
     call(1, 3)
-    _, packet = pass_sums(1, 0, back_one, [], accs[1][0])
+    out_one, packet_one = pass_sums(1, back_one, accs[1][0])
     cross = ((tok, wide + 2 * HD), BF16)
     whole = pltpu.VMEM(ring_of[0], F32)
     sent = small_call(
         functools.partial(pack_cross, (2, 3)), [cross] * 2, [SMEM] + [VMEM] * 4,
         [meta, *accs[1], sums[0], back_zero], scratch=[whole], cost=2**20,
     )
-    back_three = send_back(call(0, 3, [accs[1][0], sent[0], back_two]))
-    _, packet = pass_sums(2, 0, back_two, packet, sums[3])
+    out_two, packet_two = pass_sums(2, back_two, out_one)
+    back_three = send_back(call(0, 3, [accs[1][0], sent[0], out_two]))
     near_half = ((tok, (wide + 2 * HD) // 2), BF16)
     near_one, near_two, kept = small_call(
-        pack_near, [near_half] * 2 + [(piece[0], F32)], [SMEM] + [VMEM] * 3,
-        [meta, accs[0][1], sums[0], back_zero], scratch=[whole], cost=2**20,
+        pack_near, [near_half] * 2 + [(piece[0], F32)], [SMEM] + [VMEM] * 3 + [ANY] * 2,
+        [meta, accs[0][1], sums[0], back_zero, packet_one, packet_two], scratch=[whole], cost=2**20,
     )
     near_one, near_two = crossed(near_one, 1), crossed(near_two, 1)
     got = [crossed(part, mask) for mask, part in enumerate(sent, 2)]
     hops = small_call(
-        split_sum, [piece] * QUAD, [SMEM] + [VMEM] * 3, [meta, sums[3], back_three, *packet],
+        split_sum, [piece] * QUAD, [SMEM] + [VMEM] * 4, [meta, sums[3], back_three, packet_one, packet_two],
         scratch=[pltpu.VMEM(ring_of[0], F32)],
     )
     hops = [hopped(hops[mask], mask) for mask in range(QUAD)]

time: 91.4 us -> 98.4 us (1.077)
  waiting for transfers between devices: 24.4 us -> 30 us
  starting transfers between devices: 25.4 us -> 26.8 us
    ppermute x12, waiting for transfers between devices: 21.4 us -> 26.1 us  [shifted(): return lax.ppermute(block, axis, route)]
    ppermute x12, starting transfers between devices: 12.9 us -> 14.5 us  [shifted(): return lax.ppermute(block, axis, route)]
  transfers between devices with their start and end apart: 26 -> 26, of which waited for: 12 -> 12; matrix products, arithmetic and copies ran while one was open for 0% -> 0% of each run, Pallas kernels for 35% -> 33%
where the time goes in v3:
time: 98.4 us; the launch traced here: 98.1 us
  Pallas kernels  34.7 us (35%)
  waiting for transfers between devices  30 us (30%)
  starting transfers between devices  26.8 us (27%)
  local copies, waits for them, and re-layouts  5.58 us (6%)
    pallas_call x8, Pallas kernels, attend_call(): pl.pallas_call(functools.partial(attend, lag, masks, n_blk, n_z, first, l...  27.3 us
    ppermute x12, waiting for transfers between devices, shifted(): return lax.ppermute(block, axis, route)  26.1 us
    ppermute x12, starting transfers between devices, shifted(): return lax.ppermute(block, axis, route)  14.5 us
    pallas_call x11, Pallas kernels, small_call(): pl.pallas_call(body, out_shape=shapes, in_specs=specs, out_specs=[ANY if...  7.36 us
    ppermute x10, starting transfers between devices, crossed(): lax.ppermute(block, 'blk', [(i, i ^ mask) for i in range(lax.axis_size('b...  6.98 us
    unnamed x15, local copies, waits for them, and re-layouts  5.58 us
    ppermute x4, starting transfers between devices, hopped(): return lax.ppermute(block, ('head', 'blk'), route)  5.33 us
    ppermute x4, waiting for transfers between devices, hopped(): return lax.ppermute(block, ('head', 'blk'), route)  3.89 us
  transfers between devices with their start and end apart: 26, of which 12 were waited for; matrix products, arithmetic and copies ran while one was open for 0% of the time, Pallas kernels for 33%

profile of v3, /device:TPU:0, one launch (start us, length us, event | category | flops | bytes accessed | tf_op | source)
XLA Modules:
  0.0 98.1 jit_solution(6917080837133525059)
XLA Ops:
  3.7 2.6 %collective-permute-start.1 = (bf16[2,128,128]{2,1,0:T(8,128)(2,1)S(1)}, bf16[2,128,128]{2,1,0:T(8,128)(2,1)S(1)}, u32[]{:S(2)}, u32[]{:S(2)}) collective-permute-start(bf16[2,128,128]{2,1,0:T(8,128)(2,1)S(1)} %get-tuple-element.58), channel_id=1, source_target_pairs={{0,2},{1,3},{2,0},{3,1},{4,6},{5,7},{6,4},{7,5},{8,10},{9,11},{10,... | collective-permute-start | bytes 196616 | tf_op jit(solution)/shard_map/ppermute | solution.py:33
  12.1 2.0 %collective-permute-start.5 = (bf16[2,384,128]{2,1,0:T(8,128)(2,1)S(1)}, bf16[2,384,128]{2,1,0:T(8,128)(2,1)S(1)}, u32[]{:S(2)}, u32[]{:S(2)}) collective-permute-start(bf16[2,384,128]{2,1,0:T(8,128)(2,1)S(1)} %get-tuple-element.60.refs_1_), channel_id=1, source_target_pairs={{4,0},{5,1},{6,2},{7,3},{0,4},{1,5},{2,6},{3,7},{12,8},{13,9},{14,... | collective-permute-start | bytes 589832 | tf_op jit(solution)/shard_map/ppermute | solution.py:29
  14.1 1.6 %collective-permute-start.4 = (bf16[2,512,128]{2,1,0:T(8,128)(2,1)S(1)}, bf16[2,512,128]{2,1,0:T(8,128)(2,1)S(1)}, u32[]{:S(2)}, u32[]{:S(2)}) collective-permute-start(bf16[2,512,128]{2,1,0:T(8,128)(2,1)S(1)} %get-tuple-element.61.refs_2_), channel_id=1, source_target_pairs={{24,0},{0,8},{8,16},{16,24},{25,1},{1,9},{9,17},{17,25},{26,2},{2,... | collective-permute-start | bytes 786440 | tf_op jit(solution)/shard_map/ppermute | solution.py:29
  17.2 2.2 %collective-permute-done.5.refs_3_ = bf16[2,384,128]{2,1,0:T(8,128)(2,1)S(1)} collective-permute-done((bf16[2,384,128]{2,1,0:T(8,128)(2,1)S(1)}, bf16[2,384,128]{2,1,0:T(8,128)(2,1)S(1)}, u32[]{:S(2)}, u32[]{:S(2)}) %collective-permute-start.5) | collective-permute-done | bytes 196640 | tf_op jit(solution)/shard_map/ppermute | solution.py:29
  19.3 3.3 %attend.8 = (f32[2,128,1024]{2,1,0:T(8,128)S(1)}, f32[2,896,128]{2,1,0:T(8,128)S(1)}) custom-call(s32[2]{0:T(128)S(1)} %pad_add_fusion.meta, s32[16]{0:T(128)S(1)} %copy-done.5, bf16[272,1024]{1,0:T(8,128)(2,1)S(1)} %get-tuple-element.55.refs_0_, bf16[272,1024]{1,0:T(8,128)(2,1)S(1)} %collective-permute-done.3.refs_1_, ...), custom_call_target="tpu_custom_call" | custom-call | flops 805306368 | bytes 1048576 | tf_op jit(solution)/shard_map/attend/pallas_call | solution.py:369
  26.1 4.0 %collective-permute-done.7.refs_3_ = bf16[2,384,128]{2,1,0:T(8,128)(2,1)S(1)} collective-permute-done((bf16[2,384,128]{2,1,0:T(8,128)(2,1)S(1)}, bf16[2,384,128]{2,1,0:T(8,128)(2,1)S(1)}, u32[]{:S(2)}, u32[]{:S(2)}) %collective-permute-start.7) | collective-permute-done | bytes 196640 | tf_op jit(solution)/shard_map/ppermute | solution.py:29
  30.0 3.4 %attend.9 = (f32[2,128,1024]{2,1,0:T(8,128)S(1)}, f32[2,896,128]{2,1,0:T(8,128)S(1)}) custom-call(s32[2]{0:T(128)S(1)} %pad_add_fusion.meta, s32[16]{0:T(128)S(1)} %copy-done.5, bf16[272,1024]{1,0:T(8,128)(2,1)S(1)} %get-tuple-element.55.refs_0_, bf16[272,1024]{1,0:T(8,128)(2,1)S(1)} %collective-permute-done.3.refs_1_, ...), custom_call_target="tpu_custom_call", output_to_operand_aliasing={{0}: (6, {})} | custom-call | flops 805306368 | bytes 1048576 | tf_op jit(solution)/shard_map/attend/pallas_call | solution.py:369
  35.7 3.7 %collective-permute-done.9.refs_3_ = bf16[2,384,128]{2,1,0:T(8,128)(2,1)S(1)} collective-permute-done((bf16[2,384,128]{2,1,0:T(8,128)(2,1)S(1)}, bf16[2,384,128]{2,1,0:T(8,128)(2,1)S(1)}, u32[]{:S(2)}, u32[]{:S(2)}) %collective-permute-start.9) | collective-permute-done | bytes 196640 | tf_op jit(solution)/shard_map/ppermute | solution.py:29
  39.5 3.4 %attend.10 = (f32[2,128,1024]{2,1,0:T(8,128)S(1)}, f32[2,896,128]{2,1,0:T(8,128)S(1)}) custom-call(s32[2]{0:T(128)S(1)} %pad_add_fusion.meta, s32[16]{0:T(128)S(1)} %copy-done.5, bf16[272,1024]{1,0:T(8,128)(2,1)S(1)} %get-tuple-element.55.refs_0_, bf16[272,1024]{1,0:T(8,128)(2,1)S(1)} %collective-permute-done.3.refs_1_, ...), custom_call_target="tpu_custom_call", output_to_operand_aliasing={{0}: (6, {})} | custom-call | flops 805306368 | bytes 1048576 | tf_op jit(solution)/shard_map/attend/pallas_call | solution.py:369
  42.9 3.3 %attend.11 = (f32[2,128,1024]{2,1,0:T(8,128)S(1)}, f32[2,512,128]{2,1,0:T(8,128)S(1)}, bf16[2,384,128]{2,1,0:T(8,128)(2,1)S(1)}) custom-call(s32[2]{0:T(128)S(1)} %pad_add_fusion.meta, s32[16]{0:T(128)S(1)} %copy-done.5, bf16[272,1024]{1,0:T(8,128)(2,1)S(1)} %collective-permute-done.10.refs_0_, bf16[272,1024]{1,0:T(8,128)(2,1)S(1)} %collective-permute-done.11.refs_1_, ...), custom_call_target="tpu_custom_call" | custom-call | flops 805306368 | bytes 1048576 | tf_op jit(solution)/shard_map/attend/pallas_call | solution.py:369
  47.6 3.5 %attend.12 = (f32[2,128,1024]{2,1,0:T(8,128)S(1)}, f32[2,512,128]{2,1,0:T(8,128)S(1)}, bf16[2,384,128]{2,1,0:T(8,128)(2,1)S(1)}) custom-call(s32[2]{0:T(128)S(1)} %pad_add_fusion.meta, s32[16]{0:T(128)S(1)} %copy-done.5, bf16[272,1024]{1,0:T(8,128)(2,1)S(1)} %collective-permute-done.10.refs_0_, ...), custom_call_target="tpu_custom_call", output_to_operand_aliasing={{0}: (6, {})} | custom-call | flops 805306368 | bytes 1048576 | tf_op jit(solution)/shard_map/attend/pallas_call | solution.py:369
  51.9 3.5 %attend.13 = (f32[2,128,1024]{2,1,0:T(8,128)S(1)}, f32[2,512,128]{2,1,0:T(8,128)S(1)}, bf16[2,384,128]{2,1,0:T(8,128)(2,1)S(1)}) custom-call(s32[2]{0:T(128)S(1)} %pad_add_fusion.meta, s32[16]{0:T(128)S(1)} %copy-done.5, bf16[272,1024]{1,0:T(8,128)(2,1)S(1)} %collective-permute-done.10.refs_0_, ...), custom_call_target="tpu_custom_call", output_to_operand_aliasing={{0}: (6, {})} | custom-call | flops 805306368 | bytes 1048576 | tf_op jit(solution)/shard_map/attend/pallas_call | solution.py:369
  56.7 1.7 %collective-permute-done.12.refs_3_.back = bf16[4,384,128]{2,1,0:T(8,128)(2,1)S(1)} collective-permute-done((bf16[4,384,128]{2,1,0:T(8,128)(2,1)S(1)}, bf16[4,384,128]{2,1,0:T(8,128)(2,1)S(1)}, u32[]{:S(2)}, u32[]{:S(2)}) %collective-permute-start.12) | collective-permute-done | bytes 393248 | tf_op jit(solution)/shard_map/ppermute | solution.py:29
  58.4 3.6 %attend.14 = (bf16[128,1024]{1,0:T(8,128)(2,1)S(1)}, bf16[128,1024]{1,0:T(8,128)(2,1)S(1)}, f32[2,896,128]{2,1,0:T(8,128)S(1)}) custom-call(s32[2]{0:T(128)S(1)} %pad_add_fusion.meta, s32[16]{0:T(128)S(1)} %copy-done.5, bf16[272,1024]{1,0:T(8,128)(2,1)S(1)} %collective-permute-done.10.refs_0_, bf16[272,1024]{1,0:T(8,128)(2,1)S(1)} %collective-permute-done.11.refs_1_, ...), custom_call_target="tpu_custom_call" | custom-call | flops 805306368 | bytes 1048576 | tf_op jit(solution)/shard_map/attend/pallas_call | solution.py:369
  62.6 2.1 %collective-permute-done.13.back = bf16[2,384,128]{2,1,0:T(8,128)(2,1)S(1)} collective-permute-done((bf16[2,384,128]{2,1,0:T(8,128)(2,1)S(1)}, bf16[2,384,128]{2,1,0:T(8,128)(2,1)S(1)}, u32[]{:S(2)}, u32[]{:S(2)}) %collective-permute-start.13) | collective-permute-done | bytes 196640 | tf_op jit(solution)/shard_map/ppermute | solution.py:29
  66.1 1.6 %collective-permute-start.15 = (bf16[2,512,128]{2,1,0:T(8,128)(2,1)S(1)}, bf16[2,512,128]{2,1,0:T(8,128)(2,1)S(1)}, u32[]{:S(2)}, u32[]{:S(2)}) collective-permute-start(bf16[2,512,128]{2,1,0:T(8,128)(2,1)S(1)} %pack_sum.2._), channel_id=1, source_target_pairs={{16,0},{24,8},{0,16},{8,24},{17,1},{25,9},{1,17},{9,25},{18,2},{26... | collective-permute-start | bytes 786440 | tf_op jit(solution)/shard_map/ppermute | solution.py:29
  68.3 1.6 %collective-permute-start.19 = (bf16[128,1280]{1,0:T(8,128)(2,1)S(1)}, bf16[128,1280]{1,0:T(8,128)(2,1)S(1)}, u32[]{:S(2)}, u32[]{:S(2)}) collective-permute-start(bf16[128,1280]{1,0:T(8,128)(2,1)S(1)} %get-tuple-element.84.refs_7_), channel_id=1, source_target_pairs={{0,2},{1,3},{2,0},{3,1},{4,6},{5,7},{6,4},{7,5},{8,10},{9,11},{10,... | collective-permute-start | bytes 983048 | tf_op jit(solution)/shard_map/ppermute | solution.py:33
  69.9 3.4 %attend.15 = (bf16[128,1024]{1,0:T(8,128)(2,1)S(1)}, bf16[128,1024]{1,0:T(8,128)(2,1)S(1)}, f32[2,512,128]{2,1,0:T(8,128)S(1)}, bf16[2,384,128]{2,1,0:T(8,128)(2,1)S(1)}) custom-call(s32[2]{0:T(128)S(1)} %pad_add_fusion.meta, s32[16]{0:T(128)S(1)} %copy-done.5, bf16[272,1024]{1,0:T(8,128)(2,1)S(1)} %get-tuple-element.55.refs_0_, ...), custom_call_target="tpu_custom_call" | custom-call | flops 805306368 | bytes 1048576 | tf_op jit(solution)/shard_map/attend/pallas_call | solution.py:369
  73.8 1.9 %collective-permute-done.16.refs_1_.packet_two = bf16[2,512,128]{2,1,0:T(8,128)(2,1)S(1)} collective-permute-done((bf16[2,512,128]{2,1,0:T(8,128)(2,1)S(1)}, bf16[2,512,128]{2,1,0:T(8,128)(2,1)S(1)}, u32[]{:S(2)}, u32[]{:S(2)}) %collective-permute-start.16) | collective-permute-done | bytes 262176 | tf_op jit(solution)/shard_map/ppermute | solution.py:29
  75.7 8.3 %collective-permute-done.15.refs_0_.packet_one = bf16[2,512,128]{2,1,0:T(8,128)(2,1)S(1)} collective-permute-done((bf16[2,512,128]{2,1,0:T(8,128)(2,1)S(1)}, bf16[2,512,128]{2,1,0:T(8,128)(2,1)S(1)}, u32[]{:S(2)}, u32[]{:S(2)}) %collective-permute-start.15) | collective-permute-done | bytes 262176 | tf_op jit(solution)/shard_map/ppermute | solution.py:29
  86.2 3.6 %collective-permute-start.24 = (bf16[2,128,128]{2,1,0:T(8,128)(2,1)S(1)}, bf16[2,128,128]{2,1,0:T(8,128)(2,1)S(1)}, u32[]{:S(2)}, u32[]{:S(2)}) collective-permute-start(bf16[2,128,128]{2,1,0:T(8,128)(2,1)S(1)} %get-tuple-element.100), channel_id=1, source_target_pairs={{0,10},{1,11},{2,8},{3,9},{4,14},{5,15},{6,12},{7,13},{8,18},{9,19... | collective-permute-start | bytes 196616 | tf_op jit(solution)/shard_map/ppermute | solution.py:39
  89.8 1.6 %collective-permute-start.25 = (bf16[2,128,128]{2,1,0:T(8,128)(2,1)S(1)}, bf16[2,128,128]{2,1,0:T(8,128)(2,1)S(1)}, u32[]{:S(2)}, u32[]{:S(2)}) collective-permute-start(bf16[2,128,128]{2,1,0:T(8,128)(2,1)S(1)} %get-tuple-element.101), channel_id=1, source_target_pairs={{0,11},{1,10},{2,9},{3,8},{4,15},{5,14},{6,13},{7,12},{8,19},{9,18... | collective-permute-start | bytes 196616 | tf_op jit(solution)/shard_map/ppermute | solution.py:39
  91.4 1.5 %place_heads.1 = (bf16[1,128,4096]{2,1,0:T(8,128)(2,1)}, f32[8,128]{1,0:T(8,128)S(1)}) custom-call(s32[2]{0:T(128)S(1)} %pad_add_fusion.meta, bf16[128,1024]{1,0:T(8,128)(2,1)S(1)} %get-tuple-element.89.dq_own, bf16[128,640]{1,0:T(8,128)(2,1)S(1)} %collective-permute-done.17.near_one, bf16[128,640]{1,0:T(8,128)(2,1)S(1)} %collective-permute-done.18.near_two, ...), custom_call_target="tpu_custom_call" | custom-call | tf_op jit(solution)/shard_map/place_heads/pallas_call | solution.py:222
  92.9 3.0 %collective-permute-done.24.hop2 = bf16[2,128,128]{2,1,0:T(8,128)(2,1)S(1)} collective-permute-done((bf16[2,128,128]{2,1,0:T(8,128)(2,1)S(1)}, bf16[2,128,128]{2,1,0:T(8,128)(2,1)S(1)}, u32[]{:S(2)}, u32[]{:S(2)}) %collective-permute-start.24) | collective-permute-done | bytes 65568 | tf_op jit(solution)/shard_map/ppermute | solution.py:39
  (69 shorter events, 27.0 us)
Async XLA Ops:
  3.1 8.2 %collective-permute-start = (bf16[2,128,128]{2,1,0:T(8,128)(2,1)S(1)}, bf16[2,128,128]{2,1,0:T(8,128)(2,1)S(1)}, u32[]{:S(2)}, u32[]{:S(2)}) collective-permute-start(bf16[2,128,128]{2,1,0:T(8,128)(2,1)S(1)} %get-tuple-element.57), channel_id=1, source_target_pairs={{0,1},{1,0},{2,3},{3,2},{4,5},{5,4},{6,7},{7,6},{8,9},{9,8},{10,11... | collective-permute-start | bytes 196616 | tf_op jit(solution)/shard_map/ppermute | solution.py:33
  3.7 7.7 %collective-permute-start.1 = (bf16[2,128,128]{2,1,0:T(8,128)(2,1)S(1)}, bf16[2,128,128]{2,1,0:T(8,128)(2,1)S(1)}, u32[]{:S(2)}, u32[]{:S(2)}) collective-permute-start(bf16[2,128,128]{2,1,0:T(8,128)(2,1)S(1)} %get-tuple-element.58), channel_id=1, source_target_pairs={{0,2},{1,3},{2,0},{3,1},{4,6},{5,7},{6,4},{7,5},{8,10},{9,11},{10,... | collective-permute-start | bytes 196616 | tf_op jit(solution)/shard_map/ppermute | solution.py:33
  11.9 7.4 %collective-permute-start.3 = (bf16[272,1024]{1,0:T(8,128)(2,1)S(1)}, bf16[272,1024]{1,0:T(8,128)(2,1)S(1)}, u32[]{:S(2)}, u32[]{:S(2)}) collective-permute-start(bf16[272,1024]{1,0:T(8,128)(2,1)S(1)} %later.3), channel_id=1, source_target_pairs={{0,1},{1,0},{2,3},{3,2},{4,5},{5,4},{6,7},{7,6},{8,9},{9,8},{10,11... | collective-permute-start | bytes 1671176 | tf_op jit(solution)/shard_map/ppermute | solution.py:33
  12.1 7.2 %collective-permute-start.5 = (bf16[2,384,128]{2,1,0:T(8,128)(2,1)S(1)}, bf16[2,384,128]{2,1,0:T(8,128)(2,1)S(1)}, u32[]{:S(2)}, u32[]{:S(2)}) collective-permute-start(bf16[2,384,128]{2,1,0:T(8,128)(2,1)S(1)} %get-tuple-element.60.refs_1_), channel_id=1, source_target_pairs={{4,0},{5,1},{6,2},{7,3},{0,4},{1,5},{2,6},{3,7},{12,8},{13,9},{14,... | collective-permute-start | bytes 589832 | tf_op jit(solution)/shard_map/ppermute | solution.py:29
  14.1 10.0 %collective-permute-start.4 = (bf16[2,512,128]{2,1,0:T(8,128)(2,1)S(1)}, bf16[2,512,128]{2,1,0:T(8,128)(2,1)S(1)}, u32[]{:S(2)}, u32[]{:S(2)}) collective-permute-start(bf16[2,512,128]{2,1,0:T(8,128)(2,1)S(1)} %get-tuple-element.61.refs_2_), channel_id=1, source_target_pairs={{24,0},{0,8},{8,16},{16,24},{25,1},{1,9},{9,17},{17,25},{26,2},{2,... | collective-permute-start | bytes 786440 | tf_op jit(solution)/shard_map/ppermute | solution.py:29
  15.7 27.2 %collective-permute-start.10 = (bf16[272,1024]{1,0:T(8,128)(2,1)S(1)}, bf16[272,1024]{1,0:T(8,128)(2,1)S(1)}, u32[]{:S(2)}, u32[]{:S(2)}) collective-permute-start(bf16[272,1024]{1,0:T(8,128)(2,1)S(1)} %later.4), channel_id=1, source_target_pairs={{0,2},{1,3},{2,0},{3,1},{4,6},{5,7},{6,4},{7,5},{8,10},{9,11},{10,... | collective-permute-start | bytes 1671176 | tf_op jit(solution)/shard_map/ppermute | solution.py:33
  17.2 25.7 %collective-permute-start.11 = (bf16[272,1024]{1,0:T(8,128)(2,1)S(1)}, bf16[272,1024]{1,0:T(8,128)(2,1)S(1)}, u32[]{:S(2)}, u32[]{:S(2)}) collective-permute-start(bf16[272,1024]{1,0:T(8,128)(2,1)S(1)} %later.5), channel_id=1, source_target_pairs={{0,3},{1,2},{2,1},{3,0},{4,7},{5,6},{6,5},{7,4},{8,11},{9,10},{10,... | collective-permute-start | bytes 1671176 | tf_op jit(solution)/shard_map/ppermute | solution.py:33
  24.1 6.0 %collective-permute-start.7 = (bf16[2,384,128]{2,1,0:T(8,128)(2,1)S(1)}, bf16[2,384,128]{2,1,0:T(8,128)(2,1)S(1)}, u32[]{:S(2)}, u32[]{:S(2)}) collective-permute-start(bf16[2,384,128]{2,1,0:T(8,128)(2,1)S(1)} %get-tuple-element.64), channel_id=1, source_target_pairs={{4,0},{5,1},{6,2},{7,3},{0,4},{1,5},{2,6},{3,7},{12,8},{13,9},{14,... | collective-permute-start | bytes 589832 | tf_op jit(solution)/shard_map/ppermute | solution.py:29
  24.6 9.1 %collective-permute-start.6 = (bf16[2,512,128]{2,1,0:T(8,128)(2,1)S(1)}, bf16[2,512,128]{2,1,0:T(8,128)(2,1)S(1)}, u32[]{:S(2)}, u32[]{:S(2)}) collective-permute-start(bf16[2,512,128]{2,1,0:T(8,128)(2,1)S(1)} %get-tuple-element.63.refs_2_), channel_id=1, source_target_pairs={{24,0},{0,8},{8,16},{16,24},{25,1},{1,9},{9,17},{17,25},{26,2},{2,... | collective-permute-start | bytes 786440 | tf_op jit(solution)/shard_map/ppermute | solution.py:29
  33.7 5.7 %collective-permute-start.9 = (bf16[2,384,128]{2,1,0:T(8,128)(2,1)S(1)}, bf16[2,384,128]{2,1,0:T(8,128)(2,1)S(1)}, u32[]{:S(2)}, u32[]{:S(2)}) collective-permute-start(bf16[2,384,128]{2,1,0:T(8,128)(2,1)S(1)} %get-tuple-element.67), channel_id=1, source_target_pairs={{4,0},{5,1},{6,2},{7,3},{0,4},{1,5},{2,6},{3,7},{12,8},{13,9},{14,... | collective-permute-start | bytes 589832 | tf_op jit(solution)/shard_map/ppermute | solution.py:29
  35.1 11.1 %collective-permute-start.8 = (bf16[2,512,128]{2,1,0:T(8,128)(2,1)S(1)}, bf16[2,512,128]{2,1,0:T(8,128)(2,1)S(1)}, u32[]{:S(2)}, u32[]{:S(2)}) collective-permute-start(bf16[2,512,128]{2,1,0:T(8,128)(2,1)S(1)} %get-tuple-element.66.refs_2_), channel_id=1, source_target_pairs={{24,0},{0,8},{8,16},{16,24},{25,1},{1,9},{9,17},{17,25},{26,2},{2,... | collective-permute-start | bytes 786440 | tf_op jit(solution)/shard_map/ppermute | solution.py:29
  46.3 12.1 %collective-permute-start.12 = (bf16[4,384,128]{2,1,0:T(8,128)(2,1)S(1)}, bf16[4,384,128]{2,1,0:T(8,128)(2,1)S(1)}, u32[]{:S(2)}, u32[]{:S(2)}) collective-permute-start(bf16[4,384,128]{2,1,0:T(8,128)(2,1)S(1)} %side_by_side.1), channel_id=1, source_target_pairs={{4,0},{5,1},{6,2},{7,3},{0,4},{1,5},{2,6},{3,7},{12,8},{13,9},{14,... | collective-permute-start | bytes 1179656 | tf_op jit(solution)/shard_map/ppermute | solution.py:29
  51.1 11.5 %collective-permute-start.14 = (bf16[2,384,128]{2,1,0:T(8,128)(2,1)S(1)}, bf16[2,384,128]{2,1,0:T(8,128)(2,1)S(1)}, u32[]{:S(2)}, u32[]{:S(2)}) collective-permute-start(bf16[2,384,128]{2,1,0:T(8,128)(2,1)S(1)} %get-tuple-element.88), channel_id=1, source_target_pairs={{4,0},{5,1},{6,2},{7,3},{0,4},{1,5},{2,6},{3,7},{12,8},{13,9},{14,... | collective-permute-start | bytes 589832 | tf_op jit(solution)/shard_map/ppermute | solution.py:29
  55.3 9.4 %collective-permute-start.13 = (bf16[2,384,128]{2,1,0:T(8,128)(2,1)S(1)}, bf16[2,384,128]{2,1,0:T(8,128)(2,1)S(1)}, u32[]{:S(2)}, u32[]{:S(2)}) collective-permute-start(bf16[2,384,128]{2,1,0:T(8,128)(2,1)S(1)} %get-tuple-element.86), channel_id=1, source_target_pairs={{4,0},{5,1},{6,2},{7,3},{0,4},{1,5},{2,6},{3,7},{12,8},{13,9},{14,... | collective-permute-start | bytes 589832 | tf_op jit(solution)/shard_map/ppermute | solution.py:29
  64.8 11.0 %collective-permute-start.16 = (bf16[2,512,128]{2,1,0:T(8,128)(2,1)S(1)}, bf16[2,512,128]{2,1,0:T(8,128)(2,1)S(1)}, u32[]{:S(2)}, u32[]{:S(2)}) collective-permute-start(bf16[2,512,128]{2,1,0:T(8,128)(2,1)S(1)} %pack_sum.3.refs_8_), channel_id=1, source_target_pairs={{24,0},{0,8},{8,16},{16,24},{25,1},{1,9},{9,17},{17,25},{26,2},{2,... | collective-permute-start | bytes 786440 | tf_op jit(solution)/shard_map/ppermute | solution.py:29
  66.1 18.0 %collective-permute-start.15 = (bf16[2,512,128]{2,1,0:T(8,128)(2,1)S(1)}, bf16[2,512,128]{2,1,0:T(8,128)(2,1)S(1)}, u32[]{:S(2)}, u32[]{:S(2)}) collective-permute-start(bf16[2,512,128]{2,1,0:T(8,128)(2,1)S(1)} %pack_sum.2._), channel_id=1, source_target_pairs={{16,0},{24,8},{0,16},{8,24},{17,1},{25,9},{1,17},{9,25},{18,2},{26... | collective-permute-start | bytes 786440 | tf_op jit(solution)/shard_map/ppermute | solution.py:29
  68.3 17.7 %collective-permute-start.19 = (bf16[128,1280]{1,0:T(8,128)(2,1)S(1)}, bf16[128,1280]{1,0:T(8,128)(2,1)S(1)}, u32[]{:S(2)}, u32[]{:S(2)}) collective-permute-start(bf16[128,1280]{1,0:T(8,128)(2,1)S(1)} %get-tuple-element.84.refs_7_), channel_id=1, source_target_pairs={{0,2},{1,3},{2,0},{3,1},{4,6},{5,7},{6,4},{7,5},{8,10},{9,11},{10,... | collective-permute-start | bytes 983048 | tf_op jit(solution)/shard_map/ppermute | solution.py:33
  69.9 16.3 %collective-permute-start.20 = (bf16[128,1280]{1,0:T(8,128)(2,1)S(1)}, bf16[128,1280]{1,0:T(8,128)(2,1)S(1)}, u32[]{:S(2)}, u32[]{:S(2)}) collective-permute-start(bf16[128,1280]{1,0:T(8,128)(2,1)S(1)} %get-tuple-element.93), channel_id=1, source_target_pairs={{0,3},{1,2},{2,1},{3,0},{4,7},{5,6},{6,5},{7,4},{8,11},{9,10},{10,... | collective-permute-start | bytes 983048 | tf_op jit(solution)/shard_map/ppermute | solution.py:33
  73.3 12.0 %collective-permute-start.21 = (bf16[2,384,128]{2,1,0:T(8,128)(2,1)S(1)}, bf16[2,384,128]{2,1,0:T(8,128)(2,1)S(1)}, u32[]{:S(2)}, u32[]{:S(2)}) collective-permute-start(bf16[2,384,128]{2,1,0:T(8,128)(2,1)S(1)} %get-tuple-element.97), channel_id=1, source_target_pairs={{4,0},{5,1},{6,2},{7,3},{0,4},{1,5},{2,6},{3,7},{12,8},{13,9},{14,... | collective-permute-start | bytes 589832 | tf_op jit(solution)/shard_map/ppermute | solution.py:29
  84.8 6.6 %collective-permute-start.18 = (bf16[128,640]{1,0:T(8,128)(2,1)S(1)}, bf16[128,640]{1,0:T(8,128)(2,1)S(1)}, u32[]{:S(2)}, u32[]{:S(2)}) collective-permute-start(bf16[128,640]{1,0:T(8,128)(2,1)S(1)} %get-tuple-element.92), channel_id=1, source_target_pairs={{0,1},{1,0},{2,3},{3,2},{4,5},{5,4},{6,7},{7,6},{8,9},{9,8},{10,11... | collective-permute-start | bytes 491528 | tf_op jit(solution)/shard_map/ppermute | solution.py:33
  86.0 6.9 %collective-permute-start.22 = (bf16[2,128,128]{2,1,0:T(8,128)(2,1)S(1)}, bf16[2,128,128]{2,1,0:T(8,128)(2,1)S(1)}, u32[]{:S(2)}, u32[]{:S(2)}) collective-permute-start(bf16[2,128,128]{2,1,0:T(8,128)(2,1)S(1)} %get-tuple-element.98), channel_id=1, source_target_pairs={{0,8},{1,9},{2,10},{3,11},{4,12},{5,13},{6,14},{7,15},{8,16},{9,17... | collective-permute-start | bytes 196616 | tf_op jit(solution)/shard_map/ppermute | solution.py:39
  86.1 6.9 %collective-permute-start.23 = (bf16[2,128,128]{2,1,0:T(8,128)(2,1)S(1)}, bf16[2,128,128]{2,1,0:T(8,128)(2,1)S(1)}, u32[]{:S(2)}, u32[]{:S(2)}) collective-permute-start(bf16[2,128,128]{2,1,0:T(8,128)(2,1)S(1)} %get-tuple-element.99), channel_id=1, source_target_pairs={{0,9},{1,8},{2,11},{3,10},{4,13},{5,12},{6,15},{7,14},{8,17},{9,16... | collective-permute-start | bytes 196616 | tf_op jit(solution)/shard_map/ppermute | solution.py:39
  86.2 9.8 %collective-permute-start.24 = (bf16[2,128,128]{2,1,0:T(8,128)(2,1)S(1)}, bf16[2,128,128]{2,1,0:T(8,128)(2,1)S(1)}, u32[]{:S(2)}, u32[]{:S(2)}) collective-permute-start(bf16[2,128,128]{2,1,0:T(8,128)(2,1)S(1)} %get-tuple-element.100), channel_id=1, source_target_pairs={{0,10},{1,11},{2,8},{3,9},{4,14},{5,15},{6,12},{7,13},{8,18},{9,19... | collective-permute-start | bytes 196616 | tf_op jit(solution)/shard_map/ppermute | solution.py:39
  89.8 7.0 %collective-permute-start.25 = (bf16[2,128,128]{2,1,0:T(8,128)(2,1)S(1)}, bf16[2,128,128]{2,1,0:T(8,128)(2,1)S(1)}, u32[]{:S(2)}, u32[]{:S(2)}) collective-permute-start(bf16[2,128,128]{2,1,0:T(8,128)(2,1)S(1)} %get-tuple-element.101), channel_id=1, source_target_pairs={{0,11},{1,10},{2,9},{3,8},{4,15},{5,14},{6,13},{7,12},{8,19},{9,18... | collective-permute-start | bytes 196616 | tf_op jit(solution)/shard_map/ppermute | solution.py:39
  (9 other events, 21.6 us)

commit v4 on v2

--- a/solution.py
+++ b/solution.py
@@ -463,7 +463,7 @@
         functools.partial(pack_cross, (2, 3)), [cross] * 2, [SMEM] + [VMEM] * 4,
         [meta, *accs[1], sums[0], back_zero], scratch=[whole], cost=2**20,
     )
-    back_three = send_back(call(0, 3, [accs[1][0], sent[0], back_two]))
+    back_three = send_back(call(0, 3, [accs[1][0], sent[0]]))
     _, packet = pass_sums(2, 0, back_two, packet, sums[3])
     near_half = ((tok, (wide + 2 * HD) // 2), BF16)
     near_one, near_two, kept = small_call(

time: 91.4 us -> 90.9 us (level)
  waiting for transfers between devices: 24.4 us -> 23.2 us
    ppermute x12, waiting for transfers between devices: 21.4 us -> 20.1 us  [shifted(): return lax.ppermute(block, axis, route)]
  transfers between devices with their start and end apart: 26 -> 26, of which waited for: 12 -> 10; matrix products, arithmetic and copies ran while one was open for 0% -> 0% of each run, Pallas kernels for 35% -> 36%
where the time goes in v4:
time: 90.9 us; the launch traced here: 90.5 us
  Pallas kernels  34.7 us (38%)
  starting transfers between devices  26 us (29%)
  waiting for transfers between devices  23.2 us (26%)
  local copies, waits for them, and re-layouts  5.58 us (6%)
  between operations  0.92 us (1%)
    pallas_call x8, Pallas kernels, attend_call(): pl.pallas_call(functools.partial(attend, lag, masks, n_blk, n_z, first, l...  27.3 us
    ppermute x12, waiting for transfers between devices, shifted(): return lax.ppermute(block, axis, route)  20.1 us
    ppermute x12, starting transfers between devices, shifted(): return lax.ppermute(block, axis, route)  13.7 us
    pallas_call x11, Pallas kernels, small_call(): pl.pallas_call(body, out_shape=shapes, in_specs=specs, out_specs=[ANY if...  7.37 us
    ppermute x10, starting transfers between devices, crossed(): lax.ppermute(block, 'blk', [(i, i ^ mask) for i in range(lax.axis_size('b...  7.07 us
    unnamed x15, local copies, waits for them, and re-layouts  5.58 us
    ppermute x4, starting transfers between devices, hopped(): return lax.ppermute(block, ('head', 'blk'), route)  5.31 us
    ppermute x4, waiting for transfers between devices, hopped(): return lax.ppermute(block, ('head', 'blk'), route)  3.02 us
  transfers between devices with their start and end apart: 26, of which 10 were waited for; matrix products, arithmetic and copies ran while one was open for 0% of the time, Pallas kernels for 36%

profile of v4, /device:TPU:0, one launch (start us, length us, event | category | flops | bytes accessed | tf_op | source)
XLA Modules:
  0.0 90.5 jit_solution(9025545129594969417)
XLA Ops:
  3.7 2.6 %collective-permute-start.1 = (bf16[2,128,128]{2,1,0:T(8,128)(2,1)S(1)}, bf16[2,128,128]{2,1,0:T(8,128)(2,1)S(1)}, u32[]{:S(2)}, u32[]{:S(2)}) collective-permute-start(bf16[2,128,128]{2,1,0:T(8,128)(2,1)S(1)} %get-tuple-element.58), channel_id=1, source_target_pairs={{0,2},{1,3},{2,0},{3,1},{4,6},{5,7},{6,4},{7,5},{8,10},{9,11},{10,... | collective-permute-start | bytes 196616 | tf_op jit(solution)/shard_map/ppermute | solution.py:33
  12.1 2.0 %collective-permute-start.5 = (bf16[2,384,128]{2,1,0:T(8,128)(2,1)S(1)}, bf16[2,384,128]{2,1,0:T(8,128)(2,1)S(1)}, u32[]{:S(2)}, u32[]{:S(2)}) collective-permute-start(bf16[2,384,128]{2,1,0:T(8,128)(2,1)S(1)} %get-tuple-element.60.refs_1_), channel_id=1, source_target_pairs={{4,0},{5,1},{6,2},{7,3},{0,4},{1,5},{2,6},{3,7},{12,8},{13,9},{14,... | collective-permute-start | bytes 589832 | tf_op jit(solution)/shard_map/ppermute | solution.py:29
  14.1 1.6 %collective-permute-start.4 = (bf16[2,512,128]{2,1,0:T(8,128)(2,1)S(1)}, bf16[2,512,128]{2,1,0:T(8,128)(2,1)S(1)}, u32[]{:S(2)}, u32[]{:S(2)}) collective-permute-start(bf16[2,512,128]{2,1,0:T(8,128)(2,1)S(1)} %get-tuple-element.61.refs_2_), channel_id=1, source_target_pairs={{24,0},{0,8},{8,16},{16,24},{25,1},{1,9},{9,17},{17,25},{26,2},{2,... | collective-permute-start | bytes 786440 | tf_op jit(solution)/shard_map/ppermute | solution.py:29
  15.7 1.5 %collective-permute-start.10 = (bf16[272,1024]{1,0:T(8,128)(2,1)S(1)}, bf16[272,1024]{1,0:T(8,128)(2,1)S(1)}, u32[]{:S(2)}, u32[]{:S(2)}) collective-permute-start(bf16[272,1024]{1,0:T(8,128)(2,1)S(1)} %later.4), channel_id=1, source_target_pairs={{0,2},{1,3},{2,0},{3,1},{4,6},{5,7},{6,4},{7,5},{8,10},{9,11},{10,... | collective-permute-start | bytes 1671176 | tf_op jit(solution)/shard_map/ppermute | solution.py:33
  17.2 2.2 %collective-permute-done.5.refs_3_ = bf16[2,384,128]{2,1,0:T(8,128)(2,1)S(1)} collective-permute-done((bf16[2,384,128]{2,1,0:T(8,128)(2,1)S(1)}, bf16[2,384,128]{2,1,0:T(8,128)(2,1)S(1)}, u32[]{:S(2)}, u32[]{:S(2)}) %collective-permute-start.5) | collective-permute-done | bytes 196640 | tf_op jit(solution)/shard_map/ppermute | solution.py:29
  19.3 3.3 %attend.8 = (f32[2,128,1024]{2,1,0:T(8,128)S(1)}, f32[2,896,128]{2,1,0:T(8,128)S(1)}) custom-call(s32[2]{0:T(128)S(1)} %pad_add_fusion.meta, s32[16]{0:T(128)S(1)} %copy-done.5, bf16[272,1024]{1,0:T(8,128)(2,1)S(1)} %get-tuple-element.55.refs_0_, bf16[272,1024]{1,0:T(8,128)(2,1)S(1)} %collective-permute-done.3.refs_1_, ...), custom_call_target="tpu_custom_call" | custom-call | flops 805306368 | bytes 1048576 | tf_op jit(solution)/shard_map/attend/pallas_call | solution.py:369
  26.1 4.0 %collective-permute-done.7.refs_3_ = bf16[2,384,128]{2,1,0:T(8,128)(2,1)S(1)} collective-permute-done((bf16[2,384,128]{2,1,0:T(8,128)(2,1)S(1)}, bf16[2,384,128]{2,1,0:T(8,128)(2,1)S(1)}, u32[]{:S(2)}, u32[]{:S(2)}) %collective-permute-start.7) | collective-permute-done | bytes 196640 | tf_op jit(solution)/shard_map/ppermute | solution.py:29
  30.0 3.4 %attend.9 = (f32[2,128,1024]{2,1,0:T(8,128)S(1)}, f32[2,896,128]{2,1,0:T(8,128)S(1)}) custom-call(s32[2]{0:T(128)S(1)} %pad_add_fusion.meta, s32[16]{0:T(128)S(1)} %copy-done.5, bf16[272,1024]{1,0:T(8,128)(2,1)S(1)} %get-tuple-element.55.refs_0_, bf16[272,1024]{1,0:T(8,128)(2,1)S(1)} %collective-permute-done.3.refs_1_, ...), custom_call_target="tpu_custom_call", output_to_operand_aliasing={{0}: (6, {})} | custom-call | flops 805306368 | bytes 1048576 | tf_op jit(solution)/shard_map/attend/pallas_call | solution.py:369
  35.7 3.7 %collective-permute-done.9.refs_3_ = bf16[2,384,128]{2,1,0:T(8,128)(2,1)S(1)} collective-permute-done((bf16[2,384,128]{2,1,0:T(8,128)(2,1)S(1)}, bf16[2,384,128]{2,1,0:T(8,128)(2,1)S(1)}, u32[]{:S(2)}, u32[]{:S(2)}) %collective-permute-start.9) | collective-permute-done | bytes 196640 | tf_op jit(solution)/shard_map/ppermute | solution.py:29
  39.5 3.4 %attend.10 = (f32[2,128,1024]{2,1,0:T(8,128)S(1)}, f32[2,896,128]{2,1,0:T(8,128)S(1)}) custom-call(s32[2]{0:T(128)S(1)} %pad_add_fusion.meta, s32[16]{0:T(128)S(1)} %copy-done.5, bf16[272,1024]{1,0:T(8,128)(2,1)S(1)} %get-tuple-element.55.refs_0_, bf16[272,1024]{1,0:T(8,128)(2,1)S(1)} %collective-permute-done.3.refs_1_, ...), custom_call_target="tpu_custom_call", output_to_operand_aliasing={{0}: (6, {})} | custom-call | flops 805306368 | bytes 1048576 | tf_op jit(solution)/shard_map/attend/pallas_call | solution.py:369
  42.9 3.3 %attend.11 = (f32[2,128,1024]{2,1,0:T(8,128)S(1)}, f32[2,512,128]{2,1,0:T(8,128)S(1)}, bf16[2,384,128]{2,1,0:T(8,128)(2,1)S(1)}) custom-call(s32[2]{0:T(128)S(1)} %pad_add_fusion.meta, s32[16]{0:T(128)S(1)} %copy-done.5, bf16[272,1024]{1,0:T(8,128)(2,1)S(1)} %collective-permute-done.10.refs_0_, bf16[272,1024]{1,0:T(8,128)(2,1)S(1)} %collective-permute-done.11.refs_1_, ...), custom_call_target="tpu_custom_call" | custom-call | flops 805306368 | bytes 1048576 | tf_op jit(solution)/shard_map/attend/pallas_call | solution.py:369
  47.6 3.5 %attend.12 = (f32[2,128,1024]{2,1,0:T(8,128)S(1)}, f32[2,512,128]{2,1,0:T(8,128)S(1)}, bf16[2,384,128]{2,1,0:T(8,128)(2,1)S(1)}) custom-call(s32[2]{0:T(128)S(1)} %pad_add_fusion.meta, s32[16]{0:T(128)S(1)} %copy-done.5, bf16[272,1024]{1,0:T(8,128)(2,1)S(1)} %collective-permute-done.10.refs_0_, ...), custom_call_target="tpu_custom_call", output_to_operand_aliasing={{0}: (6, {})} | custom-call | flops 805306368 | bytes 1048576 | tf_op jit(solution)/shard_map/attend/pallas_call | solution.py:369
  51.9 3.5 %attend.13 = (f32[2,128,1024]{2,1,0:T(8,128)S(1)}, f32[2,512,128]{2,1,0:T(8,128)S(1)}, bf16[2,384,128]{2,1,0:T(8,128)(2,1)S(1)}) custom-call(s32[2]{0:T(128)S(1)} %pad_add_fusion.meta, s32[16]{0:T(128)S(1)} %copy-done.5, bf16[272,1024]{1,0:T(8,128)(2,1)S(1)} %collective-permute-done.10.refs_0_, ...), custom_call_target="tpu_custom_call", output_to_operand_aliasing={{0}: (6, {})} | custom-call | flops 805306368 | bytes 1048576 | tf_op jit(solution)/shard_map/attend/pallas_call | solution.py:369
  55.3 3.0 %collective-permute-done.12.refs_3_.back = bf16[4,384,128]{2,1,0:T(8,128)(2,1)S(1)} collective-permute-done((bf16[4,384,128]{2,1,0:T(8,128)(2,1)S(1)}, bf16[4,384,128]{2,1,0:T(8,128)(2,1)S(1)}, u32[]{:S(2)}, u32[]{:S(2)}) %collective-permute-start.12) | collective-permute-done | bytes 393248 | tf_op jit(solution)/shard_map/ppermute | solution.py:29
  58.4 3.6 %attend.14 = (bf16[128,1024]{1,0:T(8,128)(2,1)S(1)}, bf16[128,1024]{1,0:T(8,128)(2,1)S(1)}, f32[2,896,128]{2,1,0:T(8,128)S(1)}) custom-call(s32[2]{0:T(128)S(1)} %pad_add_fusion.meta, s32[16]{0:T(128)S(1)} %copy-done.5, bf16[272,1024]{1,0:T(8,128)(2,1)S(1)} %collective-permute-done.10.refs_0_, bf16[272,1024]{1,0:T(8,128)(2,1)S(1)} %collective-permute-done.11.refs_1_, ...), custom_call_target="tpu_custom_call" | custom-call | flops 805306368 | bytes 1048576 | tf_op jit(solution)/shard_map/attend/pallas_call | solution.py:369
  62.5 1.4 %collective-permute-start.18 = (bf16[2,384,128]{2,1,0:T(8,128)(2,1)S(1)}, bf16[2,384,128]{2,1,0:T(8,128)(2,1)S(1)}, u32[]{:S(2)}, u32[]{:S(2)}) collective-permute-start(bf16[2,384,128]{2,1,0:T(8,128)(2,1)S(1)} %get-tuple-element.95), channel_id=1, source_target_pairs={{4,0},{5,1},{6,2},{7,3},{0,4},{1,5},{2,6},{3,7},{12,8},{13,9},{14,... | collective-permute-start | bytes 589832 | tf_op jit(solution)/shard_map/ppermute | solution.py:29
  64.6 3.4 %attend.15 = (bf16[128,1024]{1,0:T(8,128)(2,1)S(1)}, bf16[128,1024]{1,0:T(8,128)(2,1)S(1)}, f32[2,512,128]{2,1,0:T(8,128)S(1)}, bf16[2,384,128]{2,1,0:T(8,128)(2,1)S(1)}) custom-call(s32[2]{0:T(128)S(1)} %pad_add_fusion.meta, s32[16]{0:T(128)S(1)} %copy-done.5, bf16[272,1024]{1,0:T(8,128)(2,1)S(1)} %get-tuple-element.55.refs_0_, ...), custom_call_target="tpu_custom_call" | custom-call | flops 805306368 | bytes 1048576 | tf_op jit(solution)/shard_map/attend/pallas_call | solution.py:369
  68.6 1.5 %collective-permute-start.15 = (bf16[128,1280]{1,0:T(8,128)(2,1)S(1)}, bf16[128,1280]{1,0:T(8,128)(2,1)S(1)}, u32[]{:S(2)}, u32[]{:S(2)}) collective-permute-start(bf16[128,1280]{1,0:T(8,128)(2,1)S(1)} %get-tuple-element.84.refs_7_), channel_id=1, source_target_pairs={{0,2},{1,3},{2,0},{3,1},{4,6},{5,7},{6,4},{7,5},{8,10},{9,11},{10,... | collective-permute-start | bytes 983048 | tf_op jit(solution)/shard_map/ppermute | solution.py:33
  70.4 1.5 %collective-permute-start.21 = (bf16[2,512,128]{2,1,0:T(8,128)(2,1)S(1)}, bf16[2,512,128]{2,1,0:T(8,128)(2,1)S(1)}, u32[]{:S(2)}, u32[]{:S(2)}) collective-permute-start(bf16[2,512,128]{2,1,0:T(8,128)(2,1)S(1)} %pack_sum.3), channel_id=1, source_target_pairs={{24,0},{0,8},{8,16},{16,24},{25,1},{1,9},{9,17},{17,25},{26,2},{2,... | collective-permute-start | bytes 786440 | tf_op jit(solution)/shard_map/ppermute | solution.py:29
  73.7 4.9 %collective-permute-done.21.packet = bf16[2,512,128]{2,1,0:T(8,128)(2,1)S(1)} collective-permute-done((bf16[2,512,128]{2,1,0:T(8,128)(2,1)S(1)}, bf16[2,512,128]{2,1,0:T(8,128)(2,1)S(1)}, u32[]{:S(2)}, u32[]{:S(2)}) %collective-permute-start.21) | collective-permute-done | bytes 262176 | tf_op jit(solution)/shard_map/ppermute | solution.py:29
  79.4 2.1 %collective-permute-start.24 = (bf16[2,128,128]{2,1,0:T(8,128)(2,1)S(1)}, bf16[2,128,128]{2,1,0:T(8,128)(2,1)S(1)}, u32[]{:S(2)}, u32[]{:S(2)}) collective-permute-start(bf16[2,128,128]{2,1,0:T(8,128)(2,1)S(1)} %get-tuple-element.100), channel_id=1, source_target_pairs={{0,10},{1,11},{2,8},{3,9},{4,14},{5,15},{6,12},{7,13},{8,18},{9,19... | collective-permute-start | bytes 196616 | tf_op jit(solution)/shard_map/ppermute | solution.py:39
  81.6 3.1 %collective-permute-start.25 = (bf16[2,128,128]{2,1,0:T(8,128)(2,1)S(1)}, bf16[2,128,128]{2,1,0:T(8,128)(2,1)S(1)}, u32[]{:S(2)}, u32[]{:S(2)}) collective-permute-start(bf16[2,128,128]{2,1,0:T(8,128)(2,1)S(1)} %get-tuple-element.101), channel_id=1, source_target_pairs={{0,11},{1,10},{2,9},{3,8},{4,15},{5,14},{6,13},{7,12},{8,19},{9,18... | collective-permute-start | bytes 196616 | tf_op jit(solution)/shard_map/ppermute | solution.py:39
  84.6 1.5 %place_heads.1 = (bf16[1,128,4096]{2,1,0:T(8,128)(2,1)}, f32[8,128]{1,0:T(8,128)S(1)}) custom-call(s32[2]{0:T(128)S(1)} %pad_add_fusion.meta, bf16[128,1024]{1,0:T(8,128)(2,1)S(1)} %get-tuple-element.85.dq_own, bf16[128,640]{1,0:T(8,128)(2,1)S(1)} %collective-permute-done.13.near_one, bf16[128,640]{1,0:T(8,128)(2,1)S(1)} %collective-permute-done.14.near_two, ...), custom_call_target="tpu_custom_call" | custom-call | tf_op jit(solution)/shard_map/place_heads/pallas_call | solution.py:222
  86.2 3.0 %collective-permute-done.24.hop2 = bf16[2,128,128]{2,1,0:T(8,128)(2,1)S(1)} collective-permute-done((bf16[2,128,128]{2,1,0:T(8,128)(2,1)S(1)}, bf16[2,128,128]{2,1,0:T(8,128)(2,1)S(1)}, u32[]{:S(2)}, u32[]{:S(2)}) %collective-permute-start.24) | collective-permute-done | bytes 65568 | tf_op jit(solution)/shard_map/ppermute | solution.py:39
  (69 shorter events, 22.7 us)
Async XLA Ops:
  3.1 8.2 %collective-permute-start = (bf16[2,128,128]{2,1,0:T(8,128)(2,1)S(1)}, bf16[2,128,128]{2,1,0:T(8,128)(2,1)S(1)}, u32[]{:S(2)}, u32[]{:S(2)}) collective-permute-start(bf16[2,128,128]{2,1,0:T(8,128)(2,1)S(1)} %get-tuple-element.57), channel_id=1, source_target_pairs={{0,1},{1,0},{2,3},{3,2},{4,5},{5,4},{6,7},{7,6},{8,9},{9,8},{10,11... | collective-permute-start | bytes 196616 | tf_op jit(solution)/shard_map/ppermute | solution.py:33
  3.7 7.7 %collective-permute-start.1 = (bf16[2,128,128]{2,1,0:T(8,128)(2,1)S(1)}, bf16[2,128,128]{2,1,0:T(8,128)(2,1)S(1)}, u32[]{:S(2)}, u32[]{:S(2)}) collective-permute-start(bf16[2,128,128]{2,1,0:T(8,128)(2,1)S(1)} %get-tuple-element.58), channel_id=1, source_target_pairs={{0,2},{1,3},{2,0},{3,1},{4,6},{5,7},{6,4},{7,5},{8,10},{9,11},{10,... | collective-permute-start | bytes 196616 | tf_op jit(solution)/shard_map/ppermute | solution.py:33
  11.9 7.4 %collective-permute-start.3 = (bf16[272,1024]{1,0:T(8,128)(2,1)S(1)}, bf16[272,1024]{1,0:T(8,128)(2,1)S(1)}, u32[]{:S(2)}, u32[]{:S(2)}) collective-permute-start(bf16[272,1024]{1,0:T(8,128)(2,1)S(1)} %later.3), channel_id=1, source_target_pairs={{0,1},{1,0},{2,3},{3,2},{4,5},{5,4},{6,7},{7,6},{8,9},{9,8},{10,11... | collective-permute-start | bytes 1671176 | tf_op jit(solution)/shard_map/ppermute | solution.py:33
  12.1 7.2 %collective-permute-start.5 = (bf16[2,384,128]{2,1,0:T(8,128)(2,1)S(1)}, bf16[2,384,128]{2,1,0:T(8,128)(2,1)S(1)}, u32[]{:S(2)}, u32[]{:S(2)}) collective-permute-start(bf16[2,384,128]{2,1,0:T(8,128)(2,1)S(1)} %get-tuple-element.60.refs_1_), channel_id=1, source_target_pairs={{4,0},{5,1},{6,2},{7,3},{0,4},{1,5},{2,6},{3,7},{12,8},{13,9},{14,... | collective-permute-start | bytes 589832 | tf_op jit(solution)/shard_map/ppermute | solution.py:29
  14.1 10.0 %collective-permute-start.4 = (bf16[2,512,128]{2,1,0:T(8,128)(2,1)S(1)}, bf16[2,512,128]{2,1,0:T(8,128)(2,1)S(1)}, u32[]{:S(2)}, u32[]{:S(2)}) collective-permute-start(bf16[2,512,128]{2,1,0:T(8,128)(2,1)S(1)} %get-tuple-element.61.refs_2_), channel_id=1, source_target_pairs={{24,0},{0,8},{8,16},{16,24},{25,1},{1,9},{9,17},{17,25},{26,2},{2,... | collective-permute-start | bytes 786440 | tf_op jit(solution)/shard_map/ppermute | solution.py:29
  15.7 27.2 %collective-permute-start.10 = (bf16[272,1024]{1,0:T(8,128)(2,1)S(1)}, bf16[272,1024]{1,0:T(8,128)(2,1)S(1)}, u32[]{:S(2)}, u32[]{:S(2)}) collective-permute-start(bf16[272,1024]{1,0:T(8,128)(2,1)S(1)} %later.4), channel_id=1, source_target_pairs={{0,2},{1,3},{2,0},{3,1},{4,6},{5,7},{6,4},{7,5},{8,10},{9,11},{10,... | collective-permute-start | bytes 1671176 | tf_op jit(solution)/shard_map/ppermute | solution.py:33
  17.2 25.7 %collective-permute-start.11 = (bf16[272,1024]{1,0:T(8,128)(2,1)S(1)}, bf16[272,1024]{1,0:T(8,128)(2,1)S(1)}, u32[]{:S(2)}, u32[]{:S(2)}) collective-permute-start(bf16[272,1024]{1,0:T(8,128)(2,1)S(1)} %later.5), channel_id=1, source_target_pairs={{0,3},{1,2},{2,1},{3,0},{4,7},{5,6},{6,5},{7,4},{8,11},{9,10},{10,... | collective-permute-start | bytes 1671176 | tf_op jit(solution)/shard_map/ppermute | solution.py:33
  24.1 6.0 %collective-permute-start.7 = (bf16[2,384,128]{2,1,0:T(8,128)(2,1)S(1)}, bf16[2,384,128]{2,1,0:T(8,128)(2,1)S(1)}, u32[]{:S(2)}, u32[]{:S(2)}) collective-permute-start(bf16[2,384,128]{2,1,0:T(8,128)(2,1)S(1)} %get-tuple-element.64), channel_id=1, source_target_pairs={{4,0},{5,1},{6,2},{7,3},{0,4},{1,5},{2,6},{3,7},{12,8},{13,9},{14,... | collective-permute-start | bytes 589832 | tf_op jit(solution)/shard_map/ppermute | solution.py:29
  24.6 9.1 %collective-permute-start.6 = (bf16[2,512,128]{2,1,0:T(8,128)(2,1)S(1)}, bf16[2,512,128]{2,1,0:T(8,128)(2,1)S(1)}, u32[]{:S(2)}, u32[]{:S(2)}) collective-permute-start(bf16[2,512,128]{2,1,0:T(8,128)(2,1)S(1)} %get-tuple-element.63.refs_2_), channel_id=1, source_target_pairs={{24,0},{0,8},{8,16},{16,24},{25,1},{1,9},{9,17},{17,25},{26,2},{2,... | collective-permute-start | bytes 786440 | tf_op jit(solution)/shard_map/ppermute | solution.py:29
  33.7 5.7 %collective-permute-start.9 = (bf16[2,384,128]{2,1,0:T(8,128)(2,1)S(1)}, bf16[2,384,128]{2,1,0:T(8,128)(2,1)S(1)}, u32[]{:S(2)}, u32[]{:S(2)}) collective-permute-start(bf16[2,384,128]{2,1,0:T(8,128)(2,1)S(1)} %get-tuple-element.67), channel_id=1, source_target_pairs={{4,0},{5,1},{6,2},{7,3},{0,4},{1,5},{2,6},{3,7},{12,8},{13,9},{14,... | collective-permute-start | bytes 589832 | tf_op jit(solution)/shard_map/ppermute | solution.py:29
  35.1 11.1 %collective-permute-start.8 = (bf16[2,512,128]{2,1,0:T(8,128)(2,1)S(1)}, bf16[2,512,128]{2,1,0:T(8,128)(2,1)S(1)}, u32[]{:S(2)}, u32[]{:S(2)}) collective-permute-start(bf16[2,512,128]{2,1,0:T(8,128)(2,1)S(1)} %get-tuple-element.66.refs_2_), channel_id=1, source_target_pairs={{24,0},{0,8},{8,16},{16,24},{25,1},{1,9},{9,17},{17,25},{26,2},{2,... | collective-permute-start | bytes 786440 | tf_op jit(solution)/shard_map/ppermute | solution.py:29
  46.3 12.1 %collective-permute-start.12 = (bf16[4,384,128]{2,1,0:T(8,128)(2,1)S(1)}, bf16[4,384,128]{2,1,0:T(8,128)(2,1)S(1)}, u32[]{:S(2)}, u32[]{:S(2)}) collective-permute-start(bf16[4,384,128]{2,1,0:T(8,128)(2,1)S(1)} %side_by_side.1), channel_id=1, source_target_pairs={{4,0},{5,1},{6,2},{7,3},{0,4},{1,5},{2,6},{3,7},{12,8},{13,9},{14,... | collective-permute-start | bytes 1179656 | tf_op jit(solution)/shard_map/ppermute | solution.py:29
  51.1 11.0 %collective-permute-start.19 = (bf16[2,384,128]{2,1,0:T(8,128)(2,1)S(1)}, bf16[2,384,128]{2,1,0:T(8,128)(2,1)S(1)}, u32[]{:S(2)}, u32[]{:S(2)}) collective-permute-start(bf16[2,384,128]{2,1,0:T(8,128)(2,1)S(1)} %get-tuple-element.97), channel_id=1, source_target_pairs={{4,0},{5,1},{6,2},{7,3},{0,4},{1,5},{2,6},{3,7},{12,8},{13,9},{14,... | collective-permute-start | bytes 589832 | tf_op jit(solution)/shard_map/ppermute | solution.py:29
  62.1 8.2 %collective-permute-start.20 = (bf16[2,512,128]{2,1,0:T(8,128)(2,1)S(1)}, bf16[2,512,128]{2,1,0:T(8,128)(2,1)S(1)}, u32[]{:S(2)}, u32[]{:S(2)}) collective-permute-start(bf16[2,512,128]{2,1,0:T(8,128)(2,1)S(1)} %pack_sum.2), channel_id=1, source_target_pairs={{24,0},{0,8},{8,16},{16,24},{25,1},{1,9},{9,17},{17,25},{26,2},{2,... | collective-permute-start | bytes 786440 | tf_op jit(solution)/shard_map/ppermute | solution.py:29
  62.5 7.6 %collective-permute-start.18 = (bf16[2,384,128]{2,1,0:T(8,128)(2,1)S(1)}, bf16[2,384,128]{2,1,0:T(8,128)(2,1)S(1)}, u32[]{:S(2)}, u32[]{:S(2)}) collective-permute-start(bf16[2,384,128]{2,1,0:T(8,128)(2,1)S(1)} %get-tuple-element.95), channel_id=1, source_target_pairs={{4,0},{5,1},{6,2},{7,3},{0,4},{1,5},{2,6},{3,7},{12,8},{13,9},{14,... | collective-permute-start | bytes 589832 | tf_op jit(solution)/shard_map/ppermute | solution.py:29
  68.6 13.0 %collective-permute-start.15 = (bf16[128,1280]{1,0:T(8,128)(2,1)S(1)}, bf16[128,1280]{1,0:T(8,128)(2,1)S(1)}, u32[]{:S(2)}, u32[]{:S(2)}) collective-permute-start(bf16[128,1280]{1,0:T(8,128)(2,1)S(1)} %get-tuple-element.84.refs_7_), channel_id=1, source_target_pairs={{0,2},{1,3},{2,0},{3,1},{4,6},{5,7},{6,4},{7,5},{8,10},{9,11},{10,... | collective-permute-start | bytes 983048 | tf_op jit(solution)/shard_map/ppermute | solution.py:33
  70.4 8.2 %collective-permute-start.21 = (bf16[2,512,128]{2,1,0:T(8,128)(2,1)S(1)}, bf16[2,512,128]{2,1,0:T(8,128)(2,1)S(1)}, u32[]{:S(2)}, u32[]{:S(2)}) collective-permute-start(bf16[2,512,128]{2,1,0:T(8,128)(2,1)S(1)} %pack_sum.3), channel_id=1, source_target_pairs={{24,0},{0,8},{8,16},{16,24},{25,1},{1,9},{9,17},{17,25},{26,2},{2,... | collective-permute-start | bytes 786440 | tf_op jit(solution)/shard_map/ppermute | solution.py:29
  71.9 12.8 %collective-permute-start.16 = (bf16[128,1280]{1,0:T(8,128)(2,1)S(1)}, bf16[128,1280]{1,0:T(8,128)(2,1)S(1)}, u32[]{:S(2)}, u32[]{:S(2)}) collective-permute-start(bf16[128,1280]{1,0:T(8,128)(2,1)S(1)} %get-tuple-element.89), channel_id=1, source_target_pairs={{0,3},{1,2},{2,1},{3,0},{4,7},{5,6},{6,5},{7,4},{8,11},{9,10},{10,... | collective-permute-start | bytes 983048 | tf_op jit(solution)/shard_map/ppermute | solution.py:33
  72.5 6.8 %collective-permute-start.13 = (bf16[128,640]{1,0:T(8,128)(2,1)S(1)}, bf16[128,640]{1,0:T(8,128)(2,1)S(1)}, u32[]{:S(2)}, u32[]{:S(2)}) collective-permute-start(bf16[128,640]{1,0:T(8,128)(2,1)S(1)} %get-tuple-element.87), channel_id=1, source_target_pairs={{0,1},{1,0},{2,3},{3,2},{4,5},{5,4},{6,7},{7,6},{8,9},{9,8},{10,11... | collective-permute-start | bytes 491528 | tf_op jit(solution)/shard_map/ppermute | solution.py:33
  73.7 5.7 %collective-permute-start.14 = (bf16[128,640]{1,0:T(8,128)(2,1)S(1)}, bf16[128,640]{1,0:T(8,128)(2,1)S(1)}, u32[]{:S(2)}, u32[]{:S(2)}) collective-permute-start(bf16[128,640]{1,0:T(8,128)(2,1)S(1)} %get-tuple-element.88), channel_id=1, source_target_pairs={{0,1},{1,0},{2,3},{3,2},{4,5},{5,4},{6,7},{7,6},{8,9},{9,8},{10,11... | collective-permute-start | bytes 491528 | tf_op jit(solution)/shard_map/ppermute | solution.py:33
  79.3 6.9 %collective-permute-start.22 = (bf16[2,128,128]{2,1,0:T(8,128)(2,1)S(1)}, bf16[2,128,128]{2,1,0:T(8,128)(2,1)S(1)}, u32[]{:S(2)}, u32[]{:S(2)}) collective-permute-start(bf16[2,128,128]{2,1,0:T(8,128)(2,1)S(1)} %get-tuple-element.98), channel_id=1, source_target_pairs={{0,8},{1,9},{2,10},{3,11},{4,12},{5,13},{6,14},{7,15},{8,16},{9,17... | collective-permute-start | bytes 196616 | tf_op jit(solution)/shard_map/ppermute | solution.py:39
  79.4 6.8 %collective-permute-start.23 = (bf16[2,128,128]{2,1,0:T(8,128)(2,1)S(1)}, bf16[2,128,128]{2,1,0:T(8,128)(2,1)S(1)}, u32[]{:S(2)}, u32[]{:S(2)}) collective-permute-start(bf16[2,128,128]{2,1,0:T(8,128)(2,1)S(1)} %get-tuple-element.99), channel_id=1, source_target_pairs={{0,9},{1,8},{2,11},{3,10},{4,13},{5,12},{6,15},{7,14},{8,17},{9,16... | collective-permute-start | bytes 196616 | tf_op jit(solution)/shard_map/ppermute | solution.py:39
  79.4 9.8 %collective-permute-start.24 = (bf16[2,128,128]{2,1,0:T(8,128)(2,1)S(1)}, bf16[2,128,128]{2,1,0:T(8,128)(2,1)S(1)}, u32[]{:S(2)}, u32[]{:S(2)}) collective-permute-start(bf16[2,128,128]{2,1,0:T(8,128)(2,1)S(1)} %get-tuple-element.100), channel_id=1, source_target_pairs={{0,10},{1,11},{2,8},{3,9},{4,14},{5,15},{6,12},{7,13},{8,18},{9,19... | collective-permute-start | bytes 196616 | tf_op jit(solution)/shard_map/ppermute | solution.py:39
  81.6 7.7 %collective-permute-start.25 = (bf16[2,128,128]{2,1,0:T(8,128)(2,1)S(1)}, bf16[2,128,128]{2,1,0:T(8,128)(2,1)S(1)}, u32[]{:S(2)}, u32[]{:S(2)}) collective-permute-start(bf16[2,128,128]{2,1,0:T(8,128)(2,1)S(1)} %get-tuple-element.101), channel_id=1, source_target_pairs={{0,11},{1,10},{2,9},{3,8},{4,15},{5,14},{6,13},{7,12},{8,19},{9,18... | collective-permute-start | bytes 196616 | tf_op jit(solution)/shard_map/ppermute | solution.py:39
  (9 other events, 22.3 us)

commit v5 on v4

--- a/solution.py
+++ b/solution.py
@@ -463,7 +463,7 @@
         functools.partial(pack_cross, (2, 3)), [cross] * 2, [SMEM] + [VMEM] * 4,
         [meta, *accs[1], sums[0], back_zero], scratch=[whole], cost=2**20,
     )
-    back_three = send_back(call(0, 3, [accs[1][0], sent[0]]))
+    back_three = send_back(call(0, 3, [accs[1][0]]))
     _, packet = pass_sums(2, 0, back_two, packet, sums[3])
     near_half = ((tok, (wide + 2 * HD) // 2), BF16)
     near_one, near_two, kept = small_call(

time: 90.9 us -> 90.8 us (level)
  starting transfers between devices: 26 us -> 27 us
  waiting for transfers between devices: 23.2 us -> 22.2 us
    ppermute x12, waiting for transfers between devices: 20.1 us -> 19.2 us  [shifted(): return lax.ppermute(block, axis, route)]
  transfers between devices with their start and end apart: 26 -> 26, of which waited for: 10 -> 9; matrix products, arithmetic and copies ran while one was open for 0% -> 0% of each run, Pallas kernels for 36% -> 35%
where the time goes in v5:
time: 90.8 us; the launch traced here: 90.5 us
  Pallas kernels  34.7 us (38%)
  starting transfers between devices  27 us (30%)
  waiting for transfers between devices  22.2 us (24%)
  local copies, waits for them, and re-layouts  5.58 us (6%)
  between operations  0.92 us (1%)
    pallas_call x8, Pallas kernels, attend_call(): pl.pallas_call(functools.partial(attend, lag, masks, n_blk, n_z, first, l...  27.3 us
    ppermute x12, waiting for transfers between devices, shifted(): return lax.ppermute(block, axis, route)  19.2 us
    ppermute x12, starting transfers between devices, shifted(): return lax.ppermute(block, axis, route)  13.8 us
    ppermute x10, starting transfers between devices, crossed(): lax.ppermute(block, 'blk', [(i, i ^ mask) for i in range(lax.axis_size('b...  7.96 us
    pallas_call x11, Pallas kernels, small_call(): pl.pallas_call(body, out_shape=shapes, in_specs=specs, out_specs=[ANY if...  7.33 us
    unnamed x15, local copies, waits for them, and re-layouts  5.58 us
    ppermute x4, starting transfers between devices, hopped(): return lax.ppermute(block, ('head', 'blk'), route)  5.31 us
    ppermute x4, waiting for transfers between devices, hopped(): return lax.ppermute(block, ('head', 'blk'), route)  3.05 us
  transfers between devices with their start and end apart: 26, of which 9 were waited for; matrix products, arithmetic and copies ran while one was open for 0% of the time, Pallas kernels for 35%

profile of v5, /device:TPU:0, one launch (start us, length us, event | category | flops | bytes accessed | tf_op | source)
XLA Modules:
  0.0 90.5 jit_solution(6328085879665336751)
XLA Ops:
  3.7 2.6 %collective-permute-start.1 = (bf16[2,128,128]{2,1,0:T(8,128)(2,1)S(1)}, bf16[2,128,128]{2,1,0:T(8,128)(2,1)S(1)}, u32[]{:S(2)}, u32[]{:S(2)}) collective-permute-start(bf16[2,128,128]{2,1,0:T(8,128)(2,1)S(1)} %get-tuple-element.58), channel_id=1, source_target_pairs={{0,2},{1,3},{2,0},{3,1},{4,6},{5,7},{6,4},{7,5},{8,10},{9,11},{10,... | collective-permute-start | bytes 196616 | tf_op jit(solution)/shard_map/ppermute | solution.py:33
  12.1 2.0 %collective-permute-start.5 = (bf16[2,384,128]{2,1,0:T(8,128)(2,1)S(1)}, bf16[2,384,128]{2,1,0:T(8,128)(2,1)S(1)}, u32[]{:S(2)}, u32[]{:S(2)}) collective-permute-start(bf16[2,384,128]{2,1,0:T(8,128)(2,1)S(1)} %get-tuple-element.60.refs_1_), channel_id=1, source_target_pairs={{4,0},{5,1},{6,2},{7,3},{0,4},{1,5},{2,6},{3,7},{12,8},{13,9},{14,... | collective-permute-start | bytes 589832 | tf_op jit(solution)/shard_map/ppermute | solution.py:29
  14.1 1.6 %collective-permute-start.4 = (bf16[2,512,128]{2,1,0:T(8,128)(2,1)S(1)}, bf16[2,512,128]{2,1,0:T(8,128)(2,1)S(1)}, u32[]{:S(2)}, u32[]{:S(2)}) collective-permute-start(bf16[2,512,128]{2,1,0:T(8,128)(2,1)S(1)} %get-tuple-element.61.refs_2_), channel_id=1, source_target_pairs={{24,0},{0,8},{8,16},{16,24},{25,1},{1,9},{9,17},{17,25},{26,2},{2,... | collective-permute-start | bytes 786440 | tf_op jit(solution)/shard_map/ppermute | solution.py:29
  15.7 1.5 %collective-permute-start.10 = (bf16[272,1024]{1,0:T(8,128)(2,1)S(1)}, bf16[272,1024]{1,0:T(8,128)(2,1)S(1)}, u32[]{:S(2)}, u32[]{:S(2)}) collective-permute-start(bf16[272,1024]{1,0:T(8,128)(2,1)S(1)} %later.4), channel_id=1, source_target_pairs={{0,2},{1,3},{2,0},{3,1},{4,6},{5,7},{6,4},{7,5},{8,10},{9,11},{10,... | collective-permute-start | bytes 1671176 | tf_op jit(solution)/shard_map/ppermute | solution.py:33
  17.2 2.2 %collective-permute-done.5.refs_3_ = bf16[2,384,128]{2,1,0:T(8,128)(2,1)S(1)} collective-permute-done((bf16[2,384,128]{2,1,0:T(8,128)(2,1)S(1)}, bf16[2,384,128]{2,1,0:T(8,128)(2,1)S(1)}, u32[]{:S(2)}, u32[]{:S(2)}) %collective-permute-start.5) | collective-permute-done | bytes 196640 | tf_op jit(solution)/shard_map/ppermute | solution.py:29
  19.3 3.3 %attend.8 = (f32[2,128,1024]{2,1,0:T(8,128)S(1)}, f32[2,896,128]{2,1,0:T(8,128)S(1)}) custom-call(s32[2]{0:T(128)S(1)} %pad_add_fusion.meta, s32[16]{0:T(128)S(1)} %copy-done.5, bf16[272,1024]{1,0:T(8,128)(2,1)S(1)} %get-tuple-element.55.refs_0_, bf16[272,1024]{1,0:T(8,128)(2,1)S(1)} %collective-permute-done.3.refs_1_, ...), custom_call_target="tpu_custom_call" | custom-call | flops 805306368 | bytes 1048576 | tf_op jit(solution)/shard_map/attend/pallas_call | solution.py:369
  26.0 4.0 %collective-permute-done.7.refs_3_ = bf16[2,384,128]{2,1,0:T(8,128)(2,1)S(1)} collective-permute-done((bf16[2,384,128]{2,1,0:T(8,128)(2,1)S(1)}, bf16[2,384,128]{2,1,0:T(8,128)(2,1)S(1)}, u32[]{:S(2)}, u32[]{:S(2)}) %collective-permute-start.7) | collective-permute-done | bytes 196640 | tf_op jit(solution)/shard_map/ppermute | solution.py:29
  30.0 3.4 %attend.9 = (f32[2,128,1024]{2,1,0:T(8,128)S(1)}, f32[2,896,128]{2,1,0:T(8,128)S(1)}) custom-call(s32[2]{0:T(128)S(1)} %pad_add_fusion.meta, s32[16]{0:T(128)S(1)} %copy-done.5, bf16[272,1024]{1,0:T(8,128)(2,1)S(1)} %get-tuple-element.55.refs_0_, bf16[272,1024]{1,0:T(8,128)(2,1)S(1)} %collective-permute-done.3.refs_1_, ...), custom_call_target="tpu_custom_call", output_to_operand_aliasing={{0}: (6, {})} | custom-call | flops 805306368 | bytes 1048576 | tf_op jit(solution)/shard_map/attend/pallas_call | solution.py:369
  35.7 3.7 %collective-permute-done.9.refs_3_ = bf16[2,384,128]{2,1,0:T(8,128)(2,1)S(1)} collective-permute-done((bf16[2,384,128]{2,1,0:T(8,128)(2,1)S(1)}, bf16[2,384,128]{2,1,0:T(8,128)(2,1)S(1)}, u32[]{:S(2)}, u32[]{:S(2)}) %collective-permute-start.9) | collective-permute-done | bytes 196640 | tf_op jit(solution)/shard_map/ppermute | solution.py:29
  39.5 3.4 %attend.10 = (f32[2,128,1024]{2,1,0:T(8,128)S(1)}, f32[2,896,128]{2,1,0:T(8,128)S(1)}) custom-call(s32[2]{0:T(128)S(1)} %pad_add_fusion.meta, s32[16]{0:T(128)S(1)} %copy-done.5, bf16[272,1024]{1,0:T(8,128)(2,1)S(1)} %get-tuple-element.55.refs_0_, bf16[272,1024]{1,0:T(8,128)(2,1)S(1)} %collective-permute-done.3.refs_1_, ...), custom_call_target="tpu_custom_call", output_to_operand_aliasing={{0}: (6, {})} | custom-call | flops 805306368 | bytes 1048576 | tf_op jit(solution)/shard_map/attend/pallas_call | solution.py:369
  42.9 3.3 %attend.11 = (f32[2,128,1024]{2,1,0:T(8,128)S(1)}, f32[2,512,128]{2,1,0:T(8,128)S(1)}, bf16[2,384,128]{2,1,0:T(8,128)(2,1)S(1)}) custom-call(s32[2]{0:T(128)S(1)} %pad_add_fusion.meta, s32[16]{0:T(128)S(1)} %copy-done.5, bf16[272,1024]{1,0:T(8,128)(2,1)S(1)} %collective-permute-done.10.refs_0_, bf16[272,1024]{1,0:T(8,128)(2,1)S(1)} %collective-permute-done.11.refs_1_, ...), custom_call_target="tpu_custom_call" | custom-call | flops 805306368 | bytes 1048576 | tf_op jit(solution)/shard_map/attend/pallas_call | solution.py:369
  47.6 3.5 %attend.12 = (f32[2,128,1024]{2,1,0:T(8,128)S(1)}, f32[2,512,128]{2,1,0:T(8,128)S(1)}, bf16[2,384,128]{2,1,0:T(8,128)(2,1)S(1)}) custom-call(s32[2]{0:T(128)S(1)} %pad_add_fusion.meta, s32[16]{0:T(128)S(1)} %copy-done.5, bf16[272,1024]{1,0:T(8,128)(2,1)S(1)} %collective-permute-done.10.refs_0_, ...), custom_call_target="tpu_custom_call", output_to_operand_aliasing={{0}: (6, {})} | custom-call | flops 805306368 | bytes 1048576 | tf_op jit(solution)/shard_map/attend/pallas_call | solution.py:369
  51.9 3.5 %attend.13 = (f32[2,128,1024]{2,1,0:T(8,128)S(1)}, f32[2,512,128]{2,1,0:T(8,128)S(1)}, bf16[2,384,128]{2,1,0:T(8,128)(2,1)S(1)}) custom-call(s32[2]{0:T(128)S(1)} %pad_add_fusion.meta, s32[16]{0:T(128)S(1)} %copy-done.5, bf16[272,1024]{1,0:T(8,128)(2,1)S(1)} %collective-permute-done.10.refs_0_, ...), custom_call_target="tpu_custom_call", output_to_operand_aliasing={{0}: (6, {})} | custom-call | flops 805306368 | bytes 1048576 | tf_op jit(solution)/shard_map/attend/pallas_call | solution.py:369
  55.3 3.0 %collective-permute-done.12.refs_3_.back = bf16[4,384,128]{2,1,0:T(8,128)(2,1)S(1)} collective-permute-done((bf16[4,384,128]{2,1,0:T(8,128)(2,1)S(1)}, bf16[4,384,128]{2,1,0:T(8,128)(2,1)S(1)}, u32[]{:S(2)}, u32[]{:S(2)}) %collective-permute-start.12) | collective-permute-done | bytes 393248 | tf_op jit(solution)/shard_map/ppermute | solution.py:29
  58.4 3.6 %attend.14 = (bf16[128,1024]{1,0:T(8,128)(2,1)S(1)}, bf16[128,1024]{1,0:T(8,128)(2,1)S(1)}, f32[2,896,128]{2,1,0:T(8,128)S(1)}) custom-call(s32[2]{0:T(128)S(1)} %pad_add_fusion.meta, s32[16]{0:T(128)S(1)} %copy-done.5, bf16[272,1024]{1,0:T(8,128)(2,1)S(1)} %collective-permute-done.10.refs_0_, bf16[272,1024]{1,0:T(8,128)(2,1)S(1)} %collective-permute-done.11.refs_1_, ...), custom_call_target="tpu_custom_call" | custom-call | flops 805306368 | bytes 1048576 | tf_op jit(solution)/shard_map/attend/pallas_call | solution.py:369
  63.9 3.4 %attend.15 = (bf16[128,1024]{1,0:T(8,128)(2,1)S(1)}, bf16[128,1024]{1,0:T(8,128)(2,1)S(1)}, f32[2,512,128]{2,1,0:T(8,128)S(1)}, bf16[2,384,128]{2,1,0:T(8,128)(2,1)S(1)}) custom-call(s32[2]{0:T(128)S(1)} %pad_add_fusion.meta, s32[16]{0:T(128)S(1)} %copy-done.5, bf16[272,1024]{1,0:T(8,128)(2,1)S(1)} %get-tuple-element.55.refs_0_, ...), custom_call_target="tpu_custom_call" | custom-call | flops 805306368 | bytes 1048576 | tf_op jit(solution)/shard_map/attend/pallas_call | solution.py:369
  68.6 1.6 %collective-permute-start.15 = (bf16[128,1280]{1,0:T(8,128)(2,1)S(1)}, bf16[128,1280]{1,0:T(8,128)(2,1)S(1)}, u32[]{:S(2)}, u32[]{:S(2)}) collective-permute-start(bf16[128,1280]{1,0:T(8,128)(2,1)S(1)} %get-tuple-element.88), channel_id=1, source_target_pairs={{0,2},{1,3},{2,0},{3,1},{4,6},{5,7},{6,4},{7,5},{8,10},{9,11},{10,... | collective-permute-start | bytes 983048 | tf_op jit(solution)/shard_map/ppermute | solution.py:33
  70.4 1.5 %collective-permute-start.21 = (bf16[2,512,128]{2,1,0:T(8,128)(2,1)S(1)}, bf16[2,512,128]{2,1,0:T(8,128)(2,1)S(1)}, u32[]{:S(2)}, u32[]{:S(2)}) collective-permute-start(bf16[2,512,128]{2,1,0:T(8,128)(2,1)S(1)} %pack_sum.3), channel_id=1, source_target_pairs={{24,0},{0,8},{8,16},{16,24},{25,1},{1,9},{9,17},{17,25},{26,2},{2,... | collective-permute-start | bytes 786440 | tf_op jit(solution)/shard_map/ppermute | solution.py:29
  72.5 1.4 %collective-permute-start.13 = (bf16[128,640]{1,0:T(8,128)(2,1)S(1)}, bf16[128,640]{1,0:T(8,128)(2,1)S(1)}, u32[]{:S(2)}, u32[]{:S(2)}) collective-permute-start(bf16[128,640]{1,0:T(8,128)(2,1)S(1)} %get-tuple-element.85), channel_id=1, source_target_pairs={{0,1},{1,0},{2,3},{3,2},{4,5},{5,4},{6,7},{7,6},{8,9},{9,8},{10,11... | collective-permute-start | bytes 491528 | tf_op jit(solution)/shard_map/ppermute | solution.py:33
  74.1 4.5 %collective-permute-done.21.packet = bf16[2,512,128]{2,1,0:T(8,128)(2,1)S(1)} collective-permute-done((bf16[2,512,128]{2,1,0:T(8,128)(2,1)S(1)}, bf16[2,512,128]{2,1,0:T(8,128)(2,1)S(1)}, u32[]{:S(2)}, u32[]{:S(2)}) %collective-permute-start.21) | collective-permute-done | bytes 262176 | tf_op jit(solution)/shard_map/ppermute | solution.py:29
  79.4 1.5 %collective-permute-start.24 = (bf16[2,128,128]{2,1,0:T(8,128)(2,1)S(1)}, bf16[2,128,128]{2,1,0:T(8,128)(2,1)S(1)}, u32[]{:S(2)}, u32[]{:S(2)}) collective-permute-start(bf16[2,128,128]{2,1,0:T(8,128)(2,1)S(1)} %get-tuple-element.100), channel_id=1, source_target_pairs={{0,10},{1,11},{2,8},{3,9},{4,14},{5,15},{6,12},{7,13},{8,18},{9,19... | collective-permute-start | bytes 196616 | tf_op jit(solution)/shard_map/ppermute | solution.py:39
  80.9 3.7 %collective-permute-start.25 = (bf16[2,128,128]{2,1,0:T(8,128)(2,1)S(1)}, bf16[2,128,128]{2,1,0:T(8,128)(2,1)S(1)}, u32[]{:S(2)}, u32[]{:S(2)}) collective-permute-start(bf16[2,128,128]{2,1,0:T(8,128)(2,1)S(1)} %get-tuple-element.101), channel_id=1, source_target_pairs={{0,11},{1,10},{2,9},{3,8},{4,15},{5,14},{6,13},{7,12},{8,19},{9,18... | collective-permute-start | bytes 196616 | tf_op jit(solution)/shard_map/ppermute | solution.py:39
  84.6 1.5 %place_heads.1 = (bf16[1,128,4096]{2,1,0:T(8,128)(2,1)}, f32[8,128]{1,0:T(8,128)S(1)}) custom-call(s32[2]{0:T(128)S(1)} %pad_add_fusion.meta, bf16[128,1024]{1,0:T(8,128)(2,1)S(1)} %get-tuple-element.82.dq_own, bf16[128,640]{1,0:T(8,128)(2,1)S(1)} %collective-permute-done.13.near_one, bf16[128,640]{1,0:T(8,128)(2,1)S(1)} %collective-permute-done.14.near_two, ...), custom_call_target="tpu_custom_call" | custom-call | tf_op jit(solution)/shard_map/place_heads/pallas_call | solution.py:222
  86.2 3.0 %collective-permute-done.24.hop2 = bf16[2,128,128]{2,1,0:T(8,128)(2,1)S(1)} collective-permute-done((bf16[2,128,128]{2,1,0:T(8,128)(2,1)S(1)}, bf16[2,128,128]{2,1,0:T(8,128)(2,1)S(1)}, u32[]{:S(2)}, u32[]{:S(2)}) %collective-permute-start.24) | collective-permute-done | bytes 65568 | tf_op jit(solution)/shard_map/ppermute | solution.py:39
  (69 shorter events, 23.0 us)
Async XLA Ops:
  3.1 8.2 %collective-permute-start = (bf16[2,128,128]{2,1,0:T(8,128)(2,1)S(1)}, bf16[2,128,128]{2,1,0:T(8,128)(2,1)S(1)}, u32[]{:S(2)}, u32[]{:S(2)}) collective-permute-start(bf16[2,128,128]{2,1,0:T(8,128)(2,1)S(1)} %get-tuple-element.57), channel_id=1, source_target_pairs={{0,1},{1,0},{2,3},{3,2},{4,5},{5,4},{6,7},{7,6},{8,9},{9,8},{10,11... | collective-permute-start | bytes 196616 | tf_op jit(solution)/shard_map/ppermute | solution.py:33
  3.7 7.7 %collective-permute-start.1 = (bf16[2,128,128]{2,1,0:T(8,128)(2,1)S(1)}, bf16[2,128,128]{2,1,0:T(8,128)(2,1)S(1)}, u32[]{:S(2)}, u32[]{:S(2)}) collective-permute-start(bf16[2,128,128]{2,1,0:T(8,128)(2,1)S(1)} %get-tuple-element.58), channel_id=1, source_target_pairs={{0,2},{1,3},{2,0},{3,1},{4,6},{5,7},{6,4},{7,5},{8,10},{9,11},{10,... | collective-permute-start | bytes 196616 | tf_op jit(solution)/shard_map/ppermute | solution.py:33
  11.9 7.4 %collective-permute-start.3 = (bf16[272,1024]{1,0:T(8,128)(2,1)S(1)}, bf16[272,1024]{1,0:T(8,128)(2,1)S(1)}, u32[]{:S(2)}, u32[]{:S(2)}) collective-permute-start(bf16[272,1024]{1,0:T(8,128)(2,1)S(1)} %later.3), channel_id=1, source_target_pairs={{0,1},{1,0},{2,3},{3,2},{4,5},{5,4},{6,7},{7,6},{8,9},{9,8},{10,11... | collective-permute-start | bytes 1671176 | tf_op jit(solution)/shard_map/ppermute | solution.py:33
  12.1 7.2 %collective-permute-start.5 = (bf16[2,384,128]{2,1,0:T(8,128)(2,1)S(1)}, bf16[2,384,128]{2,1,0:T(8,128)(2,1)S(1)}, u32[]{:S(2)}, u32[]{:S(2)}) collective-permute-start(bf16[2,384,128]{2,1,0:T(8,128)(2,1)S(1)} %get-tuple-element.60.refs_1_), channel_id=1, source_target_pairs={{4,0},{5,1},{6,2},{7,3},{0,4},{1,5},{2,6},{3,7},{12,8},{13,9},{14,... | collective-permute-start | bytes 589832 | tf_op jit(solution)/shard_map/ppermute | solution.py:29
  14.1 10.0 %collective-permute-start.4 = (bf16[2,512,128]{2,1,0:T(8,128)(2,1)S(1)}, bf16[2,512,128]{2,1,0:T(8,128)(2,1)S(1)}, u32[]{:S(2)}, u32[]{:S(2)}) collective-permute-start(bf16[2,512,128]{2,1,0:T(8,128)(2,1)S(1)} %get-tuple-element.61.refs_2_), channel_id=1, source_target_pairs={{24,0},{0,8},{8,16},{16,24},{25,1},{1,9},{9,17},{17,25},{26,2},{2,... | collective-permute-start | bytes 786440 | tf_op jit(solution)/shard_map/ppermute | solution.py:29
  15.7 27.2 %collective-permute-start.10 = (bf16[272,1024]{1,0:T(8,128)(2,1)S(1)}, bf16[272,1024]{1,0:T(8,128)(2,1)S(1)}, u32[]{:S(2)}, u32[]{:S(2)}) collective-permute-start(bf16[272,1024]{1,0:T(8,128)(2,1)S(1)} %later.4), channel_id=1, source_target_pairs={{0,2},{1,3},{2,0},{3,1},{4,6},{5,7},{6,4},{7,5},{8,10},{9,11},{10,... | collective-permute-start | bytes 1671176 | tf_op jit(solution)/shard_map/ppermute | solution.py:33
  17.2 25.7 %collective-permute-start.11 = (bf16[272,1024]{1,0:T(8,128)(2,1)S(1)}, bf16[272,1024]{1,0:T(8,128)(2,1)S(1)}, u32[]{:S(2)}, u32[]{:S(2)}) collective-permute-start(bf16[272,1024]{1,0:T(8,128)(2,1)S(1)} %later.5), channel_id=1, source_target_pairs={{0,3},{1,2},{2,1},{3,0},{4,7},{5,6},{6,5},{7,4},{8,11},{9,10},{10,... | collective-permute-start | bytes 1671176 | tf_op jit(solution)/shard_map/ppermute | solution.py:33
  24.1 6.0 %collective-permute-start.7 = (bf16[2,384,128]{2,1,0:T(8,128)(2,1)S(1)}, bf16[2,384,128]{2,1,0:T(8,128)(2,1)S(1)}, u32[]{:S(2)}, u32[]{:S(2)}) collective-permute-start(bf16[2,384,128]{2,1,0:T(8,128)(2,1)S(1)} %get-tuple-element.64), channel_id=1, source_target_pairs={{4,0},{5,1},{6,2},{7,3},{0,4},{1,5},{2,6},{3,7},{12,8},{13,9},{14,... | collective-permute-start | bytes 589832 | tf_op jit(solution)/shard_map/ppermute | solution.py:29
  24.6 9.1 %collective-permute-start.6 = (bf16[2,512,128]{2,1,0:T(8,128)(2,1)S(1)}, bf16[2,512,128]{2,1,0:T(8,128)(2,1)S(1)}, u32[]{:S(2)}, u32[]{:S(2)}) collective-permute-start(bf16[2,512,128]{2,1,0:T(8,128)(2,1)S(1)} %get-tuple-element.63.refs_2_), channel_id=1, source_target_pairs={{24,0},{0,8},{8,16},{16,24},{25,1},{1,9},{9,17},{17,25},{26,2},{2,... | collective-permute-start | bytes 786440 | tf_op jit(solution)/shard_map/ppermute | solution.py:29
  33.7 5.7 %collective-permute-start.9 = (bf16[2,384,128]{2,1,0:T(8,128)(2,1)S(1)}, bf16[2,384,128]{2,1,0:T(8,128)(2,1)S(1)}, u32[]{:S(2)}, u32[]{:S(2)}) collective-permute-start(bf16[2,384,128]{2,1,0:T(8,128)(2,1)S(1)} %get-tuple-element.67), channel_id=1, source_target_pairs={{4,0},{5,1},{6,2},{7,3},{0,4},{1,5},{2,6},{3,7},{12,8},{13,9},{14,... | collective-permute-start | bytes 589832 | tf_op jit(solution)/shard_map/ppermute | solution.py:29
  35.1 11.1 %collective-permute-start.8 = (bf16[2,512,128]{2,1,0:T(8,128)(2,1)S(1)}, bf16[2,512,128]{2,1,0:T(8,128)(2,1)S(1)}, u32[]{:S(2)}, u32[]{:S(2)}) collective-permute-start(bf16[2,512,128]{2,1,0:T(8,128)(2,1)S(1)} %get-tuple-element.66.refs_2_), channel_id=1, source_target_pairs={{24,0},{0,8},{8,16},{16,24},{25,1},{1,9},{9,17},{17,25},{26,2},{2,... | collective-permute-start | bytes 786440 | tf_op jit(solution)/shard_map/ppermute | solution.py:29
  46.3 12.1 %collective-permute-start.12 = (bf16[4,384,128]{2,1,0:T(8,128)(2,1)S(1)}, bf16[4,384,128]{2,1,0:T(8,128)(2,1)S(1)}, u32[]{:S(2)}, u32[]{:S(2)}) collective-permute-start(bf16[4,384,128]{2,1,0:T(8,128)(2,1)S(1)} %side_by_side.1), channel_id=1, source_target_pairs={{4,0},{5,1},{6,2},{7,3},{0,4},{1,5},{2,6},{3,7},{12,8},{13,9},{14,... | collective-permute-start | bytes 1179656 | tf_op jit(solution)/shard_map/ppermute | solution.py:29
  51.1 10.9 %collective-permute-start.19 = (bf16[2,384,128]{2,1,0:T(8,128)(2,1)S(1)}, bf16[2,384,128]{2,1,0:T(8,128)(2,1)S(1)}, u32[]{:S(2)}, u32[]{:S(2)}) collective-permute-start(bf16[2,384,128]{2,1,0:T(8,128)(2,1)S(1)} %get-tuple-element.97), channel_id=1, source_target_pairs={{4,0},{5,1},{6,2},{7,3},{0,4},{1,5},{2,6},{3,7},{12,8},{13,9},{14,... | collective-permute-start | bytes 589832 | tf_op jit(solution)/shard_map/ppermute | solution.py:29
  62.1 8.2 %collective-permute-start.20 = (bf16[2,512,128]{2,1,0:T(8,128)(2,1)S(1)}, bf16[2,512,128]{2,1,0:T(8,128)(2,1)S(1)}, u32[]{:S(2)}, u32[]{:S(2)}) collective-permute-start(bf16[2,512,128]{2,1,0:T(8,128)(2,1)S(1)} %pack_sum.2), channel_id=1, source_target_pairs={{24,0},{0,8},{8,16},{16,24},{25,1},{1,9},{9,17},{17,25},{26,2},{2,... | collective-permute-start | bytes 786440 | tf_op jit(solution)/shard_map/ppermute | solution.py:29
  62.5 7.7 %collective-permute-start.18 = (bf16[2,384,128]{2,1,0:T(8,128)(2,1)S(1)}, bf16[2,384,128]{2,1,0:T(8,128)(2,1)S(1)}, u32[]{:S(2)}, u32[]{:S(2)}) collective-permute-start(bf16[2,384,128]{2,1,0:T(8,128)(2,1)S(1)} %get-tuple-element.95), channel_id=1, source_target_pairs={{4,0},{5,1},{6,2},{7,3},{0,4},{1,5},{2,6},{3,7},{12,8},{13,9},{14,... | collective-permute-start | bytes 589832 | tf_op jit(solution)/shard_map/ppermute | solution.py:29
  67.3 6.7 %collective-permute-start.17 = (bf16[2,384,128]{2,1,0:T(8,128)(2,1)S(1)}, bf16[2,384,128]{2,1,0:T(8,128)(2,1)S(1)}, u32[]{:S(2)}, u32[]{:S(2)}) collective-permute-start(bf16[2,384,128]{2,1,0:T(8,128)(2,1)S(1)} %get-tuple-element.93), channel_id=1, source_target_pairs={{4,0},{5,1},{6,2},{7,3},{0,4},{1,5},{2,6},{3,7},{12,8},{13,9},{14,... | collective-permute-start | bytes 589832 | tf_op jit(solution)/shard_map/ppermute | solution.py:29
  68.6 12.3 %collective-permute-start.15 = (bf16[128,1280]{1,0:T(8,128)(2,1)S(1)}, bf16[128,1280]{1,0:T(8,128)(2,1)S(1)}, u32[]{:S(2)}, u32[]{:S(2)}) collective-permute-start(bf16[128,1280]{1,0:T(8,128)(2,1)S(1)} %get-tuple-element.88), channel_id=1, source_target_pairs={{0,2},{1,3},{2,0},{3,1},{4,6},{5,7},{6,4},{7,5},{8,10},{9,11},{10,... | collective-permute-start | bytes 983048 | tf_op jit(solution)/shard_map/ppermute | solution.py:33
  70.4 8.2 %collective-permute-start.21 = (bf16[2,512,128]{2,1,0:T(8,128)(2,1)S(1)}, bf16[2,512,128]{2,1,0:T(8,128)(2,1)S(1)}, u32[]{:S(2)}, u32[]{:S(2)}) collective-permute-start(bf16[2,512,128]{2,1,0:T(8,128)(2,1)S(1)} %pack_sum.3), channel_id=1, source_target_pairs={{24,0},{0,8},{8,16},{16,24},{25,1},{1,9},{9,17},{17,25},{26,2},{2,... | collective-permute-start | bytes 786440 | tf_op jit(solution)/shard_map/ppermute | solution.py:29
  71.9 12.7 %collective-permute-start.16 = (bf16[128,1280]{1,0:T(8,128)(2,1)S(1)}, bf16[128,1280]{1,0:T(8,128)(2,1)S(1)}, u32[]{:S(2)}, u32[]{:S(2)}) collective-permute-start(bf16[128,1280]{1,0:T(8,128)(2,1)S(1)} %get-tuple-element.89), channel_id=1, source_target_pairs={{0,3},{1,2},{2,1},{3,0},{4,7},{5,6},{6,5},{7,4},{8,11},{9,10},{10,... | collective-permute-start | bytes 983048 | tf_op jit(solution)/shard_map/ppermute | solution.py:33
  72.5 6.8 %collective-permute-start.13 = (bf16[128,640]{1,0:T(8,128)(2,1)S(1)}, bf16[128,640]{1,0:T(8,128)(2,1)S(1)}, u32[]{:S(2)}, u32[]{:S(2)}) collective-permute-start(bf16[128,640]{1,0:T(8,128)(2,1)S(1)} %get-tuple-element.85), channel_id=1, source_target_pairs={{0,1},{1,0},{2,3},{3,2},{4,5},{5,4},{6,7},{7,6},{8,9},{9,8},{10,11... | collective-permute-start | bytes 491528 | tf_op jit(solution)/shard_map/ppermute | solution.py:33
  79.2 6.9 %collective-permute-start.22 = (bf16[2,128,128]{2,1,0:T(8,128)(2,1)S(1)}, bf16[2,128,128]{2,1,0:T(8,128)(2,1)S(1)}, u32[]{:S(2)}, u32[]{:S(2)}) collective-permute-start(bf16[2,128,128]{2,1,0:T(8,128)(2,1)S(1)} %get-tuple-element.98), channel_id=1, source_target_pairs={{0,8},{1,9},{2,10},{3,11},{4,12},{5,13},{6,14},{7,15},{8,16},{9,17... | collective-permute-start | bytes 196616 | tf_op jit(solution)/shard_map/ppermute | solution.py:39
  79.3 6.8 %collective-permute-start.23 = (bf16[2,128,128]{2,1,0:T(8,128)(2,1)S(1)}, bf16[2,128,128]{2,1,0:T(8,128)(2,1)S(1)}, u32[]{:S(2)}, u32[]{:S(2)}) collective-permute-start(bf16[2,128,128]{2,1,0:T(8,128)(2,1)S(1)} %get-tuple-element.99), channel_id=1, source_target_pairs={{0,9},{1,8},{2,11},{3,10},{4,13},{5,12},{6,15},{7,14},{8,17},{9,16... | collective-permute-start | bytes 196616 | tf_op jit(solution)/shard_map/ppermute | solution.py:39
  79.4 9.8 %collective-permute-start.24 = (bf16[2,128,128]{2,1,0:T(8,128)(2,1)S(1)}, bf16[2,128,128]{2,1,0:T(8,128)(2,1)S(1)}, u32[]{:S(2)}, u32[]{:S(2)}) collective-permute-start(bf16[2,128,128]{2,1,0:T(8,128)(2,1)S(1)} %get-tuple-element.100), channel_id=1, source_target_pairs={{0,10},{1,11},{2,8},{3,9},{4,14},{5,15},{6,12},{7,13},{8,18},{9,19... | collective-permute-start | bytes 196616 | tf_op jit(solution)/shard_map/ppermute | solution.py:39
  80.9 8.3 %collective-permute-start.25 = (bf16[2,128,128]{2,1,0:T(8,128)(2,1)S(1)}, bf16[2,128,128]{2,1,0:T(8,128)(2,1)S(1)}, u32[]{:S(2)}, u32[]{:S(2)}) collective-permute-start(bf16[2,128,128]{2,1,0:T(8,128)(2,1)S(1)} %get-tuple-element.101), channel_id=1, source_target_pairs={{0,11},{1,10},{2,9},{3,8},{4,15},{5,14},{6,13},{7,12},{8,19},{9,18... | collective-permute-start | bytes 196616 | tf_op jit(solution)/shard_map/ppermute | solution.py:39
  (9 other events, 21.9 us)
